TPU v7x, 32 devices: a whole 2x2x4 slice. The times are simulated.
32 devices in a mesh: row: 4 (over x, core), col: 8 (over z, y).
Axes of the slice: x: 2, y: 2, z: 4, core: 2. Of those that a mesh axis runs over, the one named last changes fastest.
Arguments:
- amplitudes: bfloat16 [8, 8, 768, 768], P('row', 'col'), may hold values from -0.59765625 to 0.59765625
- ints: bfloat16 [8, 768, 2304], P('row', None, 'col'), may hold values from -0.3984375 to 0.3984375
- eps_occ: float32 [8], replicated, may hold values from -2 to -0.5
- eps_vir: float32 [768], replicated, may hold values from 0.2 to 3
- fock_vir: bfloat16 [768, 768], replicated, may hold values from -2 to 2, as said below
Outputs:
- updated: bfloat16 [8, 8, 768, 768], P('row', 'col')
Inputs may be any that keep to these rules, and one draw needn't show every extreme that they name: fock_vir is zero on its diagonal.
All inputs are finite; a program needn't handle non-finite values.
Results may differ from a plain program's by a relative error of at most 0.019.
Values may be sent and summed in bfloat16 or wider, within the bound.
No kernel may reach another device: no remote copies, remote signals or barrier semaphores. Data moves between devices by JAX's collectives and lax.ppermute only.
A program may use at most 64 MiB of HBM per device.

v0:
```python
import jax
import jax.numpy as jnp
from jax import lax
from jax.sharding import PartitionSpec as P


def local(amplitudes, ints, eps_occ, eps_vir, fock_vir):
    occ_row = amplitudes.shape[0]
    occ_col = amplitudes.shape[1]
    second_ids = lax.axis_index("col") * occ_col + jnp.arange(occ_col, dtype=jnp.int32)
    first_ids = lax.axis_index("row") * occ_row + jnp.arange(occ_row, dtype=jnp.int32)
    picker = (second_ids[:, None] == first_ids[None, :]).astype(jnp.bfloat16)
    full_rows = lax.all_gather(ints, "col", axis=2, tiled=True)
    own_part = jnp.einsum("ji,iaq->jaq", picker, full_rows, preferred_element_type=jnp.float32)
    cross_part = own_part + jnp.einsum(
        "kjcb,kcq->jbq", amplitudes, full_rows, preferred_element_type=jnp.float32
    )
    dressed = lax.psum(cross_part.astype(jnp.bfloat16), "row")
    numer = jnp.einsum("iaq,jbq->ijab", full_rows, dressed, preferred_element_type=jnp.float32)
    numer = numer + jnp.einsum(
        "ijac,cb->ijab", amplitudes, fock_vir, preferred_element_type=jnp.float32
    )
    eps_first = lax.dynamic_slice_in_dim(eps_occ, lax.axis_index("row") * occ_row, occ_row, 0)
    eps_second = lax.dynamic_slice_in_dim(eps_occ, lax.axis_index("col") * occ_col, occ_col, 0)
    denom = (
        eps_vir[None, None, :, None]
        + eps_vir[None, None, None, :]
        - eps_first[:, None, None, None]
        - eps_second[None, :, None, None]
    )
    return (amplitudes.astype(jnp.float32) - numer / denom).astype(jnp.bfloat16)


def solution(mesh):
    placed = (P("row", "col", None, None), P("row", None, "col"), P(), P(), P())
    return jax.shard_map(
        local, mesh=mesh, in_specs=placed, out_specs=P("row", "col", None, None), check_vma=False
    )
```

profile of v0, /device:TPU:0, one launch (start us, length us, event | category | flops | bytes accessed | tf_op | source)
XLA Modules:
  0.0 250.9 jit_solution(8362615616687983431)
XLA Ops:
  6.5 0.0 copy-start
  6.5 0.0 all-gather.2.cloned.1.call-start
  6.5 0.7 all-gather.2.cloned.1.call-update
  7.3 0.0 all-reduce.2.cloned.1.call-start
  7.3 113.8 %all-gather.2.cloned.1.call-done = bf16[2,768,2304]{1,2,0:T(8,128)(2,1)} async-done(((bf16[2,768,288]{1,2,0:T(8,128)(2,1)}), bf16[2,768,2304]{1,2,0:T(8,128)(2,1)}) %all-gather.2.cloned.1.call-update) | async-done | bytes 7077904 | tf_op jit(solution)/shard_map/all_gather | solution.py:13
  121.1 18.3 %copy.9 = bf16[2,768,2304]{2,0,1:T(2,128)(2,1)} copy(bf16[2,768,2304]{1,2,0:T(8,128)(2,1)} %all-gather.2.cloned.1.call-done) | data formatting | bytes 14155776 | tf_op jit(solution)/shard_map/all_gather | solution.py:13
  139.4 0.0 copy-start.1
  139.4 0.0 copy-start.2
  139.4 9.6 %fusion.12 = f32[1,768,2304]{2,0,1:T(1,128)S(1)} fusion(bf16[2,768,2304]{2,0,1:T(2,128)(2,1)} %copy.9, s32[]{:T(128)S(6)} %mul.4, s32[]{:T(128)S(6)} %axis_index.14), kind=kOutput, calls=%fused_computation.14 | convolution fusion | flops 7077892 | bytes 14155784 | tf_op jit(solution)/shard_map/ji,iaq->jaq/dot_general | solution.py:14
  149.0 0.0 copy-done.1
  149.0 0.0 copy-done.2
  149.0 7.4 %fusion = bf16[768,2304]{1,0:T(8,128)(2,1)} fusion(f32[1,768,2304]{2,0,1:T(1,128)S(1)} %fusion.12, bf16[2,768,2304]{1,2,0:T(8,128)(2,1)S(1)} %copy-done.1, bf16[2,1,768,768]{3,2,1,0:T(8,128)(2,1)S(1)} %copy-done.2), kind=kOutput, calls=%fused_computation.1 | convolution fusion | flops 5439356928 | bytes 20054016 | tf_op jit(solution)/shard_map/kjcb,kcq->jbq/dot_general | solution.py:15
  156.4 0.0 all-reduce.2.cloned.1.call-update
  156.4 2.4 copy.6
  158.8 0.0 copy-done.4
  158.8 0.1 dynamic_slice.6
  158.9 0.5 dynamic_slice.7
  159.5 0.0 copy-done.3
  159.5 1.6 broadcast_add_fusion
  161.1 0.0 copy-done
  161.1 4.3 %fusion.6 = f32[2,768,768]{1,2,0:T(8,128)} fusion(bf16[2,1,768,768]{3,2,1,0:T(8,128)(2,1)S(1)} %copy-done.2, bf16[768,768]{1,0:T(8,128)(2,1)S(1)} %copy-done), kind=kOutput, calls=%fused_computation.8 | convolution fusion | flops 1811939328 | bytes 8257536 | tf_op jit(solution)/shard_map/ijac,cb->ijab/dot_general | solution.py:20
  165.3 64.3 %all-reduce.2.cloned.1.call-done = bf16[768,2304]{1,0:T(8,128)(2,1)} async-done(((bf16[768,2304]{1,0:T(8,128)(2,1)}), bf16[768,2304]{1,0:T(8,128)(2,1)}) %all-reduce.2.cloned.1.call-update) | async-done | bytes 3538960 | tf_op jit(solution)/shard_map/psum | solution.py:18
  229.6 12.0 %fusion.3 = bf16[2,1,768,768]{2,3,0,1:T(8,128)(2,1)S(1)} fusion(f32[2,768,768]{1,2,0:T(8,128)} %fusion.6, bf16[2,1,768,768]{2,3,0,1:T(8,128)(2,1)} %copy.6, f32[]{:T(128)} %bitcast.9, f32[2]{0:T(128)S(1)} %dynamic_slice.6, f32[768,768]{0,1:T(8,128)} %broadcast_add_fusion, bf16[2,768,2304]{1,2,0:T(8,128)(2,1)} %all-gather.2.cloned.1.call-done, ...), kind=kOutput, calls=%fused_computation.5 | convolution fusion | flops 5444075520 | bytes 22413324 | tf_op jit(solution)/shard_map/iaq,jbq->ijab/dot_general | solution.py:19
  241.6 2.4 copy.8
  (2 shorter events, 0.0 us)
Async XLA Ops:
  6.5 154.5 %copy-start = (bf16[768,768]{1,0:T(8,128)(2,1)S(1)}, bf16[768,768]{1,0:T(8,128)(2,1)}, u32[]{:S(2)}) copy-start(bf16[768,768]{1,0:T(8,128)(2,1)} %param.9) | copy-start | bytes 3538948
  6.5 114.5 %all-gather.2.cloned.1.call-start = ((), (), s32[]{:S(2)}) async-start(), calls=%async_computation | async-start | bytes 7962624 | tf_op jit(solution)/shard_map/all_gather | solution.py:13
  7.3 222.4 %all-reduce.2.cloned.1.call-start = ((), (), s32[]{:S(2)}) async-start(), calls=%async_computation.1 | async-start | bytes 7077888 | tf_op jit(solution)/shard_map/psum | solution.py:18
  139.4 9.6 %copy-start.1 = (bf16[2,768,2304]{1,2,0:T(8,128)(2,1)S(1)}, bf16[2,768,2304]{1,2,0:T(8,128)(2,1)}, u32[]{:S(2)}) copy-start(bf16[2,768,2304]{1,2,0:T(8,128)(2,1)} %all-gather.2.cloned.1.call-done) | copy-start | bytes 21233668
  139.4 9.6 %copy-start.2 = (bf16[2,1,768,768]{3,2,1,0:T(8,128)(2,1)S(1)}, bf16[2,1,768,768]{3,2,1,0:T(8,128)(2,1)}, u32[]{:S(2)}) copy-start(bf16[2,1,768,768]{3,2,1,0:T(8,128)(2,1)} %param.5) | copy-start | bytes 7077892
  156.4 2.5 copy-start.4
  156.4 3.1 %copy-start.3 = (f32[768]{0:T(1024)S(1)}, f32[768]{0:T(1024)}, u32[]{:S(2)}) copy-start(f32[768]{0:T(1024)} %param.8) | copy-start | bytes 9220
Sparse Core Ops, SparseCore 0:
  9.6 111.4 all-gather.1
  156.5 73.0 all-reduce.1
where the time goes:
time: 251 us
  waiting for transfers between devices  179 us (71%)
  matrix products  33.2 us (13%)
  local copies, waits for them, and re-layouts  23.8 us (9%)
  between operations  13.4 us (5%)
    all_gather x1, waiting for transfers between devices, local(): full_rows = lax.all_gather(ints, 'col', axis=2, tiled=True)  114 us
    psum x1, waiting for transfers between devices, local(): dressed = lax.psum(cross_part.astype(jnp.bfloat16), 'row')  64.3 us
    all_gather x1, local copies, waits for them, and re-layouts, local(): full_rows = lax.all_gather(ints, 'col', axis=2, tiled=True)  18.3 us
    dot_general x1, matrix products, local(): jnp.einsum('iaq,jbq->ijab', full_rows, dressed, preferred_element_type=jn...  12 us
    dot_general x1, matrix products, local(): jnp.einsum('ji,iaq->jaq', picker, full_rows, preferred_element_type=jnp.f...  9.61 us
    dot_general x1, matrix products, local(): jnp.einsum('kjcb,kcq->jbq', amplitudes, full_rows, preferred_element_type...  7.36 us
  transfers between devices with their start and end apart: 2, of which 2 were waited for; matrix products, arithmetic and copies ran while one was open for 4% of the time, Pallas kernels for 0%

commit v1 on v0

v1 whole, which is shorter than its diff:
```python
import functools

import jax
import jax.numpy as jnp
from jax import lax
from jax.experimental import pallas as pl
from jax.experimental.pallas import tpu as pltpu
from jax.sharding import PartitionSpec as P

VMEM_LIMIT = 56 * 1024 * 1024


def ring_order(n):
    low = max(d for d in range(1, n + 1) if n % d == 0 and d * d <= n)
    high = n // low
    if low == 1 or high % 2:
        return list(range(n))
    order = [h * low for h in range(high)]
    for turn, h in enumerate(reversed(range(high))):
        lows = range(1, low) if turn % 2 == 0 else range(low - 1, 0, -1)
        order += [h * low + l for l in lows]
    return order


def group_sizes(total):
    sizes = []
    size = 1
    while total:
        sizes.append(min(size, total))
        total -= sizes[-1]
        if len(sizes) > 1:
            size *= 2
    return sizes[::-1]


def cross_kernel(flags, t_ref, *refs):
    chunks, (keep_ref, send_ref, full) = refs[:-3], refs[-3:]
    occ, vir = t_ref.shape[0], t_ref.shape[2]
    half = vir // 2
    for start in range(0, vir, 256):
        cols = slice(start, min(start + 256, vir))
        total = None
        for k in range(occ):
            rows = jnp.concatenate([c[k] for c in chunks], axis=0)
            part = jnp.dot(rows, t_ref[k, :, cols], preferred_element_type=jnp.float32)
            own = jnp.concatenate([c[k, :, cols] for c in chunks], axis=0).astype(jnp.float32)
            part = part + jnp.where(flags[1 + k] == 1, own, 0.0)
            total = part if total is None else total + part
        full[:, cols] = total
    low, high = full[:, :half], full[:, half:]
    first = flags[0] == 0
    keep_ref[...] = jnp.where(first, low, high)
    send_ref[...] = jnp.where(first, high, low).astype(send_ref.dtype)


def cross(flags, t, chunks):
    rows = sum(c.shape[1] for c in chunks)
    vir = t.shape[2]
    vmem = pl.BlockSpec(memory_space=pltpu.VMEM)
    return pl.pallas_call(
        cross_kernel,
        out_shape=(
            jax.ShapeDtypeStruct((rows, vir // 2), jnp.float32),
            jax.ShapeDtypeStruct((rows, vir // 2), jnp.bfloat16),
        ),
        in_specs=[pl.BlockSpec(memory_space=pltpu.SMEM)] + [vmem] * (1 + len(chunks)),
        out_specs=(vmem, vmem),
        scratch_shapes=[pltpu.VMEM((rows, vir), jnp.float32)],
        compiler_params=pltpu.CompilerParams(vmem_limit_bytes=VMEM_LIMIT),
        cost_estimate=pl.CostEstimate(
            flops=2 * rows * vir * vir * t.shape[0],
            bytes_accessed=2 * t.size + 2 * rows * vir * (t.shape[0] + 2),
            transcendentals=0,
        ),
        name="cross",
    )(flags, t, *chunks)


def joined(first, mine, other):
    return jnp.concatenate(
        [jnp.where(first, mine, other), jnp.where(first, other, mine)], axis=1
    )


def numer_kernel(counts, flags, t_ref, fock_ref, *refs):
    groups = len(counts)
    chunks = refs[: sum(counts)]
    mine, other = refs[sum(counts):][:groups], refs[sum(counts) + groups:][:groups]
    out_ref, dressed = refs[-2:]
    first = flags[0] == 0
    at = 0
    for m, o in zip(mine, other):
        rows = m.shape[0]
        dressed[at:at + rows, :] = joined(first, m[...], o[...])
        at += rows
    vir = t_ref.shape[2]
    step = 256 if vir % 256 == 0 else vir
    for k in range(t_ref.shape[0]):
        for start in range(0, vir, step):
            cols = slice(start, start + step)
            total = jnp.dot(t_ref[k, cols, :], fock_ref[...], preferred_element_type=jnp.float32)
            left = jnp.concatenate([c[k, :, cols] for c in chunks], axis=0)
            total += lax.dot_general(
                left, dressed[...], (((0,), (0,)), ((), ())), preferred_element_type=jnp.float32
            )
            out_ref[k, cols, :] = total


def numer(flags, t, fock, chunk_groups, mine, other):
    chunks = [c for group in chunk_groups for c in group]
    rows = sum(c.shape[1] for c in chunks)
    occ, vir = t.shape[0], t.shape[2]
    vmem = pl.BlockSpec(memory_space=pltpu.VMEM)
    return pl.pallas_call(
        functools.partial(numer_kernel, [len(group) for group in chunk_groups]),
        out_shape=jax.ShapeDtypeStruct((occ, vir, vir), jnp.float32),
        in_specs=[pl.BlockSpec(memory_space=pltpu.SMEM)]
        + [vmem] * (2 + len(chunks) + len(mine) + len(other)),
        out_specs=vmem,
        scratch_shapes=[pltpu.VMEM((rows, vir), jnp.bfloat16)],
        compiler_params=pltpu.CompilerParams(vmem_limit_bytes=VMEM_LIMIT),
        cost_estimate=pl.CostEstimate(
            flops=2 * occ * vir * vir * (rows + vir),
            bytes_accessed=2 * rows * vir * (occ + 1) + 6 * t.size,
            transcendentals=0,
        ),
        name="numer",
    )(flags, t, fock, *chunks, *mine, *other)


def turn_kernel(*refs):
    out_ref = refs[-1]
    for k in range(out_ref.shape[0]):
        out_ref[k] = jnp.concatenate([c[k] for c in refs[:-1]], axis=0).T


def turn(chunks):
    rows = sum(c.shape[1] for c in chunks)
    occ, _, vir = chunks[0].shape
    vmem = pl.BlockSpec(memory_space=pltpu.VMEM)
    return pl.pallas_call(
        turn_kernel,
        out_shape=jax.ShapeDtypeStruct((occ, vir, rows), jnp.bfloat16),
        in_specs=[vmem] * len(chunks),
        out_specs=vmem,
        compiler_params=pltpu.CompilerParams(vmem_limit_bytes=VMEM_LIMIT),
        cost_estimate=pl.CostEstimate(
            flops=0, bytes_accessed=4 * occ * vir * rows, transcendentals=0
        ),
        name="turn",
    )(*chunks)


def final_kernel(flags, eps_first, acc_ref, left_ref, t_ref, mine, other, rows_ref, cols_ref, out_ref):
    dressed = joined(flags[0] == 0, mine[...], other[...])
    total = acc_ref[0] + jnp.dot(left_ref[0], dressed, preferred_element_type=jnp.float32)
    denom = (rows_ref[...] - eps_first[pl.program_id(0)]) + cols_ref[...]
    out_ref[0, 0] = (t_ref[0, 0].astype(jnp.float32) - total / denom).astype(out_ref.dtype)


def final(flags, eps_first, acc, left, t, mine, other, eps_rows, eps_cols):
    occ, vir, rows = left.shape
    step = 256 if vir % 256 == 0 else vir
    smem = pl.BlockSpec(memory_space=pltpu.SMEM)
    return pl.pallas_call(
        final_kernel,
        grid=(occ, vir // step),
        out_shape=jax.ShapeDtypeStruct(t.shape, t.dtype),
        in_specs=[
            smem,
            smem,
            pl.BlockSpec((1, step, vir), lambda k, a: (k, a, 0)),
            pl.BlockSpec((1, step, rows), lambda k, a: (k, a, 0)),
            pl.BlockSpec((1, 1, step, vir), lambda k, a: (k, 0, a, 0)),
            pl.BlockSpec(mine.shape, lambda k, a: (0, 0)),
            pl.BlockSpec(other.shape, lambda k, a: (0, 0)),
            pl.BlockSpec((step, 1), lambda k, a: (a, 0)),
            pl.BlockSpec((1, vir), lambda k, a: (0, 0)),
        ],
        out_specs=pl.BlockSpec((1, 1, step, vir), lambda k, a: (k, 0, a, 0)),
        compiler_params=pltpu.CompilerParams(vmem_limit_bytes=VMEM_LIMIT),
        cost_estimate=pl.CostEstimate(
            flops=2 * occ * vir * vir * rows, bytes_accessed=8 * t.size, transcendentals=0
        ),
        name="final",
    )(flags, eps_first, acc, left, t, mine, other, eps_rows, eps_cols)


def local(n_row, n_col, amplitudes, ints, eps_occ, eps_vir, fock_vir):
    occ, _, vir, _ = amplitudes.shape
    row, col = lax.axis_index("row"), lax.axis_index("col")
    t = amplitudes[:, 0]
    shard = jnp.swapaxes(ints, 1, 2)
    q = shard.shape[1]
    cut = (q // 2 + 15) // 16 * 16

    order = ring_order(n_col)
    up = [(order[p], order[(p + 1) % n_col]) for p in range(n_col)]
    down = [(b, a) for a, b in up]

    own = [shard[:, :cut], shard[:, cut:]]
    steps = []
    ups, downs = list(own), list(own)
    for step in range(n_col - 2):
        h = step % 2
        ups[h] = lax.ppermute(ups[h], "col", up)
        downs[h] = lax.ppermute(downs[h], "col", down)
        steps.append([ups[h], downs[h]])
    steps.append([lax.ppermute(ups[0], "col", up), lax.ppermute(downs[1], "col", down)])

    groups = []
    at = 0
    for size in group_sizes(len(steps)):
        groups.append([c for pair in steps[at:at + size] for c in pair])
        at += size
    groups[0] = own + groups[0]

    core = row % 2
    first_ids = row * occ + jnp.arange(occ, dtype=jnp.int32)
    flags = jnp.concatenate(
        [core[None].astype(jnp.int32), (first_ids == col).astype(jnp.int32)]
    )

    def swap(x, bit):
        return lax.ppermute(x, "row", [(r, r ^ bit) for r in range(n_row)])

    mine, other = [], []
    for group in groups:
        total, send = cross(flags, t, group)
        total = total + swap(send, 1).astype(jnp.float32)
        bit = 2
        while bit < n_row:
            total = total + swap(total.astype(jnp.bfloat16), bit).astype(jnp.float32)
            bit *= 2
        mine.append(total.astype(jnp.bfloat16))
        other.append(swap(mine[-1], 1))

    acc = numer(flags, t, fock_vir, groups[:-1], mine[:-1], other[:-1])
    left = turn(groups[-1])
    eps_first = lax.dynamic_slice_in_dim(eps_occ, row * occ, occ, 0)
    eps_second = lax.dynamic_slice_in_dim(eps_occ, col, 1, 0)
    eps_rows = (eps_vir - eps_second)[:, None]
    return final(
        flags, eps_first, acc, left, amplitudes, mine[-1], other[-1], eps_rows, eps_vir[None, :]
    )


def solution(mesh):
    placed = (P("row", "col", None, None), P("row", None, "col"), P(), P(), P())
    body = functools.partial(local, mesh.shape["row"], mesh.shape["col"])
    return jax.shard_map(
        body, mesh=mesh, in_specs=placed, out_specs=P("row", "col", None, None), check_vma=False
    )
```

time: 251 us -> 134 us (0.53)
  waiting for transfers between devices: 179 us -> 52.6 us
  Pallas kernels: 0 us -> 42.9 us
  matrix products: 33.2 us -> 0 us
  starting transfers between devices: 0.04 us -> 21.7 us
  local copies, waits for them, and re-layouts: 23.8 us -> 9.41 us
  between operations: 13.4 us -> 0.33 us
  other arithmetic: 1.61 us -> 6.28 us
    all_gather x1 -> x0, waiting for transfers between devices: 114 us -> none  [local(): full_rows = lax.all_gather(ints, 'col', axis=2, tiled=True)]
    psum x1 -> x0, waiting for transfers between devices: 64.3 us -> none  [local(): dressed = lax.psum(cross_part.astype(jnp.bfloat16), 'row')]
    ppermute x0 -> x26, waiting for transfers between devices: none -> 52.6 us  [the longest x6 35.5 us: local(): ups[h] = lax.ppermute(ups[h], 'col', up)]
    pallas_call x0 -> x7, Pallas kernels: none -> 42.9 us  [the longest x4 19.3 us: cross(): pl.pallas_call(cross_kernel, out_shape=(jax.ShapeDtypeStruct((rows, vir /...]
    dot_general x4 -> x0, matrix products: 33.2 us -> none  [the longest x1 12 us: local(): jnp.einsum('iaq,jbq->ijab', full_rows, dressed, preferred_element_type=jn...]
    ppermute x0 -> x26, starting transfers between devices: none -> 21.7 us  [the longest x6 11.9 us: local(): ups[h] = lax.ppermute(ups[h], 'col', up)]
    all_gather x1 -> x0, local copies, waits for them, and re-layouts: 18.3 us -> none  [local(): full_rows = lax.all_gather(ints, 'col', axis=2, tiled=True)]
    convert_element_type x0 -> x9, other arithmetic: none -> 5.06 us  [the longest x4 3.51 us: local(): total = total + swap(total.astype(jnp.bfloat16), bit).astype(jnp.float32)]
  transfers between devices with their start and end apart: 2 -> 26, of which waited for: 2 -> 14; matrix products, arithmetic and copies ran while one was open for 4% -> 7% of each run, Pallas kernels for 0% -> 21%
where the time goes in v1:
time: 134 us; the launch traced here: 133 us
  waiting for transfers between devices  52.6 us (39%)
  Pallas kernels  42.9 us (32%)
  starting transfers between devices  21.7 us (16%)
  local copies, waits for them, and re-layouts  9.41 us (7%)
  other arithmetic  6.28 us (5%)
    ppermute x6, waiting for transfers between devices, local(): ups[h] = lax.ppermute(ups[h], 'col', up)  35.5 us
    pallas_call x4, Pallas kernels, cross(): pl.pallas_call(cross_kernel, out_shape=(jax.ShapeDtypeStruct((rows, vir /...  19.3 us
    pallas_call x1, Pallas kernels, numer(): pl.pallas_call(functools.partial(numer_kernel, [len(group) for group in c...  13.7 us
    ppermute x6, starting transfers between devices, local(): ups[h] = lax.ppermute(ups[h], 'col', up)  11.9 us
    pallas_call x1, Pallas kernels, final(): pl.pallas_call(final_kernel, grid=(occ, vir // step), out_shape=jax.Shape...  7.32 us
    ppermute x1, waiting for transfers between devices, local(): lax.ppermute(ups[0], 'col', up)  6.83 us
    ppermute x6, waiting for transfers between devices, local(): downs[h] = lax.ppermute(downs[h], 'col', down)  6.54 us
    ppermute x12, starting transfers between devices, swap(): return lax.ppermute(x, 'row', [(r, r ^ bit) for r in range(n_row)])  6.4 us
  transfers between devices with their start and end apart: 26, of which 14 were waited for; matrix products, arithmetic and copies ran while one was open for 7% of the time, Pallas kernels for 21%

profile of v1, /device:TPU:0, one launch (start us, length us, event | category | flops | bytes accessed | tf_op | source)
XLA Modules:
  0.0 133.3 jit_solution(14896861731140181560)
XLA Ops:
  1.2 3.1 %collective-permute-start = (bf16[2,144,768]{2,1,0:T(8,128)(2,1)S(1)}, bf16[2,144,768]{2,1,0:T(8,128)(2,1)S(1)}, u32[]{:S(2)}, u32[]{:S(2)}) collective-permute-start(bf16[2,144,768]{2,1,0:T(8,128)(2,1)S(1)} %get-tuple-element.22.refs_0_), channel_id=1, source_target_pairs={{0,2},{2,4},{4,6},{6,7},{7,5},{5,3},{3,1},{1,0},{8,10},{10,12},{12... | collective-permute-start | bytes 1327112 | tf_op jit(solution)/shard_map/ppermute | solution.py:206
  4.3 2.0 %collective-permute-start.2 = (bf16[2,144,768]{2,1,0:T(8,128)(2,1)S(1)}, bf16[2,144,768]{2,1,0:T(8,128)(2,1)S(1)}, u32[]{:S(2)}, u32[]{:S(2)}) collective-permute-start(bf16[2,144,768]{2,1,0:T(8,128)(2,1)S(1)} %get-tuple-element.21.refs_1_), channel_id=1, source_target_pairs={{0,2},{2,4},{4,6},{6,7},{7,5},{5,3},{3,1},{1,0},{8,10},{10,12},{12... | collective-permute-start | bytes 1327112 | tf_op jit(solution)/shard_map/ppermute | solution.py:206
  6.3 8.9 %collective-permute-done.refs_2_ = bf16[2,144,768]{2,1,0:T(8,128)(2,1)S(1)} collective-permute-done((bf16[2,144,768]{2,1,0:T(8,128)(2,1)S(1)}, bf16[2,144,768]{2,1,0:T(8,128)(2,1)S(1)}, u32[]{:S(2)}, u32[]{:S(2)}) %collective-permute-start) | collective-permute-done | bytes 442400 | tf_op jit(solution)/shard_map/ppermute | solution.py:206
  15.2 2.1 %collective-permute-start.4 = (bf16[2,144,768]{2,1,0:T(8,128)(2,1)S(1)}, bf16[2,144,768]{2,1,0:T(8,128)(2,1)S(1)}, u32[]{:S(2)}, u32[]{:S(2)}) collective-permute-start(bf16[2,144,768]{2,1,0:T(8,128)(2,1)S(1)} %collective-permute-done.refs_2_), channel_id=1, source_target_pairs={{0,2},{2,4},{4,6},{6,7},{7,5},{5,3},{3,1},{1,0},{8,10},{10,12},{12... | collective-permute-start | bytes 1327112 | tf_op jit(solution)/shard_map/ppermute | solution.py:206
  18.1 6.7 %collective-permute-done.2.refs_4_ = bf16[2,144,768]{2,1,0:T(8,128)(2,1)S(1)} collective-permute-done((bf16[2,144,768]{2,1,0:T(8,128)(2,1)S(1)}, bf16[2,144,768]{2,1,0:T(8,128)(2,1)S(1)}, u32[]{:S(2)}, u32[]{:S(2)}) %collective-permute-start.2) | collective-permute-done | bytes 442400 | tf_op jit(solution)/shard_map/ppermute | solution.py:206
  24.7 2.2 %collective-permute-done.3.refs_5_ = bf16[2,144,768]{2,1,0:T(8,128)(2,1)S(1)} collective-permute-done((bf16[2,144,768]{2,1,0:T(8,128)(2,1)S(1)}, bf16[2,144,768]{2,1,0:T(8,128)(2,1)S(1)}, u32[]{:S(2)}, u32[]{:S(2)}) %collective-permute-start.3) | collective-permute-done | bytes 442400 | tf_op jit(solution)/shard_map/ppermute | solution.py:207
  26.9 6.5 %collective-permute-done.4.refs_6_ = bf16[2,144,768]{2,1,0:T(8,128)(2,1)S(1)} collective-permute-done((bf16[2,144,768]{2,1,0:T(8,128)(2,1)S(1)}, bf16[2,144,768]{2,1,0:T(8,128)(2,1)S(1)}, u32[]{:S(2)}, u32[]{:S(2)}) %collective-permute-start.4) | collective-permute-done | bytes 442400 | tf_op jit(solution)/shard_map/ppermute | solution.py:206
  35.7 7.3 %cross.4 = (f32[1152,384]{1,0:T(8,128)}, bf16[1152,384]{1,0:T(8,128)(2,1)}) custom-call(s32[3]{0:T(128)} %pad_add_fusion.flags, bf16[2,768,768]{2,1,0:T(8,128)(2,1)} %bitcast.4, bf16[2,144,768]{2,1,0:T(8,128)(2,1)} %copy-done.9, bf16[2,144,768]{2,1,0:T(8,128)(2,1)} %copy-done.8, bf16[2,144,768]{2,1,0:T(8,128)(2,1)} %copy-done.17, ...), custom_call_target="tpu_custom_call" | custom-call | flops 2717908992 | bytes 9437184 | tf_op jit(solution)/shard_map/cross/pallas_call | solution.py:60
  43.0 1.6 %collective-permute-start.6 = (bf16[2,144,768]{2,1,0:T(8,128)(2,1)}, bf16[2,144,768]{2,1,0:T(8,128)(2,1)S(1)}, u32[]{:S(2)}, u32[]{:S(2)}) collective-permute-start(bf16[2,144,768]{2,1,0:T(8,128)(2,1)} %copy-done.19), channel_id=1, source_target_pairs={{0,2},{2,4},{4,6},{6,7},{7,5},{5,3},{3,1},{1,0},{8,10},{10,12},{12... | collective-permute-start | bytes 1327112 | tf_op jit(solution)/shard_map/ppermute | solution.py:206
  46.8 1.6 %collective-permute-start.8 = (bf16[2,144,768]{2,1,0:T(8,128)(2,1)}, bf16[2,144,768]{2,1,0:T(8,128)(2,1)}, u32[]{:S(2)}, u32[]{:S(2)}) collective-permute-start(bf16[2,144,768]{2,1,0:T(8,128)(2,1)} %copy-done.21), channel_id=1, source_target_pairs={{0,2},{2,4},{4,6},{6,7},{7,5},{5,3},{3,1},{1,0},{8,10},{10,12},{12... | collective-permute-start | bytes 1327112 | tf_op jit(solution)/shard_map/ppermute | solution.py:206
  48.8 7.4 %collective-permute-done.6.refs_0_.refs_8_ = bf16[2,144,768]{2,1,0:T(8,128)(2,1)S(1)} collective-permute-done((bf16[2,144,768]{2,1,0:T(8,128)(2,1)}, bf16[2,144,768]{2,1,0:T(8,128)(2,1)S(1)}, u32[]{:S(2)}, u32[]{:S(2)}) %collective-permute-start.6) | collective-permute-done | bytes 442400 | tf_op jit(solution)/shard_map/ppermute | solution.py:206
  56.2 1.6 %collective-permute-start.10 = (bf16[2,144,768]{2,1,0:T(8,128)(2,1)S(1)}, bf16[2,144,768]{2,1,0:T(8,128)(2,1)S(1)}, u32[]{:S(2)}, u32[]{:S(2)}) collective-permute-start(bf16[2,144,768]{2,1,0:T(8,128)(2,1)S(1)} %collective-permute-done.6.refs_0_.refs_8_), channel_id=1, source_target_pairs={{0,2},{2,4},{4,6},{6,7},{7,5},{5,3},{3,1},{1,0},{8,10},{10,12},{12... | collective-permute-start | bytes 1327112 | tf_op jit(solution)/shard_map/ppermute | solution.py:206
  58.2 1.7 %fusion = bf16[1152,384]{1,0:T(8,128)(2,1)S(1)} fusion(f32[1152,384]{1,0:T(8,128)} %get-tuple-element.13, bf16[1152,384]{1,0:T(8,128)(2,1)S(1)} %collective-permute-done.12), kind=kLoop, calls=%fused_computation.2 | loop fusion | flops 1327104 | bytes 3538944 | tf_op jit(solution)/shard_map/convert_element_type | solution.py:233
  61.5 4.3 %collective-permute-done.8.refs_2_.refs_10_ = bf16[2,144,768]{2,1,0:T(8,128)(2,1)} collective-permute-done((bf16[2,144,768]{2,1,0:T(8,128)(2,1)}, bf16[2,144,768]{2,1,0:T(8,128)(2,1)}, u32[]{:S(2)}, u32[]{:S(2)}) %collective-permute-start.8) | collective-permute-done | bytes 442400 | tf_op jit(solution)/shard_map/ppermute | solution.py:206
  68.1 4.9 %cross.5 = (f32[576,384]{1,0:T(8,128)}, bf16[576,384]{1,0:T(8,128)(2,1)}) custom-call(s32[3]{0:T(128)} %pad_add_fusion.flags, bf16[2,768,768]{2,1,0:T(8,128)(2,1)} %bitcast.5, bf16[2,144,768]{2,1,0:T(8,128)(2,1)} %copy-done.23, bf16[2,144,768]{2,1,0:T(8,128)(2,1)} %copy-done.24, bf16[2,144,768]{2,1,0:T(8,128)(2,1)} %collective-permute-done.8.refs_2_.refs_10_, ...), custom_call_target="tpu_custom_call" | custom-call | flops 1358954496 | bytes 5898240 | tf_op jit(solution)/shard_map/cross/pallas_call | solution.py:60
  72.9 1.8 %collective-permute-done.10.refs_0_.refs_12_ = bf16[2,144,768]{2,1,0:T(8,128)(2,1)S(1)} collective-permute-done((bf16[2,144,768]{2,1,0:T(8,128)(2,1)S(1)}, bf16[2,144,768]{2,1,0:T(8,128)(2,1)S(1)}, u32[]{:S(2)}, u32[]{:S(2)}) %collective-permute-start.10) | collective-permute-done | bytes 442400 | tf_op jit(solution)/shard_map/ppermute | solution.py:206
  76.8 3.6 %cross.6 = (f32[288,384]{1,0:T(8,128)}, bf16[288,384]{1,0:T(8,128)(2,1)}) custom-call(s32[3]{0:T(128)} %pad_add_fusion.flags, bf16[2,768,768]{2,1,0:T(8,128)(2,1)} %bitcast.6, bf16[2,144,768]{2,1,0:T(8,128)(2,1)} %copy-done.10, bf16[2,144,768]{2,1,0:T(8,128)(2,1)} %copy-done.11), custom_call_target="tpu_custom_call" | custom-call | flops 679477248 | bytes 4128768 | tf_op jit(solution)/shard_map/cross/pallas_call | solution.py:60
  83.9 1.7 %fusion.2 = bf16[288,384]{1,0:T(8,128)(2,1)} fusion(f32[288,384]{1,0:T(8,128)} %get-tuple-element.17, bf16[288,384]{1,0:T(8,128)(2,1)S(1)} %collective-permute-done.16), kind=kLoop, calls=%fused_computation.10 | loop fusion | flops 331776 | bytes 884736 | tf_op jit(solution)/shard_map/convert_element_type | solution.py:233
  87.9 6.8 %collective-permute-done.21.refs_0_ = bf16[2,144,768]{2,1,0:T(8,128)(2,1)S(1)} collective-permute-done((bf16[2,144,768]{2,1,0:T(8,128)(2,1)}, bf16[2,144,768]{2,1,0:T(8,128)(2,1)S(1)}, u32[]{:S(2)}, u32[]{:S(2)}) %collective-permute-start.21) | collective-permute-done | bytes 442400 | tf_op jit(solution)/shard_map/ppermute | solution.py:209
  96.8 3.6 %cross.7 = (f32[288,384]{1,0:T(8,128)}, bf16[288,384]{1,0:T(8,128)(2,1)}) custom-call(s32[3]{0:T(128)} %pad_add_fusion.flags, bf16[2,768,768]{2,1,0:T(8,128)(2,1)} %bitcast.7, bf16[2,144,768]{2,1,0:T(8,128)(2,1)} %copy-done.4, bf16[2,144,768]{2,1,0:T(8,128)(2,1)} %copy-done.5), custom_call_target="tpu_custom_call" | custom-call | flops 679477248 | bytes 4128768 | tf_op jit(solution)/shard_map/cross/pallas_call | solution.py:60
  105.5 2.5 %turn.1.left_ref = bf16[2,768,288]{2,1,0:T(8,128)(2,1)} custom-call(bf16[2,144,768]{2,1,0:T(8,128)(2,1)} %copy-done.4, bf16[2,144,768]{2,1,0:T(8,128)(2,1)} %copy-done.5), custom_call_target="tpu_custom_call" | custom-call | bytes 1769472 | tf_op jit(solution)/shard_map/turn/pallas_call | solution.py:141
  108.0 1.6 %collective-permute-done.24 = bf16[288,384]{1,0:T(8,128)(2,1)S(1)} collective-permute-done((bf16[288,384]{1,0:T(8,128)(2,1)S(1)}, bf16[288,384]{1,0:T(8,128)(2,1)S(1)}, u32[]{:S(2)}, u32[]{:S(2)}) %collective-permute-start.24) | collective-permute-done | bytes 221216 | tf_op jit(solution)/shard_map/ppermute | solution.py:225
  111.5 13.7 %numer.1.acc_ref = f32[2,768,768]{2,1,0:T(8,128)} custom-call(s32[3]{0:T(128)} %pad_add_fusion.flags, bf16[2,768,768]{2,1,0:T(8,128)(2,1)} %bitcast.8, bf16[768,768]{1,0:T(8,128)(2,1)} %fock_ref.1, bf16[2,144,768]{2,1,0:T(8,128)(2,1)} %copy-done.9, bf16[2,144,768]{2,1,0:T(8,128)(2,1)} %copy-done.8, bf16[2,144,768]{2,1,0:T(8,128)(2,1)} %copy-done.17, ...), custom_call_target="tpu_custom_call" | custom-call | flops 6568280064 | bytes 16367616 | tf_op jit(solution)/shard_map/numer/pallas_call | solution.py:114
  126.0 7.3 %final.1 = bf16[2,1,768,768]{3,2,1,0:T(8,128)(2,1)} custom-call(s32[3]{0:T(128)} %pad_add_fusion.flags, f32[2]{0:T(128)} %dynamic_slice.6.eps_first, f32[2,768,768]{2,1,0:T(8,128)} %numer.1.acc_ref, bf16[2,768,288]{2,1,0:T(8,128)(2,1)} %turn.1.left_ref, bf16[2,1,768,768]{3,2,1,0:T(8,128)(2,1)} %t_ref.1, bf16[288,384]{1,0:T(8,128)(2,1)} %copy-done.7, ...), custom_call_target="tpu_custom_call" | custom-call | flops 679477248 | bytes 9437184 | tf_op jit(solution)/shard_map/final/pallas_call | solution.py:165
  (109 shorter events, 28.6 us)
Async XLA Ops:
  1.2 14.0 %collective-permute-start = (bf16[2,144,768]{2,1,0:T(8,128)(2,1)S(1)}, bf16[2,144,768]{2,1,0:T(8,128)(2,1)S(1)}, u32[]{:S(2)}, u32[]{:S(2)}) collective-permute-start(bf16[2,144,768]{2,1,0:T(8,128)(2,1)S(1)} %get-tuple-element.22.refs_0_), channel_id=1, source_target_pairs={{0,2},{2,4},{4,6},{6,7},{7,5},{5,3},{3,1},{1,0},{8,10},{10,12},{12... | collective-permute-start | bytes 1327112 | tf_op jit(solution)/shard_map/ppermute | solution.py:206
  4.3 13.1 %collective-permute-start.1 = (bf16[2,144,768]{2,1,0:T(8,128)(2,1)S(1)}, bf16[2,144,768]{2,1,0:T(8,128)(2,1)S(1)}, u32[]{:S(2)}, u32[]{:S(2)}) collective-permute-start(bf16[2,144,768]{2,1,0:T(8,128)(2,1)S(1)} %get-tuple-element.22.refs_0_), channel_id=1, source_target_pairs={{2,0},{4,2},{6,4},{7,6},{5,7},{3,5},{1,3},{0,1},{10,8},{12,10},{14... | collective-permute-start | bytes 1327112 | tf_op jit(solution)/shard_map/ppermute | solution.py:207
  4.3 20.4 %collective-permute-start.2 = (bf16[2,144,768]{2,1,0:T(8,128)(2,1)S(1)}, bf16[2,144,768]{2,1,0:T(8,128)(2,1)S(1)}, u32[]{:S(2)}, u32[]{:S(2)}) collective-permute-start(bf16[2,144,768]{2,1,0:T(8,128)(2,1)S(1)} %get-tuple-element.21.refs_1_), channel_id=1, source_target_pairs={{0,2},{2,4},{4,6},{6,7},{7,5},{5,3},{3,1},{1,0},{8,10},{10,12},{12... | collective-permute-start | bytes 1327112 | tf_op jit(solution)/shard_map/ppermute | solution.py:206
  6.3 20.5 %collective-permute-start.3 = (bf16[2,144,768]{2,1,0:T(8,128)(2,1)S(1)}, bf16[2,144,768]{2,1,0:T(8,128)(2,1)S(1)}, u32[]{:S(2)}, u32[]{:S(2)}) collective-permute-start(bf16[2,144,768]{2,1,0:T(8,128)(2,1)S(1)} %get-tuple-element.21.refs_1_), channel_id=1, source_target_pairs={{2,0},{4,2},{6,4},{7,6},{5,7},{3,5},{1,3},{0,1},{10,8},{12,10},{14... | collective-permute-start | bytes 1327112 | tf_op jit(solution)/shard_map/ppermute | solution.py:207
  15.2 18.1 %collective-permute-start.4 = (bf16[2,144,768]{2,1,0:T(8,128)(2,1)S(1)}, bf16[2,144,768]{2,1,0:T(8,128)(2,1)S(1)}, u32[]{:S(2)}, u32[]{:S(2)}) collective-permute-start(bf16[2,144,768]{2,1,0:T(8,128)(2,1)S(1)} %collective-permute-done.refs_2_), channel_id=1, source_target_pairs={{0,2},{2,4},{4,6},{6,7},{7,5},{5,3},{3,1},{1,0},{8,10},{10,12},{12... | collective-permute-start | bytes 1327112 | tf_op jit(solution)/shard_map/ppermute | solution.py:206
  17.4 17.5 %collective-permute-start.5 = (bf16[2,144,768]{2,1,0:T(8,128)(2,1)S(1)}, bf16[2,144,768]{2,1,0:T(8,128)(2,1)S(1)}, u32[]{:S(2)}, u32[]{:S(2)}) collective-permute-start(bf16[2,144,768]{2,1,0:T(8,128)(2,1)S(1)} %collective-permute-done.1.refs_3_), channel_id=1, source_target_pairs={{2,0},{4,2},{6,4},{7,6},{5,7},{3,5},{1,3},{0,1},{10,8},{12,10},{14... | collective-permute-start | bytes 1327112 | tf_op jit(solution)/shard_map/ppermute | solution.py:207
  43.0 15.2 %collective-permute-start.12 = (bf16[1152,384]{1,0:T(8,128)(2,1)}, bf16[1152,384]{1,0:T(8,128)(2,1)S(1)}, u32[]{:S(2)}, u32[]{:S(2)}) collective-permute-start(bf16[1152,384]{1,0:T(8,128)(2,1)} %get-tuple-element.14), channel_id=1, source_target_pairs={{0,8},{8,0},{16,24},{24,16},{1,9},{9,1},{17,25},{25,17},{2,10},{10... | collective-permute-start | bytes 2654216 | tf_op jit(solution)/shard_map/ppermute | solution.py:225
  43.0 13.2 %collective-permute-start.6 = (bf16[2,144,768]{2,1,0:T(8,128)(2,1)}, bf16[2,144,768]{2,1,0:T(8,128)(2,1)S(1)}, u32[]{:S(2)}, u32[]{:S(2)}) collective-permute-start(bf16[2,144,768]{2,1,0:T(8,128)(2,1)} %copy-done.19), channel_id=1, source_target_pairs={{0,2},{2,4},{4,6},{6,7},{7,5},{5,3},{3,1},{1,0},{8,10},{10,12},{12... | collective-permute-start | bytes 1327112 | tf_op jit(solution)/shard_map/ppermute | solution.py:206
  44.6 13.2 %collective-permute-start.7 = (bf16[2,144,768]{2,1,0:T(8,128)(2,1)}, bf16[2,144,768]{2,1,0:T(8,128)(2,1)S(1)}, u32[]{:S(2)}, u32[]{:S(2)}) collective-permute-start(bf16[2,144,768]{2,1,0:T(8,128)(2,1)} %copy-done.20), channel_id=1, source_target_pairs={{2,0},{4,2},{6,4},{7,6},{5,7},{3,5},{1,3},{0,1},{10,8},{12,10},{14... | collective-permute-start | bytes 1327112 | tf_op jit(solution)/shard_map/ppermute | solution.py:207
  46.8 19.0 %collective-permute-start.8 = (bf16[2,144,768]{2,1,0:T(8,128)(2,1)}, bf16[2,144,768]{2,1,0:T(8,128)(2,1)}, u32[]{:S(2)}, u32[]{:S(2)}) collective-permute-start(bf16[2,144,768]{2,1,0:T(8,128)(2,1)} %copy-done.21), channel_id=1, source_target_pairs={{0,2},{2,4},{4,6},{6,7},{7,5},{5,3},{3,1},{1,0},{8,10},{10,12},{12... | collective-permute-start | bytes 1327112 | tf_op jit(solution)/shard_map/ppermute | solution.py:206
  48.4 18.9 %collective-permute-start.9 = (bf16[2,144,768]{2,1,0:T(8,128)(2,1)}, bf16[2,144,768]{2,1,0:T(8,128)(2,1)S(1)}, u32[]{:S(2)}, u32[]{:S(2)}) collective-permute-start(bf16[2,144,768]{2,1,0:T(8,128)(2,1)} %copy-done.22), channel_id=1, source_target_pairs={{2,0},{4,2},{6,4},{7,6},{5,7},{3,5},{1,3},{0,1},{10,8},{12,10},{14... | collective-permute-start | bytes 1327112 | tf_op jit(solution)/shard_map/ppermute | solution.py:207
  56.2 18.6 %collective-permute-start.10 = (bf16[2,144,768]{2,1,0:T(8,128)(2,1)S(1)}, bf16[2,144,768]{2,1,0:T(8,128)(2,1)S(1)}, u32[]{:S(2)}, u32[]{:S(2)}) collective-permute-start(bf16[2,144,768]{2,1,0:T(8,128)(2,1)S(1)} %collective-permute-done.6.refs_0_.refs_8_), channel_id=1, source_target_pairs={{0,2},{2,4},{4,6},{6,7},{7,5},{5,3},{3,1},{1,0},{8,10},{10,12},{12... | collective-permute-start | bytes 1327112 | tf_op jit(solution)/shard_map/ppermute | solution.py:206
  57.8 18.3 %collective-permute-start.11 = (bf16[2,144,768]{2,1,0:T(8,128)(2,1)S(1)}, bf16[2,144,768]{2,1,0:T(8,128)(2,1)S(1)}, u32[]{:S(2)}, u32[]{:S(2)}) collective-permute-start(bf16[2,144,768]{2,1,0:T(8,128)(2,1)S(1)} %collective-permute-done.7.refs_1_.refs_9_), channel_id=1, source_target_pairs={{2,0},{4,2},{6,4},{7,6},{5,7},{3,5},{1,3},{0,1},{10,8},{12,10},{14... | collective-permute-start | bytes 1327112 | tf_op jit(solution)/shard_map/ppermute | solution.py:207
  59.9 40.4 %collective-permute-start.13 = (bf16[1152,384]{1,0:T(8,128)(2,1)S(1)}, bf16[1152,384]{1,0:T(8,128)(2,1)S(1)}, u32[]{:S(2)}, u32[]{:S(2)}) collective-permute-start(bf16[1152,384]{1,0:T(8,128)(2,1)S(1)} %fusion), channel_id=1, source_target_pairs={{0,16},{8,24},{16,0},{24,8},{1,17},{9,25},{17,1},{25,9},{2,18},{10... | collective-permute-start | bytes 2654216 | tf_op jit(solution)/shard_map/ppermute | solution.py:225
  72.9 14.3 %collective-permute-start.14 = (bf16[576,384]{1,0:T(8,128)(2,1)}, bf16[576,384]{1,0:T(8,128)(2,1)S(1)}, u32[]{:S(2)}, u32[]{:S(2)}) collective-permute-start(bf16[576,384]{1,0:T(8,128)(2,1)} %get-tuple-element.16), channel_id=1, source_target_pairs={{0,8},{8,0},{16,24},{24,16},{1,9},{9,1},{17,25},{25,17},{2,10},{10... | collective-permute-start | bytes 1327112 | tf_op jit(solution)/shard_map/ppermute | solution.py:225
  81.9 12.8 %collective-permute-start.21 = (bf16[2,144,768]{2,1,0:T(8,128)(2,1)}, bf16[2,144,768]{2,1,0:T(8,128)(2,1)S(1)}, u32[]{:S(2)}, u32[]{:S(2)}) collective-permute-start(bf16[2,144,768]{2,1,0:T(8,128)(2,1)} %collective-permute-done.8.refs_2_.refs_10_), channel_id=1, source_target_pairs={{0,2},{2,4},{4,6},{6,7},{7,5},{5,3},{3,1},{1,0},{8,10},{10,12},{12... | collective-permute-start | bytes 1327112 | tf_op jit(solution)/shard_map/ppermute | solution.py:209
  83.5 12.5 %collective-permute-start.22 = (bf16[2,144,768]{2,1,0:T(8,128)(2,1)}, bf16[2,144,768]{2,1,0:T(8,128)(2,1)S(1)}, u32[]{:S(2)}, u32[]{:S(2)}) collective-permute-start(bf16[2,144,768]{2,1,0:T(8,128)(2,1)} %copy-done.11), channel_id=1, source_target_pairs={{2,0},{4,2},{6,4},{7,6},{5,7},{3,5},{1,3},{0,1},{10,8},{12,10},{14... | collective-permute-start | bytes 1327112 | tf_op jit(solution)/shard_map/ppermute | solution.py:209
  85.7 18.2 %collective-permute-start.17 = (bf16[288,384]{1,0:T(8,128)(2,1)}, bf16[288,384]{1,0:T(8,128)(2,1)}, u32[]{:S(2)}, u32[]{:S(2)}) collective-permute-start(bf16[288,384]{1,0:T(8,128)(2,1)} %fusion.2), channel_id=1, source_target_pairs={{0,16},{8,24},{16,0},{24,8},{1,17},{9,25},{17,1},{25,9},{2,18},{10... | collective-permute-start | bytes 663560 | tf_op jit(solution)/shard_map/ppermute | solution.py:225
  87.3 16.4 %collective-permute-start.15 = (bf16[576,384]{1,0:T(8,128)(2,1)S(1)}, bf16[576,384]{1,0:T(8,128)(2,1)S(1)}, u32[]{:S(2)}, u32[]{:S(2)}) collective-permute-start(bf16[576,384]{1,0:T(8,128)(2,1)S(1)} %fusion.1), channel_id=1, source_target_pairs={{0,16},{8,24},{16,0},{24,8},{1,17},{9,25},{17,1},{25,9},{2,18},{10... | collective-permute-start | bytes 1327112 | tf_op jit(solution)/shard_map/ppermute | solution.py:225
  100.7 9.2 %collective-permute-start.18 = (bf16[1152,384]{1,0:T(8,128)(2,1)S(1)}, bf16[1152,384]{1,0:T(8,128)(2,1)S(1)}, u32[]{:S(2)}, u32[]{:S(2)}) collective-permute-start(bf16[1152,384]{1,0:T(8,128)(2,1)S(1)} %add_convert_fusion.refs_14_), channel_id=1, source_target_pairs={{0,8},{8,0},{16,24},{24,16},{1,9},{9,1},{17,25},{25,17},{2,10},{10... | collective-permute-start | bytes 2654216 | tf_op jit(solution)/shard_map/ppermute | solution.py:225
  102.1 7.5 %collective-permute-start.24 = (bf16[288,384]{1,0:T(8,128)(2,1)S(1)}, bf16[288,384]{1,0:T(8,128)(2,1)S(1)}, u32[]{:S(2)}, u32[]{:S(2)}) collective-permute-start(bf16[288,384]{1,0:T(8,128)(2,1)S(1)} %fusion.3), channel_id=1, source_target_pairs={{0,16},{8,24},{16,0},{24,8},{1,17},{9,25},{17,1},{25,9},{2,18},{10... | collective-permute-start | bytes 663560 | tf_op jit(solution)/shard_map/ppermute | solution.py:225
  103.8 6.0 %collective-permute-start.19 = (bf16[576,384]{1,0:T(8,128)(2,1)S(1)}, bf16[576,384]{1,0:T(8,128)(2,1)S(1)}, u32[]{:S(2)}, u32[]{:S(2)}) collective-permute-start(bf16[576,384]{1,0:T(8,128)(2,1)S(1)} %add_convert_fusion.1.refs_15_), channel_id=1, source_target_pairs={{0,8},{8,0},{16,24},{24,16},{1,9},{9,1},{17,25},{25,17},{2,10},{10... | collective-permute-start | bytes 1327112 | tf_op jit(solution)/shard_map/ppermute | solution.py:225
  105.0 4.8 %collective-permute-start.20 = (bf16[288,384]{1,0:T(8,128)(2,1)S(1)}, bf16[288,384]{1,0:T(8,128)(2,1)S(1)}, u32[]{:S(2)}, u32[]{:S(2)}) collective-permute-start(bf16[288,384]{1,0:T(8,128)(2,1)S(1)} %add_convert_fusion.3.refs_16_), channel_id=1, source_target_pairs={{0,8},{8,0},{16,24},{24,16},{1,9},{9,1},{17,25},{25,17},{2,10},{10... | collective-permute-start | bytes 663560 | tf_op jit(solution)/shard_map/ppermute | solution.py:225
  109.7 15.5 %collective-permute-start.25 = (bf16[288,384]{1,0:T(8,128)(2,1)S(1)}, bf16[288,384]{1,0:T(8,128)(2,1)S(1)}, u32[]{:S(2)}, u32[]{:S(2)}) collective-permute-start(bf16[288,384]{1,0:T(8,128)(2,1)S(1)} %add_convert_fusion.2.mine), channel_id=1, source_target_pairs={{0,8},{8,0},{16,24},{24,16},{1,9},{9,1},{17,25},{25,17},{2,10},{10... | collective-permute-start | bytes 663560 | tf_op jit(solution)/shard_map/ppermute | solution.py:225
  (31 other events, 227.0 us)

commit v2 on v0

v2 whole, which is shorter than its diff:
```python
import functools

import jax
import jax.numpy as jnp
from jax import lax
from jax.experimental import pallas as pl
from jax.experimental.pallas import tpu as pltpu
from jax.sharding import PartitionSpec as P

MIB = 1024 * 1024
VMEM = pl.BlockSpec(memory_space=pltpu.VMEM)
SMEM = pl.BlockSpec(memory_space=pltpu.SMEM)


def cost(flops, moved):
    return pl.CostEstimate(
        flops=flops // 1000 + 1, bytes_accessed=moved // 1000 + 1, transcendentals=0
    )


def ring_order(n):
    low = max(d for d in range(1, n + 1) if n % d == 0 and d * d <= n)
    high = n // low
    if low == 1 or high % 2:
        return list(range(n))
    order = [h * low for h in range(high)]
    for turn, h in enumerate(reversed(range(high))):
        lows = range(1, low) if turn % 2 == 0 else range(low - 1, 0, -1)
        order += [h * low + l for l in lows]
    return order


def after(values, gate):
    return lax.optimization_barrier((values, gate))[0]


def cross_kernel(flags, t_ref, *refs):
    chunks, (keep_ref, send_ref) = refs[:-2], refs[-2:]
    occ, vir = t_ref.shape[0], t_ref.shape[2]
    half = vir // 2
    first = flags[0] == 0
    at = 0
    for c in chunks:
        total = None
        for k in range(occ):
            part = jnp.dot(c[k], t_ref[k], preferred_element_type=jnp.float32)
            part = part + jnp.where(flags[2 + k] == 1, c[k].astype(jnp.float32), 0.0)
            total = part if total is None else total + part
        low, high = total[:, :half], total[:, half:]
        rows = slice(at, at + c.shape[1])
        keep_ref[rows, :] = jnp.where(first, low, high)
        send_ref[rows, :] = jnp.where(first, high, low).astype(send_ref.dtype)
        at += c.shape[1]


def cross(flags, t, chunks):
    rows = sum(c.shape[1] for c in chunks)
    occ, _, vir = t.shape
    return pl.pallas_call(
        cross_kernel,
        out_shape=(
            jax.ShapeDtypeStruct((rows, vir // 2), jnp.float32),
            jax.ShapeDtypeStruct((rows, vir // 2), jnp.bfloat16),
        ),
        in_specs=[SMEM] + [VMEM] * (1 + len(chunks)),
        out_specs=(VMEM, VMEM),
        compiler_params=pltpu.CompilerParams(vmem_limit_bytes=20 * MIB),
        cost_estimate=cost(2 * rows * vir * vir * occ, 2 * t.size + 2 * rows * vir * (occ + 2)),
        name="cross",
    )(flags, t, *chunks)


def dressed_rows(flags, mine, other):
    first = flags[0] == 0
    return jnp.concatenate(
        [jnp.where(first, mine, other), jnp.where(first, other, mine)], axis=1
    )


def tiles(vir):
    step = 256 if vir % 256 == 0 else vir
    return [slice(start, start + step) for start in range(0, vir, step)]


def pair_product(chunks, dressed, k, cols):
    left = jnp.concatenate([c[k, :, cols] for c in chunks], axis=0)
    return lax.dot_general(
        left, dressed, (((0,), (0,)), ((), ())), preferred_element_type=jnp.float32
    )


def numer_kernel(n_chunks, n_groups, fresh, flags, *refs):
    refs = list(refs)
    lead = [refs.pop(0) for _ in range(2 if fresh else 1)]
    chunks = [refs.pop(0) for _ in range(n_chunks)]
    mine = [refs.pop(0) for _ in range(n_groups)]
    other = [refs.pop(0) for _ in range(n_groups)]
    out_ref, dressed = refs
    at = 0
    for m, o in zip(mine, other):
        dressed[at:at + m.shape[0], :] = dressed_rows(flags, m[...], o[...])
        at += m.shape[0]
    occ, vir = out_ref.shape[:2]
    for k in range(occ):
        for cols in tiles(vir):
            if fresh:
                total = jnp.dot(
                    lead[0][k, cols, :], lead[1][...], preferred_element_type=jnp.float32
                )
            else:
                total = lead[0][k, cols, :]
            out_ref[k, cols, :] = total + pair_product(chunks, dressed[...], k, cols)


def numer(flags, lead, chunk_groups, mine, other):
    fresh = len(lead) == 2
    chunks = [c for group in chunk_groups for c in group]
    rows = sum(c.shape[1] for c in chunks)
    occ, vir = lead[0].shape[:2]
    operands = [flags, *lead, *chunks, *mine, *other]
    return pl.pallas_call(
        functools.partial(numer_kernel, len(chunks), len(mine), fresh),
        out_shape=jax.ShapeDtypeStruct((occ, vir, vir), jnp.float32),
        in_specs=[SMEM] + [VMEM] * (len(operands) - 1),
        out_specs=VMEM,
        input_output_aliases={} if fresh else {1: 0},
        scratch_shapes=[pltpu.VMEM((rows, vir), jnp.bfloat16)],
        compiler_params=pltpu.CompilerParams(vmem_limit_bytes=30 * MIB),
        cost_estimate=cost(
            2 * occ * vir * vir * (rows + vir * fresh),
            2 * rows * vir * (occ + 1) + 6 * occ * vir * vir,
        ),
        name="numer",
    )(*operands)


def final_kernel(n_chunks, n_groups, flags, eps_occ, acc_ref, t_ref, eps_row, eps_col, *refs):
    refs = list(refs)
    chunks = [refs.pop(0) for _ in range(n_chunks)]
    mine = [refs.pop(0) for _ in range(n_groups)]
    other = [refs.pop(0) for _ in range(n_groups)]
    out_ref, dressed, tile, sems = refs
    at = 0
    for m, o in zip(mine, other):
        dressed[at:at + m.shape[0], :] = dressed_rows(flags, m[...], o[...])
        at += m.shape[0]
    occ, vir = acc_ref.shape[:2]
    second = eps_occ[flags[1]]
    copies = []
    for k in range(occ):
        first = eps_occ[flags[2 + occ] + k]
        for n, cols in enumerate(tiles(vir)):
            total = acc_ref[k, cols, :] + pair_product(chunks, dressed[...], k, cols)
            denom = (eps_col[cols, :] - first) + (eps_row[...] - second)
            new = t_ref[k, cols, :].astype(jnp.float32) - total / denom
            tile[k, cols, :] = new.astype(tile.dtype)
            copy = pltpu.make_async_copy(
                tile.at[k, cols, :], out_ref.at[k, 0, cols, :], sems.at[k, n]
            )
            copy.start()
            copies.append(copy)
    for copy in copies:
        copy.wait()


def final(flags, eps_occ, acc, t, eps_vir, chunk_groups, mine, other):
    occ, vir = acc.shape[:2]
    chunks = [c for group in chunk_groups for c in group]
    rows = sum(c.shape[1] for c in chunks)
    operands = [flags, eps_occ, acc, t, eps_vir[None, :], eps_vir[:, None], *chunks, *mine, *other]
    return pl.pallas_call(
        functools.partial(final_kernel, len(chunks), len(mine)),
        out_shape=jax.ShapeDtypeStruct((occ, 1, vir, vir), t.dtype),
        in_specs=[SMEM, SMEM] + [VMEM] * (len(operands) - 2),
        out_specs=pl.BlockSpec(memory_space=pl.ANY),
        scratch_shapes=[
            pltpu.VMEM((rows, vir), t.dtype),
            pltpu.VMEM((occ, vir, vir), t.dtype),
            pltpu.SemaphoreType.DMA((occ, len(tiles(vir)))),
        ],
        compiler_params=pltpu.CompilerParams(vmem_limit_bytes=24 * MIB),
        cost_estimate=cost(2 * occ * vir * vir * rows, 8 * t.size),
        name="final",
    )(*operands)


def local(n_row, n_col, amplitudes, ints, eps_occ, eps_vir, fock_vir):
    occ = amplitudes.shape[0]
    row, col = lax.axis_index("row"), lax.axis_index("col")
    t = amplitudes[:, 0]
    shard = jnp.swapaxes(ints, 1, 2)
    q = shard.shape[1]
    cut = (q // 2 + 15) // 16 * 16

    order = ring_order(n_col)
    up = [(order[p], order[(p + 1) % n_col]) for p in range(n_col)]
    down = [(b, a) for a, b in up]

    first_ids = row * occ + jnp.arange(occ, dtype=jnp.int32)
    flags = jnp.concatenate(
        [
            jnp.stack([row % 2, col]).astype(jnp.int32),
            (first_ids == col).astype(jnp.int32),
            first_ids[:1],
        ]
    )

    def swap(x, bit):
        return lax.ppermute(x, "row", [(r, r ^ bit) for r in range(n_row)])

    last = n_col - 1
    own = [shard[:, :cut], shard[:, cut:]]
    ups, downs = list(own), list(own)
    vals = {}
    pairs = last - 3
    sizes = [1] + [2] * (pairs // 2) + [1] * (pairs % 2) + [1, 1]
    ng = len(sizes)
    ends = [sum(sizes[:n + 1]) for n in range(ng)]
    ties = {}
    for n, end in enumerate(ends[:-1]):
        z_at = "R%d" % (end + 4) if end + 4 <= last else "C%d" % (n + 1)
        ties.setdefault(z_at, []).append("Z%d" % n)
        if n < ng - 3:
            w_at = "R%d" % (end + 6) if end + 6 <= last else "C%d" % (ng - 1)
            ties.setdefault(w_at, []).append("W%d" % n)

    def tie(value, target):
        src = [vals[x] for x in ties.get(target, [])]
        return after(value, src) if src else value

    def ring_step(step):
        h = (step - 1) % 2
        up_h, down_h = (0, 1) if step == last else (h, 1 - h)
        ups[up_h], downs[down_h] = tie((ups[up_h], downs[down_h]), "R%d" % step)
        ups[up_h] = lax.ppermute(ups[up_h], "col", up)
        downs[down_h] = lax.ppermute(downs[down_h], "col", down)
        return [ups[up_h], downs[down_h]]

    groups, mine, other = [], [], []
    n0, n1 = max(ng - 4, 1), ng - 2
    numer_at = {"C%d" % (ng - 1): "N0", "G%d" % (ng - 1): "N1"}

    def through(value, target):
        name = numer_at.get(target)
        if name == "N0":
            vals[name] = numer(flags, (t, fock_vir), groups[:n0], mine[:n0], other[:n0])
        elif name == "N1":
            vals[name] = numer(flags, (vals["N0"],), groups[n0:n1], mine[n0:n1], other[n0:n1])
        if name:
            value, vals[name] = lax.optimization_barrier((value, vals[name]))
        return tie(value, target)

    group, g = list(own), 0
    for step in range(1, last + 1):
        group = group + ring_step(step)
        if step not in ends:
            continue
        group = through(group, "C%d" % g)
        total, send = cross(flags, t, group)
        total = total + swap(send, 1).astype(jnp.float32)
        bit = 2
        while bit < n_row:
            send = total.astype(jnp.bfloat16)
            vals["Z%d" % g] = send
            got = through(swap(send, bit), "G%d" % g)
            total = total + got.astype(jnp.float32)
            bit *= 2
        groups.append(group)
        total = total.astype(jnp.bfloat16)
        vals["W%d" % g] = total
        mine.append(total)
        other.append(swap(total, 1))
        group = []
        g += 1
    acc = vals["N1"]
    return final(flags, eps_occ, acc, t, eps_vir, groups[n1:], mine[n1:], other[n1:])


def solution(mesh):
    placed = (P("row", "col", None, None), P("row", None, "col"), P(), P(), P())
    body = functools.partial(local, mesh.shape["row"], mesh.shape["col"])
    return jax.shard_map(
        body, mesh=mesh, in_specs=placed, out_specs=P("row", "col", None, None), check_vma=False
    )
```

time: 251 us -> 94.8 us (0.38)
  waiting for transfers between devices: 179 us -> 42.2 us
  matrix products: 33.2 us -> 0 us
  starting transfers between devices: 0.04 us -> 25.8 us
  Pallas kernels: 0 us -> 22.1 us
  local copies, waits for them, and re-layouts: 23.8 us -> 3.05 us
  between operations: 13.4 us -> 0.46 us
    all_gather x1 -> x0, waiting for transfers between devices: 114 us -> none  [local(): full_rows = lax.all_gather(ints, 'col', axis=2, tiled=True)]
    psum x1 -> x0, waiting for transfers between devices: 64.3 us -> none  [local(): dressed = lax.psum(cross_part.astype(jnp.bfloat16), 'row')]
    ppermute x0 -> x29, waiting for transfers between devices: none -> 42.2 us  [the longest x7 30.1 us: ring_step(): ups[up_h] = lax.ppermute(ups[up_h], 'col', up)]
    dot_general x4 -> x0, matrix products: 33.2 us -> none  [the longest x1 12 us: local(): jnp.einsum('iaq,jbq->ijab', full_rows, dressed, preferred_element_type=jn...]
    ppermute x0 -> x29, starting transfers between devices: none -> 25.8 us  [the longest x7 13.2 us: ring_step(): ups[up_h] = lax.ppermute(ups[up_h], 'col', up)]
    pallas_call x0 -> x8, Pallas kernels: none -> 22.1 us  [the longest x5 9.62 us: cross(): pl.pallas_call(cross_kernel, out_shape=(jax.ShapeDtypeStruct((rows, vir /...]
    all_gather x1 -> x0, local copies, waits for them, and re-layouts: 18.3 us -> none  [local(): full_rows = lax.all_gather(ints, 'col', axis=2, tiled=True)]
  transfers between devices with their start and end apart: 2 -> 29, of which waited for: 2 -> 14; matrix products, arithmetic and copies ran while one was open for 4% -> 1% of each run, Pallas kernels for 0% -> 19%
where the time goes in v2:
time: 94.8 us; the launch traced here: 94.7 us
  waiting for transfers between devices  42.2 us (45%)
  starting transfers between devices  25.8 us (27%)
  Pallas kernels  22.1 us (23%)
  local copies, waits for them, and re-layouts  3.05 us (3%)
  other arithmetic  1.16 us (1%)
    ppermute x7, waiting for transfers between devices, ring_step(): ups[up_h] = lax.ppermute(ups[up_h], 'col', up)  30.1 us
    ppermute x7, starting transfers between devices, ring_step(): ups[up_h] = lax.ppermute(ups[up_h], 'col', up)  13.2 us
    pallas_call x5, Pallas kernels, cross(): pl.pallas_call(cross_kernel, out_shape=(jax.ShapeDtypeStruct((rows, vir /...  9.62 us
    ppermute x15, starting transfers between devices, swap(): return lax.ppermute(x, 'row', [(r, r ^ bit) for r in range(n_row)])  8.85 us
    pallas_call x2, Pallas kernels, numer(): pl.pallas_call(functools.partial(numer_kernel, len(chunks), len(mine), fr...  8.58 us
    ppermute x15, waiting for transfers between devices, swap(): return lax.ppermute(x, 'row', [(r, r ^ bit) for r in range(n_row)])  8.03 us
    ppermute x7, waiting for transfers between devices, ring_step(): downs[down_h] = lax.ppermute(downs[down_h], 'col', down)  4.01 us
    pallas_call x1, Pallas kernels, final(): pl.pallas_call(functools.partial(final_kernel, len(chunks), len(mine)), o...  3.85 us
  transfers between devices with their start and end apart: 29, of which 14 were waited for; matrix products, arithmetic and copies ran while one was open for 1% of the time, Pallas kernels for 19%

profile of v2, /device:TPU:0, one launch (start us, length us, event | category | flops | bytes accessed | tf_op | source)
XLA Modules:
  0.0 94.7 jit_solution(1589991770937358421)
XLA Ops:
  1.2 3.1 %collective-permute-start = (bf16[2,144,768]{2,1,0:T(8,128)(2,1)S(1)}, bf16[2,144,768]{2,1,0:T(8,128)(2,1)S(1)}, u32[]{:S(2)}, u32[]{:S(2)}) collective-permute-start(bf16[2,144,768]{2,1,0:T(8,128)(2,1)S(1)} %get-tuple-element.52.refs_0_.refs_2_), channel_id=1, source_target_pairs={{0,2},{2,4},{4,6},{6,7},{7,5},{5,3},{3,1},{1,0},{8,10},{10,12},{12... | collective-permute-start | bytes 1327112 | tf_op jit(solution)/shard_map/ppermute | solution.py:235
  4.3 2.0 %collective-permute-start.8 = (bf16[2,144,768]{2,1,0:T(8,128)(2,1)S(1)}, bf16[2,144,768]{2,1,0:T(8,128)(2,1)S(1)}, u32[]{:S(2)}, u32[]{:S(2)}) collective-permute-start(bf16[2,144,768]{2,1,0:T(8,128)(2,1)S(1)} %get-tuple-element.51.refs_1_.refs_3_), channel_id=1, source_target_pairs={{0,2},{2,4},{4,6},{6,7},{7,5},{5,3},{3,1},{1,0},{8,10},{10,12},{12... | collective-permute-start | bytes 1327112 | tf_op jit(solution)/shard_map/ppermute | solution.py:235
  6.4 8.8 %collective-permute-done.refs_2_.refs_4_ = bf16[2,144,768]{2,1,0:T(8,128)(2,1)S(1)} collective-permute-done((bf16[2,144,768]{2,1,0:T(8,128)(2,1)S(1)}, bf16[2,144,768]{2,1,0:T(8,128)(2,1)S(1)}, u32[]{:S(2)}, u32[]{:S(2)}) %collective-permute-start) | collective-permute-done | bytes 442400 | tf_op jit(solution)/shard_map/ppermute | solution.py:235
  15.2 2.2 %collective-permute-done.2.refs_3_.refs_5_ = bf16[2,144,768]{2,1,0:T(8,128)(2,1)S(1)} collective-permute-done((bf16[2,144,768]{2,1,0:T(8,128)(2,1)S(1)}, bf16[2,144,768]{2,1,0:T(8,128)(2,1)S(1)}, u32[]{:S(2)}, u32[]{:S(2)}) %collective-permute-start.2) | collective-permute-done | bytes 442400 | tf_op jit(solution)/shard_map/ppermute | solution.py:236
  17.4 1.7 %copy-done = bf16[2,1,768,768]{3,2,1,0:T(8,128)(2,1)S(1)} copy-done((bf16[2,1,768,768]{3,2,1,0:T(8,128)(2,1)S(1)}, bf16[2,1,768,768]{3,2,1,0:T(8,128)(2,1)}, u32[]{:S(2)}) %copy-start) | copy-done | bytes 2359320
  19.0 2.3 %cross.5 = (f32[576,384]{1,0:T(8,128)S(1)}, bf16[576,384]{1,0:T(8,128)(2,1)S(1)}) custom-call(s32[5]{0:T(128)S(1)} %pad_add_fusion.flags, bf16[2,768,768]{2,1,0:T(8,128)(2,1)S(1)} %bitcast.5, bf16[2,144,768]{2,1,0:T(8,128)(2,1)S(1)} %get-tuple-element.52.refs_0_.refs_2_, bf16[2,144,768]{2,1,0:T(8,128)(2,1)S(1)} %get-tuple-element.51.refs_1_.refs_3_, ...), custom_call_target="tpu_custom_call" | custom-call | flops 1358955 | bytes 5899 | tf_op jit(solution)/shard_map/cross/pallas_call | solution.py:59
  21.4 1.6 %collective-permute-start.1 = (bf16[2,144,768]{2,1,0:T(8,128)(2,1)S(1)}, bf16[2,144,768]{2,1,0:T(8,128)(2,1)S(1)}, u32[]{:S(2)}, u32[]{:S(2)}) collective-permute-start(bf16[2,144,768]{2,1,0:T(8,128)(2,1)S(1)} %collective-permute-done.refs_2_.refs_4_), channel_id=1, source_target_pairs={{0,2},{2,4},{4,6},{6,7},{7,5},{5,3},{3,1},{1,0},{8,10},{10,12},{12... | collective-permute-start | bytes 1327112 | tf_op jit(solution)/shard_map/ppermute | solution.py:235
  23.9 1.8 %collective-permute-start.15 = (bf16[2,144,768]{2,1,0:T(8,128)(2,1)S(1)}, bf16[2,144,768]{2,1,0:T(8,128)(2,1)S(1)}, u32[]{:S(2)}, u32[]{:S(2)}) collective-permute-start(bf16[2,144,768]{2,1,0:T(8,128)(2,1)S(1)} %collective-permute-done.8.refs_0_.refs_1_), channel_id=1, source_target_pairs={{0,2},{2,4},{4,6},{6,7},{7,5},{5,3},{3,1},{1,0},{8,10},{10,12},{12... | collective-permute-start | bytes 1327112 | tf_op jit(solution)/shard_map/ppermute | solution.py:235
  26.6 7.8 %collective-permute-done.1.refs_2_.refs_3_ = bf16[2,144,768]{2,1,0:T(8,128)(2,1)S(1)} collective-permute-done((bf16[2,144,768]{2,1,0:T(8,128)(2,1)S(1)}, bf16[2,144,768]{2,1,0:T(8,128)(2,1)S(1)}, u32[]{:S(2)}, u32[]{:S(2)}) %collective-permute-start.1) | collective-permute-done | bytes 442400 | tf_op jit(solution)/shard_map/ppermute | solution.py:235
  34.4 1.6 %collective-permute-done.3.refs_3_.refs_4_ = bf16[2,144,768]{2,1,0:T(8,128)(2,1)S(1)} collective-permute-done((bf16[2,144,768]{2,1,0:T(8,128)(2,1)S(1)}, bf16[2,144,768]{2,1,0:T(8,128)(2,1)S(1)}, u32[]{:S(2)}, u32[]{:S(2)}) %collective-permute-start.3) | collective-permute-done | bytes 442400 | tf_op jit(solution)/shard_map/ppermute | solution.py:236
  36.0 1.6 %collective-permute-start.5 = (bf16[2,144,768]{2,1,0:T(8,128)(2,1)S(1)}, bf16[2,144,768]{2,1,0:T(8,128)(2,1)S(1)}, u32[]{:S(2)}, u32[]{:S(2)}) collective-permute-start(bf16[2,144,768]{2,1,0:T(8,128)(2,1)S(1)} %collective-permute-done.1.refs_2_.refs_3_), channel_id=1, source_target_pairs={{0,2},{2,4},{4,6},{6,7},{7,5},{5,3},{3,1},{1,0},{8,10},{10,12},{12... | collective-permute-start | bytes 1327112 | tf_op jit(solution)/shard_map/ppermute | solution.py:235
  38.1 2.2 %cross.6 = (f32[576,384]{1,0:T(8,128)S(1)}, bf16[576,384]{1,0:T(8,128)(2,1)S(1)}) custom-call(s32[5]{0:T(128)S(1)} %pad_add_fusion.flags, bf16[2,768,768]{2,1,0:T(8,128)(2,1)S(1)} %bitcast.6, bf16[2,144,768]{2,1,0:T(8,128)(2,1)S(1)} %collective-permute-done.8.refs_0_.refs_1_, bf16[2,144,768]{2,1,0:T(8,128)(2,1)S(1)} %collective-permute-done.9.refs_1_.refs_2_, ...), custom_call_target="tpu_custom_call" | custom-call | flops 1358955 | bytes 5899 | tf_op jit(solution)/shard_map/cross/pallas_call | solution.py:59
  40.4 3.5 %collective-permute-done.15.refs_0_.refs_5_ = bf16[2,144,768]{2,1,0:T(8,128)(2,1)S(1)} collective-permute-done((bf16[2,144,768]{2,1,0:T(8,128)(2,1)S(1)}, bf16[2,144,768]{2,1,0:T(8,128)(2,1)S(1)}, u32[]{:S(2)}, u32[]{:S(2)}) %collective-permute-start.15) | collective-permute-done | bytes 442400 | tf_op jit(solution)/shard_map/ppermute | solution.py:235
  45.5 1.6 %collective-permute-start.16 = (bf16[2,144,768]{2,1,0:T(8,128)(2,1)S(1)}, bf16[2,144,768]{2,1,0:T(8,128)(2,1)S(1)}, u32[]{:S(2)}, u32[]{:S(2)}) collective-permute-start(bf16[2,144,768]{2,1,0:T(8,128)(2,1)S(1)} %collective-permute-done.15.refs_0_.refs_5_), channel_id=1, source_target_pairs={{0,2},{2,4},{4,6},{6,7},{7,5},{5,3},{3,1},{1,0},{8,10},{10,12},{12... | collective-permute-start | bytes 1327112 | tf_op jit(solution)/shard_map/ppermute | solution.py:235
  47.1 6.3 %collective-permute-done.5.refs_2_.refs_7_ = bf16[2,144,768]{2,1,0:T(8,128)(2,1)S(1)} collective-permute-done((bf16[2,144,768]{2,1,0:T(8,128)(2,1)S(1)}, bf16[2,144,768]{2,1,0:T(8,128)(2,1)S(1)}, u32[]{:S(2)}, u32[]{:S(2)}) %collective-permute-start.5) | collective-permute-done | bytes 442400 | tf_op jit(solution)/shard_map/ppermute | solution.py:235
  53.4 1.5 %collective-permute-start.18 = (bf16[2,144,768]{2,1,0:T(8,128)(2,1)S(1)}, bf16[2,144,768]{2,1,0:T(8,128)(2,1)S(1)}, u32[]{:S(2)}, u32[]{:S(2)}) collective-permute-start(bf16[2,144,768]{2,1,0:T(8,128)(2,1)S(1)} %collective-permute-done.17.refs_1_.refs_6_), channel_id=1, source_target_pairs={{2,0},{4,2},{6,4},{7,6},{5,7},{3,5},{1,3},{0,1},{10,8},{12,10},{14... | collective-permute-start | bytes 1327112 | tf_op jit(solution)/shard_map/ppermute | solution.py:236
  54.9 2.2 %cross.7 = (f32[576,384]{1,0:T(8,128)S(1)}, bf16[576,384]{1,0:T(8,128)(2,1)S(1)}) custom-call(s32[5]{0:T(128)S(1)} %pad_add_fusion.flags, bf16[2,768,768]{2,1,0:T(8,128)(2,1)S(1)} %bitcast.7, bf16[2,144,768]{2,1,0:T(8,128)(2,1)S(1)} %collective-permute-done.15.refs_0_.refs_5_, bf16[2,144,768]{2,1,0:T(8,128)(2,1)S(1)} %collective-permute-done.17.refs_1_.refs_6_, ...), custom_call_target="tpu_custom_call" | custom-call | flops 1358955 | bytes 5899 | tf_op jit(solution)/shard_map/cross/pallas_call | solution.py:59
  59.1 3.3 %collective-permute-done.16.refs_0_ = bf16[2,144,768]{2,1,0:T(8,128)(2,1)S(1)} collective-permute-done((bf16[2,144,768]{2,1,0:T(8,128)(2,1)S(1)}, bf16[2,144,768]{2,1,0:T(8,128)(2,1)S(1)}, u32[]{:S(2)}, u32[]{:S(2)}) %collective-permute-start.16) | collective-permute-done | bytes 442400 | tf_op jit(solution)/shard_map/ppermute | solution.py:235
  62.4 1.6 %collective-permute-start.11 = (bf16[2,144,768]{2,1,0:T(8,128)(2,1)S(1)}, bf16[2,144,768]{2,1,0:T(8,128)(2,1)S(1)}, u32[]{:S(2)}, u32[]{:S(2)}) collective-permute-start(bf16[2,144,768]{2,1,0:T(8,128)(2,1)S(1)} %collective-permute-done.5.refs_2_.refs_7_), channel_id=1, source_target_pairs={{0,2},{2,4},{4,6},{6,7},{7,5},{5,3},{3,1},{1,0},{8,10},{10,12},{12... | collective-permute-start | bytes 1327112 | tf_op jit(solution)/shard_map/ppermute | solution.py:235
  67.6 2.8 %collective-permute-done.14 = bf16[576,384]{1,0:T(8,128)(2,1)S(1)} collective-permute-done((bf16[576,384]{1,0:T(8,128)(2,1)S(1)}, bf16[576,384]{1,0:T(8,128)(2,1)S(1)}, u32[]{:S(2)}, u32[]{:S(2)}) %collective-permute-start.14) | collective-permute-done | bytes 442400 | tf_op jit(solution)/shard_map/ppermute | solution.py:209
  71.1 4.4 %numer.2.refs_0_ = f32[2,768,768]{2,1,0:T(8,128)S(1)} custom-call(s32[5]{0:T(128)S(1)} %pad_add_fusion.flags, bf16[2,768,768]{2,1,0:T(8,128)(2,1)S(1)} %bitcast.9, bf16[768,768]{1,0:T(8,128)(2,1)S(1)} %copy-done.2, bf16[2,144,768]{2,1,0:T(8,128)(2,1)S(1)} %get-tuple-element.52.refs_0_.refs_2_, bf16[2,144,768]{2,1,0:T(8,128)(2,1)S(1)} %get-tuple-element.51.refs_1_.refs_3_, ...), custom_call_target="tpu_custom_call" | custom-call | flops 3170894 | bytes 9733 | tf_op jit(solution)/shard_map/numer/pallas_call | solution.py:121
  81.5 3.1 %collective-permute-done.26 = bf16[288,384]{1,0:T(8,128)(2,1)S(1)} collective-permute-done((bf16[288,384]{1,0:T(8,128)(2,1)S(1)}, bf16[288,384]{1,0:T(8,128)(2,1)S(1)}, u32[]{:S(2)}, u32[]{:S(2)}) %collective-permute-start.26) | collective-permute-done | bytes 221216 | tf_op jit(solution)/shard_map/ppermute | solution.py:209
  84.8 4.1 %numer.3.acc_ref = f32[2,768,768]{2,1,0:T(8,128)S(1)} custom-call(s32[5]{0:T(128)S(1)} %pad_add_fusion.flags, f32[2,768,768]{2,1,0:T(8,128)S(1)} %numer.2.refs_0_, bf16[2,144,768]{2,1,0:T(8,128)(2,1)S(1)} %collective-permute-done.8.refs_0_.refs_1_, bf16[2,144,768]{2,1,0:T(8,128)(2,1)S(1)} %collective-permute-done.9.refs_1_.refs_2_, ...), custom_call_target="tpu_custom_call", output_to_operand_aliasing={{}: (1, {})} | custom-call | flops 2717909 | bytes 12387 | tf_op jit(solution)/shard_map/numer/pallas_call | solution.py:121
  90.7 3.9 %final.1 = bf16[2,1,768,768]{3,2,1,0:T(8,128)(2,1)} custom-call(s32[5]{0:T(128)S(1)} %pad_add_fusion.flags, f32[8]{0:T(128)S(1)} %copy-done.3, f32[2,768,768]{2,1,0:T(8,128)S(1)} %numer.3.acc_ref, bf16[2,768,768]{2,1,0:T(8,128)(2,1)S(1)} %bitcast.11, f32[1,768]{1,0:T(1,128)S(1)} %broadcast_in_dim.6.eps_row, f32[768,1]{1,0:T(8,128)S(1)} %broadcast_in_dim.8.eps_col, ...), custom_call_target="tpu_custom_call" | custom-call | flops 1358955 | bytes 9438 | tf_op jit(solution)/shard_map/final/pallas_call | solution.py:171
  (68 shorter events, 19.3 us)
Async XLA Ops:
  1.2 14.0 %collective-permute-start = (bf16[2,144,768]{2,1,0:T(8,128)(2,1)S(1)}, bf16[2,144,768]{2,1,0:T(8,128)(2,1)S(1)}, u32[]{:S(2)}, u32[]{:S(2)}) collective-permute-start(bf16[2,144,768]{2,1,0:T(8,128)(2,1)S(1)} %get-tuple-element.52.refs_0_.refs_2_), channel_id=1, source_target_pairs={{0,2},{2,4},{4,6},{6,7},{7,5},{5,3},{3,1},{1,0},{8,10},{10,12},{12... | collective-permute-start | bytes 1327112 | tf_op jit(solution)/shard_map/ppermute | solution.py:235
  4.3 13.1 %collective-permute-start.2 = (bf16[2,144,768]{2,1,0:T(8,128)(2,1)S(1)}, bf16[2,144,768]{2,1,0:T(8,128)(2,1)S(1)}, u32[]{:S(2)}, u32[]{:S(2)}) collective-permute-start(bf16[2,144,768]{2,1,0:T(8,128)(2,1)S(1)} %get-tuple-element.51.refs_1_.refs_3_), channel_id=1, source_target_pairs={{2,0},{4,2},{6,4},{7,6},{5,7},{3,5},{1,3},{0,1},{10,8},{12,10},{14... | collective-permute-start | bytes 1327112 | tf_op jit(solution)/shard_map/ppermute | solution.py:236
  4.3 19.6 %collective-permute-start.8 = (bf16[2,144,768]{2,1,0:T(8,128)(2,1)S(1)}, bf16[2,144,768]{2,1,0:T(8,128)(2,1)S(1)}, u32[]{:S(2)}, u32[]{:S(2)}) collective-permute-start(bf16[2,144,768]{2,1,0:T(8,128)(2,1)S(1)} %get-tuple-element.51.refs_1_.refs_3_), channel_id=1, source_target_pairs={{0,2},{2,4},{4,6},{6,7},{7,5},{5,3},{3,1},{1,0},{8,10},{10,12},{12... | collective-permute-start | bytes 1327112 | tf_op jit(solution)/shard_map/ppermute | solution.py:235
  6.3 19.4 %collective-permute-start.9 = (bf16[2,144,768]{2,1,0:T(8,128)(2,1)S(1)}, bf16[2,144,768]{2,1,0:T(8,128)(2,1)S(1)}, u32[]{:S(2)}, u32[]{:S(2)}) collective-permute-start(bf16[2,144,768]{2,1,0:T(8,128)(2,1)S(1)} %get-tuple-element.52.refs_0_.refs_2_), channel_id=1, source_target_pairs={{2,0},{4,2},{6,4},{7,6},{5,7},{3,5},{1,3},{0,1},{10,8},{12,10},{14... | collective-permute-start | bytes 1327112 | tf_op jit(solution)/shard_map/ppermute | solution.py:236
  21.4 13.0 %collective-permute-start.1 = (bf16[2,144,768]{2,1,0:T(8,128)(2,1)S(1)}, bf16[2,144,768]{2,1,0:T(8,128)(2,1)S(1)}, u32[]{:S(2)}, u32[]{:S(2)}) collective-permute-start(bf16[2,144,768]{2,1,0:T(8,128)(2,1)S(1)} %collective-permute-done.refs_2_.refs_4_), channel_id=1, source_target_pairs={{0,2},{2,4},{4,6},{6,7},{7,5},{5,3},{3,1},{1,0},{8,10},{10,12},{12... | collective-permute-start | bytes 1327112 | tf_op jit(solution)/shard_map/ppermute | solution.py:235
  23.0 13.0 %collective-permute-start.3 = (bf16[2,144,768]{2,1,0:T(8,128)(2,1)S(1)}, bf16[2,144,768]{2,1,0:T(8,128)(2,1)S(1)}, u32[]{:S(2)}, u32[]{:S(2)}) collective-permute-start(bf16[2,144,768]{2,1,0:T(8,128)(2,1)S(1)} %collective-permute-done.2.refs_3_.refs_5_), channel_id=1, source_target_pairs={{2,0},{4,2},{6,4},{7,6},{5,7},{3,5},{1,3},{0,1},{10,8},{12,10},{14... | collective-permute-start | bytes 1327112 | tf_op jit(solution)/shard_map/ppermute | solution.py:236
  23.9 20.0 %collective-permute-start.15 = (bf16[2,144,768]{2,1,0:T(8,128)(2,1)S(1)}, bf16[2,144,768]{2,1,0:T(8,128)(2,1)S(1)}, u32[]{:S(2)}, u32[]{:S(2)}) collective-permute-start(bf16[2,144,768]{2,1,0:T(8,128)(2,1)S(1)} %collective-permute-done.8.refs_0_.refs_1_), channel_id=1, source_target_pairs={{0,2},{2,4},{4,6},{6,7},{7,5},{5,3},{3,1},{1,0},{8,10},{10,12},{12... | collective-permute-start | bytes 1327112 | tf_op jit(solution)/shard_map/ppermute | solution.py:235
  25.7 19.8 %collective-permute-start.17 = (bf16[2,144,768]{2,1,0:T(8,128)(2,1)S(1)}, bf16[2,144,768]{2,1,0:T(8,128)(2,1)S(1)}, u32[]{:S(2)}, u32[]{:S(2)}) collective-permute-start(bf16[2,144,768]{2,1,0:T(8,128)(2,1)S(1)} %collective-permute-done.9.refs_1_.refs_2_), channel_id=1, source_target_pairs={{2,0},{4,2},{6,4},{7,6},{5,7},{3,5},{1,3},{0,1},{10,8},{12,10},{14... | collective-permute-start | bytes 1327112 | tf_op jit(solution)/shard_map/ppermute | solution.py:236
  36.0 17.3 %collective-permute-start.5 = (bf16[2,144,768]{2,1,0:T(8,128)(2,1)S(1)}, bf16[2,144,768]{2,1,0:T(8,128)(2,1)S(1)}, u32[]{:S(2)}, u32[]{:S(2)}) collective-permute-start(bf16[2,144,768]{2,1,0:T(8,128)(2,1)S(1)} %collective-permute-done.1.refs_2_.refs_3_), channel_id=1, source_target_pairs={{0,2},{2,4},{4,6},{6,7},{7,5},{5,3},{3,1},{1,0},{8,10},{10,12},{12... | collective-permute-start | bytes 1327112 | tf_op jit(solution)/shard_map/ppermute | solution.py:235
  37.6 17.3 %collective-permute-start.6 = (bf16[2,144,768]{2,1,0:T(8,128)(2,1)S(1)}, bf16[2,144,768]{2,1,0:T(8,128)(2,1)S(1)}, u32[]{:S(2)}, u32[]{:S(2)}) collective-permute-start(bf16[2,144,768]{2,1,0:T(8,128)(2,1)S(1)} %collective-permute-done.3.refs_3_.refs_4_), channel_id=1, source_target_pairs={{2,0},{4,2},{6,4},{7,6},{5,7},{3,5},{1,3},{0,1},{10,8},{12,10},{14... | collective-permute-start | bytes 1327112 | tf_op jit(solution)/shard_map/ppermute | solution.py:236
  40.3 16.9 %collective-permute-start.10 = (bf16[576,384]{1,0:T(8,128)(2,1)S(1)}, bf16[576,384]{1,0:T(8,128)(2,1)S(1)}, u32[]{:S(2)}, u32[]{:S(2)}) collective-permute-start(bf16[576,384]{1,0:T(8,128)(2,1)S(1)} %get-tuple-element.33), channel_id=1, source_target_pairs={{0,8},{8,0},{16,24},{24,16},{1,9},{9,1},{17,25},{25,17},{2,10},{10... | collective-permute-start | bytes 1327112 | tf_op jit(solution)/shard_map/ppermute | solution.py:209
  43.9 14.8 %collective-permute-start.7 = (bf16[576,384]{1,0:T(8,128)(2,1)S(1)}, bf16[576,384]{1,0:T(8,128)(2,1)S(1)}, u32[]{:S(2)}, u32[]{:S(2)}) collective-permute-start(bf16[576,384]{1,0:T(8,128)(2,1)S(1)} %fusion), channel_id=1, source_target_pairs={{0,16},{8,24},{16,0},{24,8},{1,17},{9,25},{17,1},{25,9},{2,18},{10... | collective-permute-start | bytes 1327112 | tf_op jit(solution)/shard_map/ppermute | solution.py:209
  45.5 16.9 %collective-permute-start.16 = (bf16[2,144,768]{2,1,0:T(8,128)(2,1)S(1)}, bf16[2,144,768]{2,1,0:T(8,128)(2,1)S(1)}, u32[]{:S(2)}, u32[]{:S(2)}) collective-permute-start(bf16[2,144,768]{2,1,0:T(8,128)(2,1)S(1)} %collective-permute-done.15.refs_0_.refs_5_), channel_id=1, source_target_pairs={{0,2},{2,4},{4,6},{6,7},{7,5},{5,3},{3,1},{1,0},{8,10},{10,12},{12... | collective-permute-start | bytes 1327112 | tf_op jit(solution)/shard_map/ppermute | solution.py:235
  53.4 11.3 %collective-permute-start.18 = (bf16[2,144,768]{2,1,0:T(8,128)(2,1)S(1)}, bf16[2,144,768]{2,1,0:T(8,128)(2,1)S(1)}, u32[]{:S(2)}, u32[]{:S(2)}) collective-permute-start(bf16[2,144,768]{2,1,0:T(8,128)(2,1)S(1)} %collective-permute-done.17.refs_1_.refs_6_), channel_id=1, source_target_pairs={{2,0},{4,2},{6,4},{7,6},{5,7},{3,5},{1,3},{0,1},{10,8},{12,10},{14... | collective-permute-start | bytes 1327112 | tf_op jit(solution)/shard_map/ppermute | solution.py:236
  57.1 6.8 %collective-permute-start.19 = (bf16[576,384]{1,0:T(8,128)(2,1)S(1)}, bf16[576,384]{1,0:T(8,128)(2,1)S(1)}, u32[]{:S(2)}, u32[]{:S(2)}) collective-permute-start(bf16[576,384]{1,0:T(8,128)(2,1)S(1)} %get-tuple-element.39), channel_id=1, source_target_pairs={{0,8},{8,0},{16,24},{24,16},{1,9},{9,1},{17,25},{25,17},{2,10},{10... | collective-permute-start | bytes 1327112 | tf_op jit(solution)/shard_map/ppermute | solution.py:209
  57.3 13.0 %collective-permute-start.14 = (bf16[576,384]{1,0:T(8,128)(2,1)S(1)}, bf16[576,384]{1,0:T(8,128)(2,1)S(1)}, u32[]{:S(2)}, u32[]{:S(2)}) collective-permute-start(bf16[576,384]{1,0:T(8,128)(2,1)S(1)} %fusion.1), channel_id=1, source_target_pairs={{0,16},{8,24},{16,0},{24,8},{1,17},{9,25},{17,1},{25,9},{2,18},{10... | collective-permute-start | bytes 1327112 | tf_op jit(solution)/shard_map/ppermute | solution.py:209
  58.8 11.7 %collective-permute-start.13 = (bf16[576,384]{1,0:T(8,128)(2,1)S(1)}, bf16[576,384]{1,0:T(8,128)(2,1)S(1)}, u32[]{:S(2)}, u32[]{:S(2)}) collective-permute-start(bf16[576,384]{1,0:T(8,128)(2,1)S(1)} %add_convert_fusion.2.refs_6_), channel_id=1, source_target_pairs={{0,8},{8,0},{16,24},{24,16},{1,9},{9,1},{17,25},{25,17},{2,10},{10... | collective-permute-start | bytes 1327112 | tf_op jit(solution)/shard_map/ppermute | solution.py:209
  62.4 13.2 %collective-permute-start.11 = (bf16[2,144,768]{2,1,0:T(8,128)(2,1)S(1)}, bf16[2,144,768]{2,1,0:T(8,128)(2,1)S(1)}, u32[]{:S(2)}, u32[]{:S(2)}) collective-permute-start(bf16[2,144,768]{2,1,0:T(8,128)(2,1)S(1)} %collective-permute-done.5.refs_2_.refs_7_), channel_id=1, source_target_pairs={{0,2},{2,4},{4,6},{6,7},{7,5},{5,3},{3,1},{1,0},{8,10},{10,12},{12... | collective-permute-start | bytes 1327112 | tf_op jit(solution)/shard_map/ppermute | solution.py:235
  64.0 11.6 %collective-permute-start.12 = (bf16[2,144,768]{2,1,0:T(8,128)(2,1)S(1)}, bf16[2,144,768]{2,1,0:T(8,128)(2,1)S(1)}, u32[]{:S(2)}, u32[]{:S(2)}) collective-permute-start(bf16[2,144,768]{2,1,0:T(8,128)(2,1)S(1)} %collective-permute-done.6.refs_3_.refs_8_), channel_id=1, source_target_pairs={{2,0},{4,2},{6,4},{7,6},{5,7},{3,5},{1,3},{0,1},{10,8},{12,10},{14... | collective-permute-start | bytes 1327112 | tf_op jit(solution)/shard_map/ppermute | solution.py:236
  64.6 15.2 %collective-permute-start.23 = (bf16[576,384]{1,0:T(8,128)(2,1)S(1)}, bf16[576,384]{1,0:T(8,128)(2,1)S(1)}, u32[]{:S(2)}, u32[]{:S(2)}) collective-permute-start(bf16[576,384]{1,0:T(8,128)(2,1)S(1)} %fusion.2), channel_id=1, source_target_pairs={{0,16},{8,24},{16,0},{24,8},{1,17},{9,25},{17,1},{25,9},{2,18},{10... | collective-permute-start | bytes 1327112 | tf_op jit(solution)/shard_map/ppermute | solution.py:209
  70.4 5.2 %collective-permute-start.20 = (bf16[288,384]{1,0:T(8,128)(2,1)S(1)}, bf16[288,384]{1,0:T(8,128)(2,1)S(1)}, u32[]{:S(2)}, u32[]{:S(2)}) collective-permute-start(bf16[288,384]{1,0:T(8,128)(2,1)S(1)} %get-tuple-element.43), channel_id=1, source_target_pairs={{0,8},{8,0},{16,24},{24,16},{1,9},{9,1},{17,25},{25,17},{2,10},{10... | collective-permute-start | bytes 663560 | tf_op jit(solution)/shard_map/ppermute | solution.py:209
  70.5 14.2 %collective-permute-start.24 = (bf16[576,384]{1,0:T(8,128)(2,1)S(1)}, bf16[576,384]{1,0:T(8,128)(2,1)S(1)}, u32[]{:S(2)}, u32[]{:S(2)}) collective-permute-start(bf16[576,384]{1,0:T(8,128)(2,1)S(1)} %add_convert_fusion.1.refs_9_), channel_id=1, source_target_pairs={{0,8},{8,0},{16,24},{24,16},{1,9},{9,1},{17,25},{25,17},{2,10},{10... | collective-permute-start | bytes 1327112 | tf_op jit(solution)/shard_map/ppermute | solution.py:209
  75.7 8.9 %collective-permute-start.26 = (bf16[288,384]{1,0:T(8,128)(2,1)S(1)}, bf16[288,384]{1,0:T(8,128)(2,1)S(1)}, u32[]{:S(2)}, u32[]{:S(2)}) collective-permute-start(bf16[288,384]{1,0:T(8,128)(2,1)S(1)} %fusion.3), channel_id=1, source_target_pairs={{0,16},{8,24},{16,0},{24,8},{1,17},{9,25},{17,1},{25,9},{2,18},{10... | collective-permute-start | bytes 663560 | tf_op jit(solution)/shard_map/ppermute | solution.py:209
  80.2 8.8 %collective-permute-start.22 = (bf16[288,384]{1,0:T(8,128)(2,1)S(1)}, bf16[288,384]{1,0:T(8,128)(2,1)S(1)}, u32[]{:S(2)}, u32[]{:S(2)}) collective-permute-start(bf16[288,384]{1,0:T(8,128)(2,1)S(1)} %fusion.4), channel_id=1, source_target_pairs={{0,16},{8,24},{16,0},{24,8},{1,17},{9,25},{17,1},{25,9},{2,18},{10... | collective-permute-start | bytes 663560 | tf_op jit(solution)/shard_map/ppermute | solution.py:209
  (10 other events, 43.9 us)

commit v3 on v2

--- a/solution.py
+++ b/solution.py
@@ -152,7 +152,9 @@
         for n, cols in enumerate(tiles(vir)):
             total = acc_ref[k, cols, :] + pair_product(chunks, dressed[...], k, cols)
             denom = (eps_col[cols, :] - first) + (eps_row[...] - second)
-            new = t_ref[k, cols, :].astype(jnp.float32) - total / denom
+            inverse = pl.reciprocal(denom, approx=True)
+            inverse = inverse * (2.0 - denom * inverse)
+            new = t_ref[k, cols, :].astype(jnp.float32) - total * inverse
             tile[k, cols, :] = new.astype(tile.dtype)
             copy = pltpu.make_async_copy(
                 tile.at[k, cols, :], out_ref.at[k, 0, cols, :], sems.at[k, n]
@@ -218,8 +220,9 @@
     ends = [sum(sizes[:n + 1]) for n in range(ng)]
     ties = {}
     for n, end in enumerate(ends[:-1]):
-        z_at = "R%d" % (end + 4) if end + 4 <= last else "C%d" % (n + 1)
-        ties.setdefault(z_at, []).append("Z%d" % n)
+        if n != ng - 3:
+            z_at = "R%d" % (end + 4) if end + 4 <= last else "C%d" % (n + 1)
+            ties.setdefault(z_at, []).append("Z%d" % n)
         if n < ng - 3:
             w_at = "R%d" % (end + 6) if end + 6 <= last else "C%d" % (ng - 1)
             ties.setdefault(w_at, []).append("W%d" % n)
@@ -237,7 +240,7 @@
         return [ups[up_h], downs[down_h]]
 
     groups, mine, other = [], [], []
-    n0, n1 = max(ng - 4, 1), ng - 2
+    n0, n1 = ng - 3, ng - 2
     numer_at = {"C%d" % (ng - 1): "N0", "G%d" % (ng - 1): "N1"}
 
     def through(value, target):

time: 94.8 us -> 94.5 us (level)
    ppermute x7, starting transfers between devices: 3.69 us -> 1.15 us  [ring_step(): downs[down_h] = lax.ppermute(downs[down_h], 'col', down)]
    ppermute x7, waiting for transfers between devices: 4.01 us -> 2.24 us  [ring_step(): downs[down_h] = lax.ppermute(downs[down_h], 'col', down)]
    ppermute x7, waiting for transfers between devices: 30.1 us -> 31.3 us  [ring_step(): ups[up_h] = lax.ppermute(ups[up_h], 'col', up)]
    ppermute x7, starting transfers between devices: 13.2 us -> 14.3 us  [ring_step(): ups[up_h] = lax.ppermute(ups[up_h], 'col', up)]
    ppermute x15, waiting for transfers between devices: 8.03 us -> 9.1 us  [swap(): return lax.ppermute(x, 'row', [(r, r ^ bit) for r in range(n_row)])]
  transfers between devices with their start and end apart: 29 -> 29, of which waited for: 14 -> 12; matrix products, arithmetic and copies ran while one was open for 1% -> 1% of each run, Pallas kernels for 19% -> 19%
where the time goes in v3:
time: 94.5 us; the launch traced here: 94.3 us
  waiting for transfers between devices  42.6 us (45%)
  starting transfers between devices  25 us (26%)
  Pallas kernels  22.1 us (23%)
  local copies, waits for them, and re-layouts  3.06 us (3%)
  other arithmetic  1.14 us (1%)
    ppermute x7, waiting for transfers between devices, ring_step(): ups[up_h] = lax.ppermute(ups[up_h], 'col', up)  31.3 us
    ppermute x7, starting transfers between devices, ring_step(): ups[up_h] = lax.ppermute(ups[up_h], 'col', up)  14.3 us
    pallas_call x5, Pallas kernels, cross(): pl.pallas_call(cross_kernel, out_shape=(jax.ShapeDtypeStruct((rows, vir /...  9.62 us
    ppermute x15, starting transfers between devices, swap(): return lax.ppermute(x, 'row', [(r, r ^ bit) for r in range(n_row)])  9.48 us
    ppermute x15, waiting for transfers between devices, swap(): return lax.ppermute(x, 'row', [(r, r ^ bit) for r in range(n_row)])  9.1 us
    pallas_call x2, Pallas kernels, numer(): pl.pallas_call(functools.partial(numer_kernel, len(chunks), len(mine), fr...  8.48 us
    pallas_call x1, Pallas kernels, final(): pl.pallas_call(functools.partial(final_kernel, len(chunks), len(mine)), o...  3.97 us
    ppermute x7, waiting for transfers between devices, ring_step(): downs[down_h] = lax.ppermute(downs[down_h], 'col', down)  2.24 us
  transfers between devices with their start and end apart: 29, of which 12 were waited for; matrix products, arithmetic and copies ran while one was open for 1% of the time, Pallas kernels for 19%

profile of v3, /device:TPU:0, one launch (start us, length us, event | category | flops | bytes accessed | tf_op | source)
XLA Modules:
  0.0 94.3 jit_solution(11848569916712224510)
XLA Ops:
  1.2 3.1 %collective-permute-start = (bf16[2,144,768]{2,1,0:T(8,128)(2,1)S(1)}, bf16[2,144,768]{2,1,0:T(8,128)(2,1)S(1)}, u32[]{:S(2)}, u32[]{:S(2)}) collective-permute-start(bf16[2,144,768]{2,1,0:T(8,128)(2,1)S(1)} %get-tuple-element.48.refs_0_.refs_2_), channel_id=1, source_target_pairs={{0,2},{2,4},{4,6},{6,7},{7,5},{5,3},{3,1},{1,0},{8,10},{10,12},{12... | collective-permute-start | bytes 1327112 | tf_op jit(solution)/shard_map/ppermute | solution.py:238
  4.3 2.0 %collective-permute-start.8 = (bf16[2,144,768]{2,1,0:T(8,128)(2,1)S(1)}, bf16[2,144,768]{2,1,0:T(8,128)(2,1)S(1)}, u32[]{:S(2)}, u32[]{:S(2)}) collective-permute-start(bf16[2,144,768]{2,1,0:T(8,128)(2,1)S(1)} %get-tuple-element.47.refs_1_.refs_3_), channel_id=1, source_target_pairs={{0,2},{2,4},{4,6},{6,7},{7,5},{5,3},{3,1},{1,0},{8,10},{10,12},{12... | collective-permute-start | bytes 1327112 | tf_op jit(solution)/shard_map/ppermute | solution.py:238
  6.4 8.8 %collective-permute-done.refs_2_.refs_4_ = bf16[2,144,768]{2,1,0:T(8,128)(2,1)S(1)} collective-permute-done((bf16[2,144,768]{2,1,0:T(8,128)(2,1)S(1)}, bf16[2,144,768]{2,1,0:T(8,128)(2,1)S(1)}, u32[]{:S(2)}, u32[]{:S(2)}) %collective-permute-start) | collective-permute-done | bytes 442400 | tf_op jit(solution)/shard_map/ppermute | solution.py:238
  15.2 2.1 %collective-permute-start.1 = (bf16[2,144,768]{2,1,0:T(8,128)(2,1)S(1)}, bf16[2,144,768]{2,1,0:T(8,128)(2,1)S(1)}, u32[]{:S(2)}, u32[]{:S(2)}) collective-permute-start(bf16[2,144,768]{2,1,0:T(8,128)(2,1)S(1)} %collective-permute-done.refs_2_.refs_4_), channel_id=1, source_target_pairs={{0,2},{2,4},{4,6},{6,7},{7,5},{5,3},{3,1},{1,0},{8,10},{10,12},{12... | collective-permute-start | bytes 1327112 | tf_op jit(solution)/shard_map/ppermute | solution.py:238
  19.0 2.3 %cross.5 = (f32[576,384]{1,0:T(8,128)S(1)}, bf16[576,384]{1,0:T(8,128)(2,1)S(1)}) custom-call(s32[5]{0:T(128)S(1)} %pad_add_fusion.flags, bf16[2,768,768]{2,1,0:T(8,128)(2,1)S(1)} %bitcast.5, bf16[2,144,768]{2,1,0:T(8,128)(2,1)S(1)} %get-tuple-element.48.refs_0_.refs_2_, bf16[2,144,768]{2,1,0:T(8,128)(2,1)S(1)} %get-tuple-element.47.refs_1_.refs_3_, ...), custom_call_target="tpu_custom_call" | custom-call | flops 1358955 | bytes 5899 | tf_op jit(solution)/shard_map/cross/pallas_call | solution.py:59
  21.4 3.3 %collective-permute-done.8.refs_0_.refs_6_ = bf16[2,144,768]{2,1,0:T(8,128)(2,1)S(1)} collective-permute-done((bf16[2,144,768]{2,1,0:T(8,128)(2,1)S(1)}, bf16[2,144,768]{2,1,0:T(8,128)(2,1)S(1)}, u32[]{:S(2)}, u32[]{:S(2)}) %collective-permute-start.8) | collective-permute-done | bytes 442400 | tf_op jit(solution)/shard_map/ppermute | solution.py:238
  24.7 2.1 %collective-permute-start.16 = (bf16[2,144,768]{2,1,0:T(8,128)(2,1)S(1)}, bf16[2,144,768]{2,1,0:T(8,128)(2,1)S(1)}, u32[]{:S(2)}, u32[]{:S(2)}) collective-permute-start(bf16[2,144,768]{2,1,0:T(8,128)(2,1)S(1)} %collective-permute-done.8.refs_0_.refs_6_), channel_id=1, source_target_pairs={{0,2},{2,4},{4,6},{6,7},{7,5},{5,3},{3,1},{1,0},{8,10},{10,12},{12... | collective-permute-start | bytes 1327112 | tf_op jit(solution)/shard_map/ppermute | solution.py:238
  26.9 7.3 %collective-permute-done.1.refs_2_.refs_8_ = bf16[2,144,768]{2,1,0:T(8,128)(2,1)S(1)} collective-permute-done((bf16[2,144,768]{2,1,0:T(8,128)(2,1)S(1)}, bf16[2,144,768]{2,1,0:T(8,128)(2,1)S(1)}, u32[]{:S(2)}, u32[]{:S(2)}) %collective-permute-start.1) | collective-permute-done | bytes 442400 | tf_op jit(solution)/shard_map/ppermute | solution.py:238
  34.2 2.2 %collective-permute-done.3.refs_3_.refs_9_ = bf16[2,144,768]{2,1,0:T(8,128)(2,1)S(1)} collective-permute-done((bf16[2,144,768]{2,1,0:T(8,128)(2,1)S(1)}, bf16[2,144,768]{2,1,0:T(8,128)(2,1)S(1)}, u32[]{:S(2)}, u32[]{:S(2)}) %collective-permute-start.3) | collective-permute-done | bytes 442400 | tf_op jit(solution)/shard_map/ppermute | solution.py:239
  36.3 2.2 %cross.6 = (f32[576,384]{1,0:T(8,128)S(1)}, bf16[576,384]{1,0:T(8,128)(2,1)S(1)}) custom-call(s32[5]{0:T(128)S(1)} %pad_add_fusion.flags, bf16[2,768,768]{2,1,0:T(8,128)(2,1)S(1)} %bitcast.6, bf16[2,144,768]{2,1,0:T(8,128)(2,1)S(1)} %collective-permute-done.8.refs_0_.refs_6_, bf16[2,144,768]{2,1,0:T(8,128)(2,1)S(1)} %collective-permute-done.9.refs_1_.refs_7_, ...), custom_call_target="tpu_custom_call" | custom-call | flops 1358955 | bytes 5899 | tf_op jit(solution)/shard_map/cross/pallas_call | solution.py:59
  40.8 2.8 %collective-permute-done.16.refs_0_.refs_1_ = bf16[2,144,768]{2,1,0:T(8,128)(2,1)S(1)} collective-permute-done((bf16[2,144,768]{2,1,0:T(8,128)(2,1)S(1)}, bf16[2,144,768]{2,1,0:T(8,128)(2,1)S(1)}, u32[]{:S(2)}, u32[]{:S(2)}) %collective-permute-start.16) | collective-permute-done | bytes 442400 | tf_op jit(solution)/shard_map/ppermute | solution.py:238
  43.7 2.0 %collective-permute-start.7 = (bf16[576,384]{1,0:T(8,128)(2,1)S(1)}, bf16[576,384]{1,0:T(8,128)(2,1)S(1)}, u32[]{:S(2)}, u32[]{:S(2)}) collective-permute-start(bf16[576,384]{1,0:T(8,128)(2,1)S(1)} %fusion), channel_id=1, source_target_pairs={{0,16},{8,24},{16,0},{24,8},{1,17},{9,25},{17,1},{25,9},{2,18},{10... | collective-permute-start | bytes 1327112 | tf_op jit(solution)/shard_map/ppermute | solution.py:211
  47.8 5.4 %collective-permute-done.5.refs_2_.refs_3_ = bf16[2,144,768]{2,1,0:T(8,128)(2,1)S(1)} collective-permute-done((bf16[2,144,768]{2,1,0:T(8,128)(2,1)S(1)}, bf16[2,144,768]{2,1,0:T(8,128)(2,1)S(1)}, u32[]{:S(2)}, u32[]{:S(2)}) %collective-permute-start.5) | collective-permute-done | bytes 442400 | tf_op jit(solution)/shard_map/ppermute | solution.py:238
  53.1 2.0 %collective-permute-start.13 = (bf16[576,384]{1,0:T(8,128)(2,1)S(1)}, bf16[576,384]{1,0:T(8,128)(2,1)S(1)}, u32[]{:S(2)}, u32[]{:S(2)}) collective-permute-start(bf16[576,384]{1,0:T(8,128)(2,1)S(1)} %fusion.1), channel_id=1, source_target_pairs={{0,16},{8,24},{16,0},{24,8},{1,17},{9,25},{17,1},{25,9},{2,18},{10... | collective-permute-start | bytes 1327112 | tf_op jit(solution)/shard_map/ppermute | solution.py:211
  55.1 2.2 %cross.9 = (f32[576,384]{1,0:T(8,128)S(1)}, bf16[576,384]{1,0:T(8,128)(2,1)S(1)}) custom-call(s32[5]{0:T(128)S(1)} %pad_add_fusion.flags, bf16[2,768,768]{2,1,0:T(8,128)(2,1)S(1)} %bitcast.7, bf16[2,144,768]{2,1,0:T(8,128)(2,1)S(1)} %collective-permute-done.16.refs_0_.refs_1_, bf16[2,144,768]{2,1,0:T(8,128)(2,1)S(1)} %collective-permute-done.18.refs_1_.refs_2_, ...), custom_call_target="tpu_custom_call" | custom-call | flops 1358955 | bytes 5899 | tf_op jit(solution)/shard_map/cross/pallas_call | solution.py:59
  58.1 3.6 %collective-permute-done.17.refs_0_ = bf16[2,144,768]{2,1,0:T(8,128)(2,1)S(1)} collective-permute-done((bf16[2,144,768]{2,1,0:T(8,128)(2,1)S(1)}, bf16[2,144,768]{2,1,0:T(8,128)(2,1)S(1)}, u32[]{:S(2)}, u32[]{:S(2)}) %collective-permute-start.17) | collective-permute-done | bytes 442400 | tf_op jit(solution)/shard_map/ppermute | solution.py:238
  61.8 1.8 %collective-permute-start.11 = (bf16[2,144,768]{2,1,0:T(8,128)(2,1)S(1)}, bf16[2,144,768]{2,1,0:T(8,128)(2,1)S(1)}, u32[]{:S(2)}, u32[]{:S(2)}) collective-permute-start(bf16[2,144,768]{2,1,0:T(8,128)(2,1)S(1)} %collective-permute-done.5.refs_2_.refs_3_), channel_id=1, source_target_pairs={{0,2},{2,4},{4,6},{6,7},{7,5},{5,3},{3,1},{1,0},{8,10},{10,12},{12... | collective-permute-start | bytes 1327112 | tf_op jit(solution)/shard_map/ppermute | solution.py:238
  66.9 1.7 %collective-permute-start.24 = (bf16[576,384]{1,0:T(8,128)(2,1)S(1)}, bf16[576,384]{1,0:T(8,128)(2,1)S(1)}, u32[]{:S(2)}, u32[]{:S(2)}) collective-permute-start(bf16[576,384]{1,0:T(8,128)(2,1)S(1)} %fusion.2), channel_id=1, source_target_pairs={{0,16},{8,24},{16,0},{24,8},{1,17},{9,25},{17,1},{25,9},{2,18},{10... | collective-permute-start | bytes 1327112 | tf_op jit(solution)/shard_map/ppermute | solution.py:211
  69.0 5.8 %numer.2.refs_0_ = f32[2,768,768]{2,1,0:T(8,128)S(1)} custom-call(s32[5]{0:T(128)S(1)} %pad_add_fusion.flags, bf16[2,768,768]{2,1,0:T(8,128)(2,1)S(1)} %bitcast.9, bf16[768,768]{1,0:T(8,128)(2,1)S(1)} %copy-done.2, bf16[2,144,768]{2,1,0:T(8,128)(2,1)S(1)} %get-tuple-element.48.refs_0_.refs_2_, bf16[2,144,768]{2,1,0:T(8,128)(2,1)S(1)} %get-tuple-element.47.refs_1_.refs_3_, ...), custom_call_target="tpu_custom_call" | custom-call | flops 4529849 | bytes 12387 | tf_op jit(solution)/shard_map/numer/pallas_call | solution.py:121
  76.4 3.5 %collective-permute-done.24 = bf16[576,384]{1,0:T(8,128)(2,1)S(1)} collective-permute-done((bf16[576,384]{1,0:T(8,128)(2,1)S(1)}, bf16[576,384]{1,0:T(8,128)(2,1)S(1)}, u32[]{:S(2)}, u32[]{:S(2)}) %collective-permute-start.24) | collective-permute-done | bytes 442400 | tf_op jit(solution)/shard_map/ppermute | solution.py:211
  80.2 1.8 %collective-permute-start.22 = (bf16[288,384]{1,0:T(8,128)(2,1)S(1)}, bf16[288,384]{1,0:T(8,128)(2,1)S(1)}, u32[]{:S(2)}, u32[]{:S(2)}) collective-permute-start(bf16[288,384]{1,0:T(8,128)(2,1)S(1)} %fusion.4), channel_id=1, source_target_pairs={{0,16},{8,24},{16,0},{24,8},{1,17},{9,25},{17,1},{25,9},{2,18},{10... | collective-permute-start | bytes 663560 | tf_op jit(solution)/shard_map/ppermute | solution.py:211
  82.0 2.2 %collective-permute-done.26 = bf16[288,384]{1,0:T(8,128)(2,1)S(1)} collective-permute-done((bf16[288,384]{1,0:T(8,128)(2,1)S(1)}, bf16[288,384]{1,0:T(8,128)(2,1)S(1)}, u32[]{:S(2)}, u32[]{:S(2)}) %collective-permute-start.26) | collective-permute-done | bytes 221216 | tf_op jit(solution)/shard_map/ppermute | solution.py:211
  84.4 2.7 %numer.3.acc_ref = f32[2,768,768]{2,1,0:T(8,128)S(1)} custom-call(s32[5]{0:T(128)S(1)} %pad_add_fusion.flags, f32[2,768,768]{2,1,0:T(8,128)S(1)} %numer.2.refs_0_, bf16[2,144,768]{2,1,0:T(8,128)(2,1)S(1)} %collective-permute-done.16.refs_0_.refs_1_, bf16[2,144,768]{2,1,0:T(8,128)(2,1)S(1)} %collective-permute-done.18.refs_1_.refs_2_, ...), custom_call_target="tpu_custom_call", output_to_operand_aliasing={{}: (1, {})} | custom-call | flops 1358955 | bytes 9733 | tf_op jit(solution)/shard_map/numer/pallas_call | solution.py:121
  90.2 4.0 %final.1 = bf16[2,1,768,768]{3,2,1,0:T(8,128)(2,1)} custom-call(s32[5]{0:T(128)S(1)} %pad_add_fusion.flags, f32[8]{0:T(128)S(1)} %copy-done.3, f32[2,768,768]{2,1,0:T(8,128)S(1)} %numer.3.acc_ref, bf16[2,768,768]{2,1,0:T(8,128)(2,1)S(1)} %bitcast.11, f32[1,768]{1,0:T(1,128)S(1)} %broadcast_in_dim.6.eps_row, f32[768,1]{1,0:T(8,128)S(1)} %broadcast_in_dim.8.eps_col, ...), custom_call_target="tpu_custom_call" | custom-call | flops 1358955 | bytes 9438 | tf_op jit(solution)/shard_map/final/pallas_call | solution.py:173
  (68 shorter events, 16.9 us)
Async XLA Ops:
  1.2 14.0 %collective-permute-start = (bf16[2,144,768]{2,1,0:T(8,128)(2,1)S(1)}, bf16[2,144,768]{2,1,0:T(8,128)(2,1)S(1)}, u32[]{:S(2)}, u32[]{:S(2)}) collective-permute-start(bf16[2,144,768]{2,1,0:T(8,128)(2,1)S(1)} %get-tuple-element.48.refs_0_.refs_2_), channel_id=1, source_target_pairs={{0,2},{2,4},{4,6},{6,7},{7,5},{5,3},{3,1},{1,0},{8,10},{10,12},{12... | collective-permute-start | bytes 1327112 | tf_op jit(solution)/shard_map/ppermute | solution.py:238
  4.3 13.1 %collective-permute-start.2 = (bf16[2,144,768]{2,1,0:T(8,128)(2,1)S(1)}, bf16[2,144,768]{2,1,0:T(8,128)(2,1)S(1)}, u32[]{:S(2)}, u32[]{:S(2)}) collective-permute-start(bf16[2,144,768]{2,1,0:T(8,128)(2,1)S(1)} %get-tuple-element.47.refs_1_.refs_3_), channel_id=1, source_target_pairs={{2,0},{4,2},{6,4},{7,6},{5,7},{3,5},{1,3},{0,1},{10,8},{12,10},{14... | collective-permute-start | bytes 1327112 | tf_op jit(solution)/shard_map/ppermute | solution.py:239
  4.3 20.4 %collective-permute-start.8 = (bf16[2,144,768]{2,1,0:T(8,128)(2,1)S(1)}, bf16[2,144,768]{2,1,0:T(8,128)(2,1)S(1)}, u32[]{:S(2)}, u32[]{:S(2)}) collective-permute-start(bf16[2,144,768]{2,1,0:T(8,128)(2,1)S(1)} %get-tuple-element.47.refs_1_.refs_3_), channel_id=1, source_target_pairs={{0,2},{2,4},{4,6},{6,7},{7,5},{5,3},{3,1},{1,0},{8,10},{10,12},{12... | collective-permute-start | bytes 1327112 | tf_op jit(solution)/shard_map/ppermute | solution.py:238
  6.3 20.5 %collective-permute-start.9 = (bf16[2,144,768]{2,1,0:T(8,128)(2,1)S(1)}, bf16[2,144,768]{2,1,0:T(8,128)(2,1)S(1)}, u32[]{:S(2)}, u32[]{:S(2)}) collective-permute-start(bf16[2,144,768]{2,1,0:T(8,128)(2,1)S(1)} %get-tuple-element.48.refs_0_.refs_2_), channel_id=1, source_target_pairs={{2,0},{4,2},{6,4},{7,6},{5,7},{3,5},{1,3},{0,1},{10,8},{12,10},{14... | collective-permute-start | bytes 1327112 | tf_op jit(solution)/shard_map/ppermute | solution.py:239
  15.2 19.0 %collective-permute-start.1 = (bf16[2,144,768]{2,1,0:T(8,128)(2,1)S(1)}, bf16[2,144,768]{2,1,0:T(8,128)(2,1)S(1)}, u32[]{:S(2)}, u32[]{:S(2)}) collective-permute-start(bf16[2,144,768]{2,1,0:T(8,128)(2,1)S(1)} %collective-permute-done.refs_2_.refs_4_), channel_id=1, source_target_pairs={{0,2},{2,4},{4,6},{6,7},{7,5},{5,3},{3,1},{1,0},{8,10},{10,12},{12... | collective-permute-start | bytes 1327112 | tf_op jit(solution)/shard_map/ppermute | solution.py:238
  17.4 19.0 %collective-permute-start.3 = (bf16[2,144,768]{2,1,0:T(8,128)(2,1)S(1)}, bf16[2,144,768]{2,1,0:T(8,128)(2,1)S(1)}, u32[]{:S(2)}, u32[]{:S(2)}) collective-permute-start(bf16[2,144,768]{2,1,0:T(8,128)(2,1)S(1)} %collective-permute-done.2.refs_3_.refs_5_), channel_id=1, source_target_pairs={{2,0},{4,2},{6,4},{7,6},{5,7},{3,5},{1,3},{0,1},{10,8},{12,10},{14... | collective-permute-start | bytes 1327112 | tf_op jit(solution)/shard_map/ppermute | solution.py:239
  21.3 17.4 %collective-permute-start.4 = (bf16[576,384]{1,0:T(8,128)(2,1)S(1)}, bf16[576,384]{1,0:T(8,128)(2,1)S(1)}, u32[]{:S(2)}, u32[]{:S(2)}) collective-permute-start(bf16[576,384]{1,0:T(8,128)(2,1)S(1)} %get-tuple-element.27), channel_id=1, source_target_pairs={{0,8},{8,0},{16,24},{24,16},{1,9},{9,1},{17,25},{25,17},{2,10},{10... | collective-permute-start | bytes 1327112 | tf_op jit(solution)/shard_map/ppermute | solution.py:211
  24.7 19.0 %collective-permute-start.16 = (bf16[2,144,768]{2,1,0:T(8,128)(2,1)S(1)}, bf16[2,144,768]{2,1,0:T(8,128)(2,1)S(1)}, u32[]{:S(2)}, u32[]{:S(2)}) collective-permute-start(bf16[2,144,768]{2,1,0:T(8,128)(2,1)S(1)} %collective-permute-done.8.refs_0_.refs_6_), channel_id=1, source_target_pairs={{0,2},{2,4},{4,6},{6,7},{7,5},{5,3},{3,1},{1,0},{8,10},{10,12},{12... | collective-permute-start | bytes 1327112 | tf_op jit(solution)/shard_map/ppermute | solution.py:238
  26.9 18.8 %collective-permute-start.18 = (bf16[2,144,768]{2,1,0:T(8,128)(2,1)S(1)}, bf16[2,144,768]{2,1,0:T(8,128)(2,1)S(1)}, u32[]{:S(2)}, u32[]{:S(2)}) collective-permute-start(bf16[2,144,768]{2,1,0:T(8,128)(2,1)S(1)} %collective-permute-done.9.refs_1_.refs_7_), channel_id=1, source_target_pairs={{2,0},{4,2},{6,4},{7,6},{5,7},{3,5},{1,3},{0,1},{10,8},{12,10},{14... | collective-permute-start | bytes 1327112 | tf_op jit(solution)/shard_map/ppermute | solution.py:239
  38.6 8.6 %collective-permute-start.10 = (bf16[576,384]{1,0:T(8,128)(2,1)S(1)}, bf16[576,384]{1,0:T(8,128)(2,1)S(1)}, u32[]{:S(2)}, u32[]{:S(2)}) collective-permute-start(bf16[576,384]{1,0:T(8,128)(2,1)S(1)} %get-tuple-element.31), channel_id=1, source_target_pairs={{0,8},{8,0},{16,24},{24,16},{1,9},{9,1},{17,25},{25,17},{2,10},{10... | collective-permute-start | bytes 1327112 | tf_op jit(solution)/shard_map/ppermute | solution.py:211
  38.8 14.4 %collective-permute-start.5 = (bf16[2,144,768]{2,1,0:T(8,128)(2,1)S(1)}, bf16[2,144,768]{2,1,0:T(8,128)(2,1)S(1)}, u32[]{:S(2)}, u32[]{:S(2)}) collective-permute-start(bf16[2,144,768]{2,1,0:T(8,128)(2,1)S(1)} %collective-permute-done.1.refs_2_.refs_8_), channel_id=1, source_target_pairs={{0,2},{2,4},{4,6},{6,7},{7,5},{5,3},{3,1},{1,0},{8,10},{10,12},{12... | collective-permute-start | bytes 1327112 | tf_op jit(solution)/shard_map/ppermute | solution.py:238
  40.4 14.7 %collective-permute-start.6 = (bf16[2,144,768]{2,1,0:T(8,128)(2,1)S(1)}, bf16[2,144,768]{2,1,0:T(8,128)(2,1)S(1)}, u32[]{:S(2)}, u32[]{:S(2)}) collective-permute-start(bf16[2,144,768]{2,1,0:T(8,128)(2,1)S(1)} %collective-permute-done.3.refs_3_.refs_9_), channel_id=1, source_target_pairs={{2,0},{4,2},{6,4},{7,6},{5,7},{3,5},{1,3},{0,1},{10,8},{12,10},{14... | collective-permute-start | bytes 1327112 | tf_op jit(solution)/shard_map/ppermute | solution.py:239
  43.7 13.8 %collective-permute-start.7 = (bf16[576,384]{1,0:T(8,128)(2,1)S(1)}, bf16[576,384]{1,0:T(8,128)(2,1)S(1)}, u32[]{:S(2)}, u32[]{:S(2)}) collective-permute-start(bf16[576,384]{1,0:T(8,128)(2,1)S(1)} %fusion), channel_id=1, source_target_pairs={{0,16},{8,24},{16,0},{24,8},{1,17},{9,25},{17,1},{25,9},{2,18},{10... | collective-permute-start | bytes 1327112 | tf_op jit(solution)/shard_map/ppermute | solution.py:211
  45.6 16.2 %collective-permute-start.17 = (bf16[2,144,768]{2,1,0:T(8,128)(2,1)S(1)}, bf16[2,144,768]{2,1,0:T(8,128)(2,1)S(1)}, u32[]{:S(2)}, u32[]{:S(2)}) collective-permute-start(bf16[2,144,768]{2,1,0:T(8,128)(2,1)S(1)} %collective-permute-done.16.refs_0_.refs_1_), channel_id=1, source_target_pairs={{0,2},{2,4},{4,6},{6,7},{7,5},{5,3},{3,1},{1,0},{8,10},{10,12},{12... | collective-permute-start | bytes 1327112 | tf_op jit(solution)/shard_map/ppermute | solution.py:238
  47.2 16.4 %collective-permute-start.19 = (bf16[2,144,768]{2,1,0:T(8,128)(2,1)S(1)}, bf16[2,144,768]{2,1,0:T(8,128)(2,1)S(1)}, u32[]{:S(2)}, u32[]{:S(2)}) collective-permute-start(bf16[2,144,768]{2,1,0:T(8,128)(2,1)S(1)} %collective-permute-done.18.refs_1_.refs_2_), channel_id=1, source_target_pairs={{2,0},{4,2},{6,4},{7,6},{5,7},{3,5},{1,3},{0,1},{10,8},{12,10},{14... | collective-permute-start | bytes 1327112 | tf_op jit(solution)/shard_map/ppermute | solution.py:239
  53.1 12.1 %collective-permute-start.13 = (bf16[576,384]{1,0:T(8,128)(2,1)S(1)}, bf16[576,384]{1,0:T(8,128)(2,1)S(1)}, u32[]{:S(2)}, u32[]{:S(2)}) collective-permute-start(bf16[576,384]{1,0:T(8,128)(2,1)S(1)} %fusion.1), channel_id=1, source_target_pairs={{0,16},{8,24},{16,0},{24,8},{1,17},{9,25},{17,1},{25,9},{2,18},{10... | collective-permute-start | bytes 1327112 | tf_op jit(solution)/shard_map/ppermute | solution.py:211
  57.3 8.2 %collective-permute-start.23 = (bf16[576,384]{1,0:T(8,128)(2,1)S(1)}, bf16[576,384]{1,0:T(8,128)(2,1)S(1)}, u32[]{:S(2)}, u32[]{:S(2)}) collective-permute-start(bf16[576,384]{1,0:T(8,128)(2,1)S(1)} %get-tuple-element.44), channel_id=1, source_target_pairs={{0,8},{8,0},{16,24},{24,16},{1,9},{9,1},{17,25},{25,17},{2,10},{10... | collective-permute-start | bytes 1327112 | tf_op jit(solution)/shard_map/ppermute | solution.py:211
  57.6 11.0 %collective-permute-start.14 = (bf16[576,384]{1,0:T(8,128)(2,1)S(1)}, bf16[576,384]{1,0:T(8,128)(2,1)S(1)}, u32[]{:S(2)}, u32[]{:S(2)}) collective-permute-start(bf16[576,384]{1,0:T(8,128)(2,1)S(1)} %add_convert_fusion.2.refs_10_), channel_id=1, source_target_pairs={{0,8},{8,0},{16,24},{24,16},{1,9},{9,1},{17,25},{25,17},{2,10},{10... | collective-permute-start | bytes 1327112 | tf_op jit(solution)/shard_map/ppermute | solution.py:211
  61.8 13.0 %collective-permute-start.11 = (bf16[2,144,768]{2,1,0:T(8,128)(2,1)S(1)}, bf16[2,144,768]{2,1,0:T(8,128)(2,1)S(1)}, u32[]{:S(2)}, u32[]{:S(2)}) collective-permute-start(bf16[2,144,768]{2,1,0:T(8,128)(2,1)S(1)} %collective-permute-done.5.refs_2_.refs_3_), channel_id=1, source_target_pairs={{0,2},{2,4},{4,6},{6,7},{7,5},{5,3},{3,1},{1,0},{8,10},{10,12},{12... | collective-permute-start | bytes 1327112 | tf_op jit(solution)/shard_map/ppermute | solution.py:238
  63.6 11.2 %collective-permute-start.12 = (bf16[2,144,768]{2,1,0:T(8,128)(2,1)S(1)}, bf16[2,144,768]{2,1,0:T(8,128)(2,1)S(1)}, u32[]{:S(2)}, u32[]{:S(2)}) collective-permute-start(bf16[2,144,768]{2,1,0:T(8,128)(2,1)S(1)} %collective-permute-done.6.refs_3_.refs_4_), channel_id=1, source_target_pairs={{2,0},{4,2},{6,4},{7,6},{5,7},{3,5},{1,3},{0,1},{10,8},{12,10},{14... | collective-permute-start | bytes 1327112 | tf_op jit(solution)/shard_map/ppermute | solution.py:239
  66.9 13.0 %collective-permute-start.24 = (bf16[576,384]{1,0:T(8,128)(2,1)S(1)}, bf16[576,384]{1,0:T(8,128)(2,1)S(1)}, u32[]{:S(2)}, u32[]{:S(2)}) collective-permute-start(bf16[576,384]{1,0:T(8,128)(2,1)S(1)} %fusion.2), channel_id=1, source_target_pairs={{0,16},{8,24},{16,0},{24,8},{1,17},{9,25},{17,1},{25,9},{2,18},{10... | collective-permute-start | bytes 1327112 | tf_op jit(solution)/shard_map/ppermute | solution.py:211
  68.6 15.6 %collective-permute-start.26 = (bf16[288,384]{1,0:T(8,128)(2,1)S(1)}, bf16[288,384]{1,0:T(8,128)(2,1)S(1)}, u32[]{:S(2)}, u32[]{:S(2)}) collective-permute-start(bf16[288,384]{1,0:T(8,128)(2,1)S(1)} %fusion.3), channel_id=1, source_target_pairs={{0,16},{8,24},{16,0},{24,8},{1,17},{9,25},{17,1},{25,9},{2,18},{10... | collective-permute-start | bytes 663560 | tf_op jit(solution)/shard_map/ppermute | solution.py:211
  80.2 8.4 %collective-permute-start.22 = (bf16[288,384]{1,0:T(8,128)(2,1)S(1)}, bf16[288,384]{1,0:T(8,128)(2,1)S(1)}, u32[]{:S(2)}, u32[]{:S(2)}) collective-permute-start(bf16[288,384]{1,0:T(8,128)(2,1)S(1)} %fusion.4), channel_id=1, source_target_pairs={{0,16},{8,24},{16,0},{24,8},{1,17},{9,25},{17,1},{25,9},{2,18},{10... | collective-permute-start | bytes 663560 | tf_op jit(solution)/shard_map/ppermute | solution.py:211
  84.3 4.6 %collective-permute-start.27 = (bf16[288,384]{1,0:T(8,128)(2,1)S(1)}, bf16[288,384]{1,0:T(8,128)(2,1)S(1)}, u32[]{:S(2)}, u32[]{:S(2)}) collective-permute-start(bf16[288,384]{1,0:T(8,128)(2,1)S(1)} %add_convert_fusion.4.refs_4_), channel_id=1, source_target_pairs={{0,8},{8,0},{16,24},{24,16},{1,9},{9,1},{17,25},{25,17},{2,10},{10... | collective-permute-start | bytes 663560 | tf_op jit(solution)/shard_map/ppermute | solution.py:211
  (10 other events, 34.2 us)

commit v4 on v3

--- a/solution.py
+++ b/solution.py
@@ -152,9 +152,7 @@
         for n, cols in enumerate(tiles(vir)):
             total = acc_ref[k, cols, :] + pair_product(chunks, dressed[...], k, cols)
             denom = (eps_col[cols, :] - first) + (eps_row[...] - second)
-            inverse = pl.reciprocal(denom, approx=True)
-            inverse = inverse * (2.0 - denom * inverse)
-            new = t_ref[k, cols, :].astype(jnp.float32) - total * inverse
+            new = t_ref[k, cols, :].astype(jnp.float32) - total / denom
             tile[k, cols, :] = new.astype(tile.dtype)
             copy = pltpu.make_async_copy(
                 tile.at[k, cols, :], out_ref.at[k, 0, cols, :], sems.at[k, n]

time: 94.5 us -> 94.4 us (level)
  no operation moved by 1% of the time
where the time goes in v4:
time: 94.4 us; the launch traced here: 94.2 us
  waiting for transfers between devices  42.6 us (45%)
  starting transfers between devices  25 us (26%)
  Pallas kernels  22 us (23%)
  local copies, waits for them, and re-layouts  3.06 us (3%)
  other arithmetic  1.14 us (1%)
    ppermute x7, waiting for transfers between devices, ring_step(): ups[up_h] = lax.ppermute(ups[up_h], 'col', up)  31.3 us
    ppermute x7, starting transfers between devices, ring_step(): ups[up_h] = lax.ppermute(ups[up_h], 'col', up)  14.3 us
    pallas_call x5, Pallas kernels, cross(): pl.pallas_call(cross_kernel, out_shape=(jax.ShapeDtypeStruct((rows, vir /...  9.62 us
    ppermute x15, starting transfers between devices, swap(): return lax.ppermute(x, 'row', [(r, r ^ bit) for r in range(n_row)])  9.48 us
    ppermute x15, waiting for transfers between devices, swap(): return lax.ppermute(x, 'row', [(r, r ^ bit) for r in range(n_row)])  9.1 us
    pallas_call x2, Pallas kernels, numer(): pl.pallas_call(functools.partial(numer_kernel, len(chunks), len(mine), fr...  8.48 us
    pallas_call x1, Pallas kernels, final(): pl.pallas_call(functools.partial(final_kernel, len(chunks), len(mine)), o...  3.85 us
    ppermute x7, waiting for transfers between devices, ring_step(): downs[down_h] = lax.ppermute(downs[down_h], 'col', down)  2.24 us
  transfers between devices with their start and end apart: 29, of which 12 were waited for; matrix products, arithmetic and copies ran while one was open for 1% of the time, Pallas kernels for 19%

profile of v4, /device:TPU:0, one launch (start us, length us, event | category | flops | bytes accessed | tf_op | source)
XLA Modules:
  0.0 94.2 jit_solution(15121851716229909586)
XLA Ops:
  1.2 3.1 %collective-permute-start = (bf16[2,144,768]{2,1,0:T(8,128)(2,1)S(1)}, bf16[2,144,768]{2,1,0:T(8,128)(2,1)S(1)}, u32[]{:S(2)}, u32[]{:S(2)}) collective-permute-start(bf16[2,144,768]{2,1,0:T(8,128)(2,1)S(1)} %get-tuple-element.48.refs_0_.refs_2_), channel_id=1, source_target_pairs={{0,2},{2,4},{4,6},{6,7},{7,5},{5,3},{3,1},{1,0},{8,10},{10,12},{12... | collective-permute-start | bytes 1327112 | tf_op jit(solution)/shard_map/ppermute | solution.py:236
  4.3 2.0 %collective-permute-start.8 = (bf16[2,144,768]{2,1,0:T(8,128)(2,1)S(1)}, bf16[2,144,768]{2,1,0:T(8,128)(2,1)S(1)}, u32[]{:S(2)}, u32[]{:S(2)}) collective-permute-start(bf16[2,144,768]{2,1,0:T(8,128)(2,1)S(1)} %get-tuple-element.47.refs_1_.refs_3_), channel_id=1, source_target_pairs={{0,2},{2,4},{4,6},{6,7},{7,5},{5,3},{3,1},{1,0},{8,10},{10,12},{12... | collective-permute-start | bytes 1327112 | tf_op jit(solution)/shard_map/ppermute | solution.py:236
  6.4 8.8 %collective-permute-done.refs_2_.refs_4_ = bf16[2,144,768]{2,1,0:T(8,128)(2,1)S(1)} collective-permute-done((bf16[2,144,768]{2,1,0:T(8,128)(2,1)S(1)}, bf16[2,144,768]{2,1,0:T(8,128)(2,1)S(1)}, u32[]{:S(2)}, u32[]{:S(2)}) %collective-permute-start) | collective-permute-done | bytes 442400 | tf_op jit(solution)/shard_map/ppermute | solution.py:236
  15.2 2.1 %collective-permute-start.1 = (bf16[2,144,768]{2,1,0:T(8,128)(2,1)S(1)}, bf16[2,144,768]{2,1,0:T(8,128)(2,1)S(1)}, u32[]{:S(2)}, u32[]{:S(2)}) collective-permute-start(bf16[2,144,768]{2,1,0:T(8,128)(2,1)S(1)} %collective-permute-done.refs_2_.refs_4_), channel_id=1, source_target_pairs={{0,2},{2,4},{4,6},{6,7},{7,5},{5,3},{3,1},{1,0},{8,10},{10,12},{12... | collective-permute-start | bytes 1327112 | tf_op jit(solution)/shard_map/ppermute | solution.py:236
  19.0 2.3 %cross.5 = (f32[576,384]{1,0:T(8,128)S(1)}, bf16[576,384]{1,0:T(8,128)(2,1)S(1)}) custom-call(s32[5]{0:T(128)S(1)} %pad_add_fusion.flags, bf16[2,768,768]{2,1,0:T(8,128)(2,1)S(1)} %bitcast.5, bf16[2,144,768]{2,1,0:T(8,128)(2,1)S(1)} %get-tuple-element.48.refs_0_.refs_2_, bf16[2,144,768]{2,1,0:T(8,128)(2,1)S(1)} %get-tuple-element.47.refs_1_.refs_3_, ...), custom_call_target="tpu_custom_call" | custom-call | flops 1358955 | bytes 5899 | tf_op jit(solution)/shard_map/cross/pallas_call | solution.py:59
  21.4 3.3 %collective-permute-done.8.refs_0_.refs_6_ = bf16[2,144,768]{2,1,0:T(8,128)(2,1)S(1)} collective-permute-done((bf16[2,144,768]{2,1,0:T(8,128)(2,1)S(1)}, bf16[2,144,768]{2,1,0:T(8,128)(2,1)S(1)}, u32[]{:S(2)}, u32[]{:S(2)}) %collective-permute-start.8) | collective-permute-done | bytes 442400 | tf_op jit(solution)/shard_map/ppermute | solution.py:236
  24.7 2.1 %collective-permute-start.16 = (bf16[2,144,768]{2,1,0:T(8,128)(2,1)S(1)}, bf16[2,144,768]{2,1,0:T(8,128)(2,1)S(1)}, u32[]{:S(2)}, u32[]{:S(2)}) collective-permute-start(bf16[2,144,768]{2,1,0:T(8,128)(2,1)S(1)} %collective-permute-done.8.refs_0_.refs_6_), channel_id=1, source_target_pairs={{0,2},{2,4},{4,6},{6,7},{7,5},{5,3},{3,1},{1,0},{8,10},{10,12},{12... | collective-permute-start | bytes 1327112 | tf_op jit(solution)/shard_map/ppermute | solution.py:236
  26.9 7.3 %collective-permute-done.1.refs_2_.refs_8_ = bf16[2,144,768]{2,1,0:T(8,128)(2,1)S(1)} collective-permute-done((bf16[2,144,768]{2,1,0:T(8,128)(2,1)S(1)}, bf16[2,144,768]{2,1,0:T(8,128)(2,1)S(1)}, u32[]{:S(2)}, u32[]{:S(2)}) %collective-permute-start.1) | collective-permute-done | bytes 442400 | tf_op jit(solution)/shard_map/ppermute | solution.py:236
  34.2 2.2 %collective-permute-done.3.refs_3_.refs_9_ = bf16[2,144,768]{2,1,0:T(8,128)(2,1)S(1)} collective-permute-done((bf16[2,144,768]{2,1,0:T(8,128)(2,1)S(1)}, bf16[2,144,768]{2,1,0:T(8,128)(2,1)S(1)}, u32[]{:S(2)}, u32[]{:S(2)}) %collective-permute-start.3) | collective-permute-done | bytes 442400 | tf_op jit(solution)/shard_map/ppermute | solution.py:237
  36.3 2.2 %cross.6 = (f32[576,384]{1,0:T(8,128)S(1)}, bf16[576,384]{1,0:T(8,128)(2,1)S(1)}) custom-call(s32[5]{0:T(128)S(1)} %pad_add_fusion.flags, bf16[2,768,768]{2,1,0:T(8,128)(2,1)S(1)} %bitcast.6, bf16[2,144,768]{2,1,0:T(8,128)(2,1)S(1)} %collective-permute-done.8.refs_0_.refs_6_, bf16[2,144,768]{2,1,0:T(8,128)(2,1)S(1)} %collective-permute-done.9.refs_1_.refs_7_, ...), custom_call_target="tpu_custom_call" | custom-call | flops 1358955 | bytes 5899 | tf_op jit(solution)/shard_map/cross/pallas_call | solution.py:59
  40.8 2.8 %collective-permute-done.16.refs_0_.refs_1_ = bf16[2,144,768]{2,1,0:T(8,128)(2,1)S(1)} collective-permute-done((bf16[2,144,768]{2,1,0:T(8,128)(2,1)S(1)}, bf16[2,144,768]{2,1,0:T(8,128)(2,1)S(1)}, u32[]{:S(2)}, u32[]{:S(2)}) %collective-permute-start.16) | collective-permute-done | bytes 442400 | tf_op jit(solution)/shard_map/ppermute | solution.py:236
  43.7 2.0 %collective-permute-start.7 = (bf16[576,384]{1,0:T(8,128)(2,1)S(1)}, bf16[576,384]{1,0:T(8,128)(2,1)S(1)}, u32[]{:S(2)}, u32[]{:S(2)}) collective-permute-start(bf16[576,384]{1,0:T(8,128)(2,1)S(1)} %fusion), channel_id=1, source_target_pairs={{0,16},{8,24},{16,0},{24,8},{1,17},{9,25},{17,1},{25,9},{2,18},{10... | collective-permute-start | bytes 1327112 | tf_op jit(solution)/shard_map/ppermute | solution.py:209
  47.8 5.4 %collective-permute-done.5.refs_2_.refs_3_ = bf16[2,144,768]{2,1,0:T(8,128)(2,1)S(1)} collective-permute-done((bf16[2,144,768]{2,1,0:T(8,128)(2,1)S(1)}, bf16[2,144,768]{2,1,0:T(8,128)(2,1)S(1)}, u32[]{:S(2)}, u32[]{:S(2)}) %collective-permute-start.5) | collective-permute-done | bytes 442400 | tf_op jit(solution)/shard_map/ppermute | solution.py:236
  53.1 2.0 %collective-permute-start.13 = (bf16[576,384]{1,0:T(8,128)(2,1)S(1)}, bf16[576,384]{1,0:T(8,128)(2,1)S(1)}, u32[]{:S(2)}, u32[]{:S(2)}) collective-permute-start(bf16[576,384]{1,0:T(8,128)(2,1)S(1)} %fusion.1), channel_id=1, source_target_pairs={{0,16},{8,24},{16,0},{24,8},{1,17},{9,25},{17,1},{25,9},{2,18},{10... | collective-permute-start | bytes 1327112 | tf_op jit(solution)/shard_map/ppermute | solution.py:209
  55.1 2.2 %cross.9 = (f32[576,384]{1,0:T(8,128)S(1)}, bf16[576,384]{1,0:T(8,128)(2,1)S(1)}) custom-call(s32[5]{0:T(128)S(1)} %pad_add_fusion.flags, bf16[2,768,768]{2,1,0:T(8,128)(2,1)S(1)} %bitcast.7, bf16[2,144,768]{2,1,0:T(8,128)(2,1)S(1)} %collective-permute-done.16.refs_0_.refs_1_, bf16[2,144,768]{2,1,0:T(8,128)(2,1)S(1)} %collective-permute-done.18.refs_1_.refs_2_, ...), custom_call_target="tpu_custom_call" | custom-call | flops 1358955 | bytes 5899 | tf_op jit(solution)/shard_map/cross/pallas_call | solution.py:59
  58.1 3.6 %collective-permute-done.17.refs_0_ = bf16[2,144,768]{2,1,0:T(8,128)(2,1)S(1)} collective-permute-done((bf16[2,144,768]{2,1,0:T(8,128)(2,1)S(1)}, bf16[2,144,768]{2,1,0:T(8,128)(2,1)S(1)}, u32[]{:S(2)}, u32[]{:S(2)}) %collective-permute-start.17) | collective-permute-done | bytes 442400 | tf_op jit(solution)/shard_map/ppermute | solution.py:236
  61.8 1.8 %collective-permute-start.11 = (bf16[2,144,768]{2,1,0:T(8,128)(2,1)S(1)}, bf16[2,144,768]{2,1,0:T(8,128)(2,1)S(1)}, u32[]{:S(2)}, u32[]{:S(2)}) collective-permute-start(bf16[2,144,768]{2,1,0:T(8,128)(2,1)S(1)} %collective-permute-done.5.refs_2_.refs_3_), channel_id=1, source_target_pairs={{0,2},{2,4},{4,6},{6,7},{7,5},{5,3},{3,1},{1,0},{8,10},{10,12},{12... | collective-permute-start | bytes 1327112 | tf_op jit(solution)/shard_map/ppermute | solution.py:236
  66.9 1.7 %collective-permute-start.24 = (bf16[576,384]{1,0:T(8,128)(2,1)S(1)}, bf16[576,384]{1,0:T(8,128)(2,1)S(1)}, u32[]{:S(2)}, u32[]{:S(2)}) collective-permute-start(bf16[576,384]{1,0:T(8,128)(2,1)S(1)} %fusion.2), channel_id=1, source_target_pairs={{0,16},{8,24},{16,0},{24,8},{1,17},{9,25},{17,1},{25,9},{2,18},{10... | collective-permute-start | bytes 1327112 | tf_op jit(solution)/shard_map/ppermute | solution.py:209
  69.0 5.8 %numer.2.refs_0_ = f32[2,768,768]{2,1,0:T(8,128)S(1)} custom-call(s32[5]{0:T(128)S(1)} %pad_add_fusion.flags, bf16[2,768,768]{2,1,0:T(8,128)(2,1)S(1)} %bitcast.9, bf16[768,768]{1,0:T(8,128)(2,1)S(1)} %copy-done.2, bf16[2,144,768]{2,1,0:T(8,128)(2,1)S(1)} %get-tuple-element.48.refs_0_.refs_2_, bf16[2,144,768]{2,1,0:T(8,128)(2,1)S(1)} %get-tuple-element.47.refs_1_.refs_3_, ...), custom_call_target="tpu_custom_call" | custom-call | flops 4529849 | bytes 12387 | tf_op jit(solution)/shard_map/numer/pallas_call | solution.py:121
  76.4 3.5 %collective-permute-done.24 = bf16[576,384]{1,0:T(8,128)(2,1)S(1)} collective-permute-done((bf16[576,384]{1,0:T(8,128)(2,1)S(1)}, bf16[576,384]{1,0:T(8,128)(2,1)S(1)}, u32[]{:S(2)}, u32[]{:S(2)}) %collective-permute-start.24) | collective-permute-done | bytes 442400 | tf_op jit(solution)/shard_map/ppermute | solution.py:209
  80.2 1.8 %collective-permute-start.22 = (bf16[288,384]{1,0:T(8,128)(2,1)S(1)}, bf16[288,384]{1,0:T(8,128)(2,1)S(1)}, u32[]{:S(2)}, u32[]{:S(2)}) collective-permute-start(bf16[288,384]{1,0:T(8,128)(2,1)S(1)} %fusion.4), channel_id=1, source_target_pairs={{0,16},{8,24},{16,0},{24,8},{1,17},{9,25},{17,1},{25,9},{2,18},{10... | collective-permute-start | bytes 663560 | tf_op jit(solution)/shard_map/ppermute | solution.py:209
  82.0 2.2 %collective-permute-done.26 = bf16[288,384]{1,0:T(8,128)(2,1)S(1)} collective-permute-done((bf16[288,384]{1,0:T(8,128)(2,1)S(1)}, bf16[288,384]{1,0:T(8,128)(2,1)S(1)}, u32[]{:S(2)}, u32[]{:S(2)}) %collective-permute-start.26) | collective-permute-done | bytes 221216 | tf_op jit(solution)/shard_map/ppermute | solution.py:209
  84.4 2.7 %numer.3.acc_ref = f32[2,768,768]{2,1,0:T(8,128)S(1)} custom-call(s32[5]{0:T(128)S(1)} %pad_add_fusion.flags, f32[2,768,768]{2,1,0:T(8,128)S(1)} %numer.2.refs_0_, bf16[2,144,768]{2,1,0:T(8,128)(2,1)S(1)} %collective-permute-done.16.refs_0_.refs_1_, bf16[2,144,768]{2,1,0:T(8,128)(2,1)S(1)} %collective-permute-done.18.refs_1_.refs_2_, ...), custom_call_target="tpu_custom_call", output_to_operand_aliasing={{}: (1, {})} | custom-call | flops 1358955 | bytes 9733 | tf_op jit(solution)/shard_map/numer/pallas_call | solution.py:121
  90.2 3.9 %final.1 = bf16[2,1,768,768]{3,2,1,0:T(8,128)(2,1)} custom-call(s32[5]{0:T(128)S(1)} %pad_add_fusion.flags, f32[8]{0:T(128)S(1)} %copy-done.3, f32[2,768,768]{2,1,0:T(8,128)S(1)} %numer.3.acc_ref, bf16[2,768,768]{2,1,0:T(8,128)(2,1)S(1)} %bitcast.11, f32[1,768]{1,0:T(1,128)S(1)} %broadcast_in_dim.6.eps_row, f32[768,1]{1,0:T(8,128)S(1)} %broadcast_in_dim.8.eps_col, ...), custom_call_target="tpu_custom_call" | custom-call | flops 1358955 | bytes 9438 | tf_op jit(solution)/shard_map/final/pallas_call | solution.py:171
  (68 shorter events, 16.9 us)
Async XLA Ops:
  1.2 14.0 %collective-permute-start = (bf16[2,144,768]{2,1,0:T(8,128)(2,1)S(1)}, bf16[2,144,768]{2,1,0:T(8,128)(2,1)S(1)}, u32[]{:S(2)}, u32[]{:S(2)}) collective-permute-start(bf16[2,144,768]{2,1,0:T(8,128)(2,1)S(1)} %get-tuple-element.48.refs_0_.refs_2_), channel_id=1, source_target_pairs={{0,2},{2,4},{4,6},{6,7},{7,5},{5,3},{3,1},{1,0},{8,10},{10,12},{12... | collective-permute-start | bytes 1327112 | tf_op jit(solution)/shard_map/ppermute | solution.py:236
  4.3 13.1 %collective-permute-start.2 = (bf16[2,144,768]{2,1,0:T(8,128)(2,1)S(1)}, bf16[2,144,768]{2,1,0:T(8,128)(2,1)S(1)}, u32[]{:S(2)}, u32[]{:S(2)}) collective-permute-start(bf16[2,144,768]{2,1,0:T(8,128)(2,1)S(1)} %get-tuple-element.47.refs_1_.refs_3_), channel_id=1, source_target_pairs={{2,0},{4,2},{6,4},{7,6},{5,7},{3,5},{1,3},{0,1},{10,8},{12,10},{14... | collective-permute-start | bytes 1327112 | tf_op jit(solution)/shard_map/ppermute | solution.py:237
  4.3 20.4 %collective-permute-start.8 = (bf16[2,144,768]{2,1,0:T(8,128)(2,1)S(1)}, bf16[2,144,768]{2,1,0:T(8,128)(2,1)S(1)}, u32[]{:S(2)}, u32[]{:S(2)}) collective-permute-start(bf16[2,144,768]{2,1,0:T(8,128)(2,1)S(1)} %get-tuple-element.47.refs_1_.refs_3_), channel_id=1, source_target_pairs={{0,2},{2,4},{4,6},{6,7},{7,5},{5,3},{3,1},{1,0},{8,10},{10,12},{12... | collective-permute-start | bytes 1327112 | tf_op jit(solution)/shard_map/ppermute | solution.py:236
  6.3 20.5 %collective-permute-start.9 = (bf16[2,144,768]{2,1,0:T(8,128)(2,1)S(1)}, bf16[2,144,768]{2,1,0:T(8,128)(2,1)S(1)}, u32[]{:S(2)}, u32[]{:S(2)}) collective-permute-start(bf16[2,144,768]{2,1,0:T(8,128)(2,1)S(1)} %get-tuple-element.48.refs_0_.refs_2_), channel_id=1, source_target_pairs={{2,0},{4,2},{6,4},{7,6},{5,7},{3,5},{1,3},{0,1},{10,8},{12,10},{14... | collective-permute-start | bytes 1327112 | tf_op jit(solution)/shard_map/ppermute | solution.py:237
  15.2 19.0 %collective-permute-start.1 = (bf16[2,144,768]{2,1,0:T(8,128)(2,1)S(1)}, bf16[2,144,768]{2,1,0:T(8,128)(2,1)S(1)}, u32[]{:S(2)}, u32[]{:S(2)}) collective-permute-start(bf16[2,144,768]{2,1,0:T(8,128)(2,1)S(1)} %collective-permute-done.refs_2_.refs_4_), channel_id=1, source_target_pairs={{0,2},{2,4},{4,6},{6,7},{7,5},{5,3},{3,1},{1,0},{8,10},{10,12},{12... | collective-permute-start | bytes 1327112 | tf_op jit(solution)/shard_map/ppermute | solution.py:236
  17.4 19.0 %collective-permute-start.3 = (bf16[2,144,768]{2,1,0:T(8,128)(2,1)S(1)}, bf16[2,144,768]{2,1,0:T(8,128)(2,1)S(1)}, u32[]{:S(2)}, u32[]{:S(2)}) collective-permute-start(bf16[2,144,768]{2,1,0:T(8,128)(2,1)S(1)} %collective-permute-done.2.refs_3_.refs_5_), channel_id=1, source_target_pairs={{2,0},{4,2},{6,4},{7,6},{5,7},{3,5},{1,3},{0,1},{10,8},{12,10},{14... | collective-permute-start | bytes 1327112 | tf_op jit(solution)/shard_map/ppermute | solution.py:237
  21.3 17.4 %collective-permute-start.4 = (bf16[576,384]{1,0:T(8,128)(2,1)S(1)}, bf16[576,384]{1,0:T(8,128)(2,1)S(1)}, u32[]{:S(2)}, u32[]{:S(2)}) collective-permute-start(bf16[576,384]{1,0:T(8,128)(2,1)S(1)} %get-tuple-element.27), channel_id=1, source_target_pairs={{0,8},{8,0},{16,24},{24,16},{1,9},{9,1},{17,25},{25,17},{2,10},{10... | collective-permute-start | bytes 1327112 | tf_op jit(solution)/shard_map/ppermute | solution.py:209
  24.7 19.0 %collective-permute-start.16 = (bf16[2,144,768]{2,1,0:T(8,128)(2,1)S(1)}, bf16[2,144,768]{2,1,0:T(8,128)(2,1)S(1)}, u32[]{:S(2)}, u32[]{:S(2)}) collective-permute-start(bf16[2,144,768]{2,1,0:T(8,128)(2,1)S(1)} %collective-permute-done.8.refs_0_.refs_6_), channel_id=1, source_target_pairs={{0,2},{2,4},{4,6},{6,7},{7,5},{5,3},{3,1},{1,0},{8,10},{10,12},{12... | collective-permute-start | bytes 1327112 | tf_op jit(solution)/shard_map/ppermute | solution.py:236
  26.9 18.8 %collective-permute-start.18 = (bf16[2,144,768]{2,1,0:T(8,128)(2,1)S(1)}, bf16[2,144,768]{2,1,0:T(8,128)(2,1)S(1)}, u32[]{:S(2)}, u32[]{:S(2)}) collective-permute-start(bf16[2,144,768]{2,1,0:T(8,128)(2,1)S(1)} %collective-permute-done.9.refs_1_.refs_7_), channel_id=1, source_target_pairs={{2,0},{4,2},{6,4},{7,6},{5,7},{3,5},{1,3},{0,1},{10,8},{12,10},{14... | collective-permute-start | bytes 1327112 | tf_op jit(solution)/shard_map/ppermute | solution.py:237
  38.6 8.6 %collective-permute-start.10 = (bf16[576,384]{1,0:T(8,128)(2,1)S(1)}, bf16[576,384]{1,0:T(8,128)(2,1)S(1)}, u32[]{:S(2)}, u32[]{:S(2)}) collective-permute-start(bf16[576,384]{1,0:T(8,128)(2,1)S(1)} %get-tuple-element.31), channel_id=1, source_target_pairs={{0,8},{8,0},{16,24},{24,16},{1,9},{9,1},{17,25},{25,17},{2,10},{10... | collective-permute-start | bytes 1327112 | tf_op jit(solution)/shard_map/ppermute | solution.py:209
  38.8 14.4 %collective-permute-start.5 = (bf16[2,144,768]{2,1,0:T(8,128)(2,1)S(1)}, bf16[2,144,768]{2,1,0:T(8,128)(2,1)S(1)}, u32[]{:S(2)}, u32[]{:S(2)}) collective-permute-start(bf16[2,144,768]{2,1,0:T(8,128)(2,1)S(1)} %collective-permute-done.1.refs_2_.refs_8_), channel_id=1, source_target_pairs={{0,2},{2,4},{4,6},{6,7},{7,5},{5,3},{3,1},{1,0},{8,10},{10,12},{12... | collective-permute-start | bytes 1327112 | tf_op jit(solution)/shard_map/ppermute | solution.py:236
  40.4 14.7 %collective-permute-start.6 = (bf16[2,144,768]{2,1,0:T(8,128)(2,1)S(1)}, bf16[2,144,768]{2,1,0:T(8,128)(2,1)S(1)}, u32[]{:S(2)}, u32[]{:S(2)}) collective-permute-start(bf16[2,144,768]{2,1,0:T(8,128)(2,1)S(1)} %collective-permute-done.3.refs_3_.refs_9_), channel_id=1, source_target_pairs={{2,0},{4,2},{6,4},{7,6},{5,7},{3,5},{1,3},{0,1},{10,8},{12,10},{14... | collective-permute-start | bytes 1327112 | tf_op jit(solution)/shard_map/ppermute | solution.py:237
  43.7 13.8 %collective-permute-start.7 = (bf16[576,384]{1,0:T(8,128)(2,1)S(1)}, bf16[576,384]{1,0:T(8,128)(2,1)S(1)}, u32[]{:S(2)}, u32[]{:S(2)}) collective-permute-start(bf16[576,384]{1,0:T(8,128)(2,1)S(1)} %fusion), channel_id=1, source_target_pairs={{0,16},{8,24},{16,0},{24,8},{1,17},{9,25},{17,1},{25,9},{2,18},{10... | collective-permute-start | bytes 1327112 | tf_op jit(solution)/shard_map/ppermute | solution.py:209
  45.6 16.2 %collective-permute-start.17 = (bf16[2,144,768]{2,1,0:T(8,128)(2,1)S(1)}, bf16[2,144,768]{2,1,0:T(8,128)(2,1)S(1)}, u32[]{:S(2)}, u32[]{:S(2)}) collective-permute-start(bf16[2,144,768]{2,1,0:T(8,128)(2,1)S(1)} %collective-permute-done.16.refs_0_.refs_1_), channel_id=1, source_target_pairs={{0,2},{2,4},{4,6},{6,7},{7,5},{5,3},{3,1},{1,0},{8,10},{10,12},{12... | collective-permute-start | bytes 1327112 | tf_op jit(solution)/shard_map/ppermute | solution.py:236
  47.2 16.4 %collective-permute-start.19 = (bf16[2,144,768]{2,1,0:T(8,128)(2,1)S(1)}, bf16[2,144,768]{2,1,0:T(8,128)(2,1)S(1)}, u32[]{:S(2)}, u32[]{:S(2)}) collective-permute-start(bf16[2,144,768]{2,1,0:T(8,128)(2,1)S(1)} %collective-permute-done.18.refs_1_.refs_2_), channel_id=1, source_target_pairs={{2,0},{4,2},{6,4},{7,6},{5,7},{3,5},{1,3},{0,1},{10,8},{12,10},{14... | collective-permute-start | bytes 1327112 | tf_op jit(solution)/shard_map/ppermute | solution.py:237
  53.1 12.1 %collective-permute-start.13 = (bf16[576,384]{1,0:T(8,128)(2,1)S(1)}, bf16[576,384]{1,0:T(8,128)(2,1)S(1)}, u32[]{:S(2)}, u32[]{:S(2)}) collective-permute-start(bf16[576,384]{1,0:T(8,128)(2,1)S(1)} %fusion.1), channel_id=1, source_target_pairs={{0,16},{8,24},{16,0},{24,8},{1,17},{9,25},{17,1},{25,9},{2,18},{10... | collective-permute-start | bytes 1327112 | tf_op jit(solution)/shard_map/ppermute | solution.py:209
  57.3 8.2 %collective-permute-start.23 = (bf16[576,384]{1,0:T(8,128)(2,1)S(1)}, bf16[576,384]{1,0:T(8,128)(2,1)S(1)}, u32[]{:S(2)}, u32[]{:S(2)}) collective-permute-start(bf16[576,384]{1,0:T(8,128)(2,1)S(1)} %get-tuple-element.44), channel_id=1, source_target_pairs={{0,8},{8,0},{16,24},{24,16},{1,9},{9,1},{17,25},{25,17},{2,10},{10... | collective-permute-start | bytes 1327112 | tf_op jit(solution)/shard_map/ppermute | solution.py:209
  57.6 11.0 %collective-permute-start.14 = (bf16[576,384]{1,0:T(8,128)(2,1)S(1)}, bf16[576,384]{1,0:T(8,128)(2,1)S(1)}, u32[]{:S(2)}, u32[]{:S(2)}) collective-permute-start(bf16[576,384]{1,0:T(8,128)(2,1)S(1)} %add_convert_fusion.2.refs_10_), channel_id=1, source_target_pairs={{0,8},{8,0},{16,24},{24,16},{1,9},{9,1},{17,25},{25,17},{2,10},{10... | collective-permute-start | bytes 1327112 | tf_op jit(solution)/shard_map/ppermute | solution.py:209
  61.8 13.0 %collective-permute-start.11 = (bf16[2,144,768]{2,1,0:T(8,128)(2,1)S(1)}, bf16[2,144,768]{2,1,0:T(8,128)(2,1)S(1)}, u32[]{:S(2)}, u32[]{:S(2)}) collective-permute-start(bf16[2,144,768]{2,1,0:T(8,128)(2,1)S(1)} %collective-permute-done.5.refs_2_.refs_3_), channel_id=1, source_target_pairs={{0,2},{2,4},{4,6},{6,7},{7,5},{5,3},{3,1},{1,0},{8,10},{10,12},{12... | collective-permute-start | bytes 1327112 | tf_op jit(solution)/shard_map/ppermute | solution.py:236
  63.6 11.2 %collective-permute-start.12 = (bf16[2,144,768]{2,1,0:T(8,128)(2,1)S(1)}, bf16[2,144,768]{2,1,0:T(8,128)(2,1)S(1)}, u32[]{:S(2)}, u32[]{:S(2)}) collective-permute-start(bf16[2,144,768]{2,1,0:T(8,128)(2,1)S(1)} %collective-permute-done.6.refs_3_.refs_4_), channel_id=1, source_target_pairs={{2,0},{4,2},{6,4},{7,6},{5,7},{3,5},{1,3},{0,1},{10,8},{12,10},{14... | collective-permute-start | bytes 1327112 | tf_op jit(solution)/shard_map/ppermute | solution.py:237
  66.9 13.0 %collective-permute-start.24 = (bf16[576,384]{1,0:T(8,128)(2,1)S(1)}, bf16[576,384]{1,0:T(8,128)(2,1)S(1)}, u32[]{:S(2)}, u32[]{:S(2)}) collective-permute-start(bf16[576,384]{1,0:T(8,128)(2,1)S(1)} %fusion.2), channel_id=1, source_target_pairs={{0,16},{8,24},{16,0},{24,8},{1,17},{9,25},{17,1},{25,9},{2,18},{10... | collective-permute-start | bytes 1327112 | tf_op jit(solution)/shard_map/ppermute | solution.py:209
  68.6 15.6 %collective-permute-start.26 = (bf16[288,384]{1,0:T(8,128)(2,1)S(1)}, bf16[288,384]{1,0:T(8,128)(2,1)S(1)}, u32[]{:S(2)}, u32[]{:S(2)}) collective-permute-start(bf16[288,384]{1,0:T(8,128)(2,1)S(1)} %fusion.3), channel_id=1, source_target_pairs={{0,16},{8,24},{16,0},{24,8},{1,17},{9,25},{17,1},{25,9},{2,18},{10... | collective-permute-start | bytes 663560 | tf_op jit(solution)/shard_map/ppermute | solution.py:209
  80.2 8.4 %collective-permute-start.22 = (bf16[288,384]{1,0:T(8,128)(2,1)S(1)}, bf16[288,384]{1,0:T(8,128)(2,1)S(1)}, u32[]{:S(2)}, u32[]{:S(2)}) collective-permute-start(bf16[288,384]{1,0:T(8,128)(2,1)S(1)} %fusion.4), channel_id=1, source_target_pairs={{0,16},{8,24},{16,0},{24,8},{1,17},{9,25},{17,1},{25,9},{2,18},{10... | collective-permute-start | bytes 663560 | tf_op jit(solution)/shard_map/ppermute | solution.py:209
  84.3 4.6 %collective-permute-start.27 = (bf16[288,384]{1,0:T(8,128)(2,1)S(1)}, bf16[288,384]{1,0:T(8,128)(2,1)S(1)}, u32[]{:S(2)}, u32[]{:S(2)}) collective-permute-start(bf16[288,384]{1,0:T(8,128)(2,1)S(1)} %add_convert_fusion.4.refs_4_), channel_id=1, source_target_pairs={{0,8},{8,0},{16,24},{24,16},{1,9},{9,1},{17,25},{25,17},{2,10},{10... | collective-permute-start | bytes 663560 | tf_op jit(solution)/shard_map/ppermute | solution.py:209
  (10 other events, 34.2 us)

commit v5 on v4

--- a/solution.py
+++ b/solution.py
@@ -219,11 +219,11 @@
     ties = {}
     for n, end in enumerate(ends[:-1]):
         if n != ng - 3:
-            z_at = "R%d" % (end + 4) if end + 4 <= last else "C%d" % (n + 1)
+            z_at = "R%d" % (end + 4) if end + 4 < last else "C%d" % min(n + 2, ng - 1)
             ties.setdefault(z_at, []).append("Z%d" % n)
-        if n < ng - 3:
-            w_at = "R%d" % (end + 6) if end + 6 <= last else "C%d" % (ng - 1)
-            ties.setdefault(w_at, []).append("W%d" % n)
+        if n < ng - 3 and end + 6 <= last:
+            ties.setdefault("R%d" % (end + 6), []).append("W%d" % n)
+    ties.setdefault("R4", []).append("X0")
 
     def tie(value, target):
         src = [vals[x] for x in ties.get(target, [])]
@@ -258,6 +258,7 @@
             continue
         group = through(group, "C%d" % g)
         total, send = cross(flags, t, group)
+        vals["X%d" % g] = send
         total = total + swap(send, 1).astype(jnp.float32)
         bit = 2
         while bit < n_row:

time: 94.4 us -> 94.4 us (level)
    ppermute x7, waiting for transfers between devices: 2.24 us -> 4.35 us  [ring_step(): downs[down_h] = lax.ppermute(downs[down_h], 'col', down)]
    ppermute x7, waiting for transfers between devices: 31.3 us -> 29.3 us  [ring_step(): ups[up_h] = lax.ppermute(ups[up_h], 'col', up)]
  transfers between devices with their start and end apart: 29 -> 29, of which waited for: 12 -> 13; matrix products, arithmetic and copies ran while one was open for 1% -> 1% of each run, Pallas kernels for 19% -> 19%
where the time goes in v5:
time: 94.4 us; the launch traced here: 94.2 us
  waiting for transfers between devices  42.7 us (45%)
  starting transfers between devices  24.9 us (26%)
  Pallas kernels  22 us (23%)
  local copies, waits for them, and re-layouts  3.06 us (3%)
  other arithmetic  1.14 us (1%)
    ppermute x7, waiting for transfers between devices, ring_step(): ups[up_h] = lax.ppermute(ups[up_h], 'col', up)  29.3 us
    ppermute x7, starting transfers between devices, ring_step(): ups[up_h] = lax.ppermute(ups[up_h], 'col', up)  13.8 us
    pallas_call x5, Pallas kernels, cross(): pl.pallas_call(cross_kernel, out_shape=(jax.ShapeDtypeStruct((rows, vir /...  9.62 us
    ppermute x15, starting transfers between devices, swap(): return lax.ppermute(x, 'row', [(r, r ^ bit) for r in range(n_row)])  9.48 us
    ppermute x15, waiting for transfers between devices, swap(): return lax.ppermute(x, 'row', [(r, r ^ bit) for r in range(n_row)])  9.1 us
    pallas_call x2, Pallas kernels, numer(): pl.pallas_call(functools.partial(numer_kernel, len(chunks), len(mine), fr...  8.48 us
    ppermute x7, waiting for transfers between devices, ring_step(): downs[down_h] = lax.ppermute(downs[down_h], 'col', down)  4.35 us
    pallas_call x1, Pallas kernels, final(): pl.pallas_call(functools.partial(final_kernel, len(chunks), len(mine)), o...  3.85 us
  transfers between devices with their start and end apart: 29, of which 13 were waited for; matrix products, arithmetic and copies ran while one was open for 1% of the time, Pallas kernels for 19%

profile of v5, /device:TPU:0, one launch (start us, length us, event | category | flops | bytes accessed | tf_op | source)
XLA Modules:
  0.0 94.2 jit_solution(4322526243574120303)
XLA Ops:
  1.2 3.1 %collective-permute-start = (bf16[2,144,768]{2,1,0:T(8,128)(2,1)S(1)}, bf16[2,144,768]{2,1,0:T(8,128)(2,1)S(1)}, u32[]{:S(2)}, u32[]{:S(2)}) collective-permute-start(bf16[2,144,768]{2,1,0:T(8,128)(2,1)S(1)} %get-tuple-element.56.refs_0_.refs_2_), channel_id=1, source_target_pairs={{0,2},{2,4},{4,6},{6,7},{7,5},{5,3},{3,1},{1,0},{8,10},{10,12},{12... | collective-permute-start | bytes 1327112 | tf_op jit(solution)/shard_map/ppermute | solution.py:236
  4.3 2.0 %collective-permute-start.10 = (bf16[2,144,768]{2,1,0:T(8,128)(2,1)S(1)}, bf16[2,144,768]{2,1,0:T(8,128)(2,1)S(1)}, u32[]{:S(2)}, u32[]{:S(2)}) collective-permute-start(bf16[2,144,768]{2,1,0:T(8,128)(2,1)S(1)} %get-tuple-element.55.refs_1_.refs_3_), channel_id=1, source_target_pairs={{0,2},{2,4},{4,6},{6,7},{7,5},{5,3},{3,1},{1,0},{8,10},{10,12},{12... | collective-permute-start | bytes 1327112 | tf_op jit(solution)/shard_map/ppermute | solution.py:236
  6.4 8.8 %collective-permute-done.refs_2_.refs_4_ = bf16[2,144,768]{2,1,0:T(8,128)(2,1)S(1)} collective-permute-done((bf16[2,144,768]{2,1,0:T(8,128)(2,1)S(1)}, bf16[2,144,768]{2,1,0:T(8,128)(2,1)S(1)}, u32[]{:S(2)}, u32[]{:S(2)}) %collective-permute-start) | collective-permute-done | bytes 442400 | tf_op jit(solution)/shard_map/ppermute | solution.py:236
  15.2 2.1 %collective-permute-start.1 = (bf16[2,144,768]{2,1,0:T(8,128)(2,1)S(1)}, bf16[2,144,768]{2,1,0:T(8,128)(2,1)S(1)}, u32[]{:S(2)}, u32[]{:S(2)}) collective-permute-start(bf16[2,144,768]{2,1,0:T(8,128)(2,1)S(1)} %collective-permute-done.refs_2_.refs_4_), channel_id=1, source_target_pairs={{0,2},{2,4},{4,6},{6,7},{7,5},{5,3},{3,1},{1,0},{8,10},{10,12},{12... | collective-permute-start | bytes 1327112 | tf_op jit(solution)/shard_map/ppermute | solution.py:236
  19.0 2.3 %cross.5 = (f32[576,384]{1,0:T(8,128)S(1)}, bf16[576,384]{1,0:T(8,128)(2,1)S(1)}) custom-call(s32[5]{0:T(128)S(1)} %pad_add_fusion.flags, bf16[2,768,768]{2,1,0:T(8,128)(2,1)S(1)} %bitcast.5, bf16[2,144,768]{2,1,0:T(8,128)(2,1)S(1)} %get-tuple-element.56.refs_0_.refs_2_, bf16[2,144,768]{2,1,0:T(8,128)(2,1)S(1)} %get-tuple-element.55.refs_1_.refs_3_, ...), custom_call_target="tpu_custom_call" | custom-call | flops 1358955 | bytes 5899 | tf_op jit(solution)/shard_map/cross/pallas_call | solution.py:59
  21.4 3.3 %collective-permute-done.10.refs_0_.refs_6_ = bf16[2,144,768]{2,1,0:T(8,128)(2,1)S(1)} collective-permute-done((bf16[2,144,768]{2,1,0:T(8,128)(2,1)S(1)}, bf16[2,144,768]{2,1,0:T(8,128)(2,1)S(1)}, u32[]{:S(2)}, u32[]{:S(2)}) %collective-permute-start.10) | collective-permute-done | bytes 442400 | tf_op jit(solution)/shard_map/ppermute | solution.py:236
  24.7 2.2 %collective-permute-done.11.refs_1_.refs_7_ = bf16[2,144,768]{2,1,0:T(8,128)(2,1)S(1)} collective-permute-done((bf16[2,144,768]{2,1,0:T(8,128)(2,1)S(1)}, bf16[2,144,768]{2,1,0:T(8,128)(2,1)S(1)}, u32[]{:S(2)}, u32[]{:S(2)}) %collective-permute-start.11) | collective-permute-done | bytes 442400 | tf_op jit(solution)/shard_map/ppermute | solution.py:237
  28.9 5.3 %collective-permute-done.1.refs_2_.refs_8_ = bf16[2,144,768]{2,1,0:T(8,128)(2,1)S(1)} collective-permute-done((bf16[2,144,768]{2,1,0:T(8,128)(2,1)S(1)}, bf16[2,144,768]{2,1,0:T(8,128)(2,1)S(1)}, u32[]{:S(2)}, u32[]{:S(2)}) %collective-permute-start.1) | collective-permute-done | bytes 442400 | tf_op jit(solution)/shard_map/ppermute | solution.py:236
  34.2 2.2 %collective-permute-done.3.refs_3_.refs_9_ = bf16[2,144,768]{2,1,0:T(8,128)(2,1)S(1)} collective-permute-done((bf16[2,144,768]{2,1,0:T(8,128)(2,1)S(1)}, bf16[2,144,768]{2,1,0:T(8,128)(2,1)S(1)}, u32[]{:S(2)}, u32[]{:S(2)}) %collective-permute-start.3) | collective-permute-done | bytes 442400 | tf_op jit(solution)/shard_map/ppermute | solution.py:237
  36.3 2.2 %cross.6 = (f32[576,384]{1,0:T(8,128)S(1)}, bf16[576,384]{1,0:T(8,128)(2,1)S(1)}) custom-call(s32[5]{0:T(128)S(1)} %pad_add_fusion.flags, bf16[2,768,768]{2,1,0:T(8,128)(2,1)S(1)} %bitcast.6, bf16[2,144,768]{2,1,0:T(8,128)(2,1)S(1)} %collective-permute-done.10.refs_0_.refs_6_, bf16[2,144,768]{2,1,0:T(8,128)(2,1)S(1)} %collective-permute-done.11.refs_1_.refs_7_, ...), custom_call_target="tpu_custom_call" | custom-call | flops 1358955 | bytes 5899 | tf_op jit(solution)/shard_map/cross/pallas_call | solution.py:59
  40.8 2.8 %collective-permute-done.16.refs_0_.refs_1_ = bf16[2,144,768]{2,1,0:T(8,128)(2,1)S(1)} collective-permute-done((bf16[2,144,768]{2,1,0:T(8,128)(2,1)S(1)}, bf16[2,144,768]{2,1,0:T(8,128)(2,1)S(1)}, u32[]{:S(2)}, u32[]{:S(2)}) %collective-permute-start.16) | collective-permute-done | bytes 442400 | tf_op jit(solution)/shard_map/ppermute | solution.py:236
  43.7 2.0 %collective-permute-start.7 = (bf16[576,384]{1,0:T(8,128)(2,1)S(1)}, bf16[576,384]{1,0:T(8,128)(2,1)S(1)}, u32[]{:S(2)}, u32[]{:S(2)}) collective-permute-start(bf16[576,384]{1,0:T(8,128)(2,1)S(1)} %fusion), channel_id=1, source_target_pairs={{0,16},{8,24},{16,0},{24,8},{1,17},{9,25},{17,1},{25,9},{2,18},{10... | collective-permute-start | bytes 1327112 | tf_op jit(solution)/shard_map/ppermute | solution.py:209
  47.8 5.4 %collective-permute-done.5.refs_2_.refs_3_ = bf16[2,144,768]{2,1,0:T(8,128)(2,1)S(1)} collective-permute-done((bf16[2,144,768]{2,1,0:T(8,128)(2,1)S(1)}, bf16[2,144,768]{2,1,0:T(8,128)(2,1)S(1)}, u32[]{:S(2)}, u32[]{:S(2)}) %collective-permute-start.5) | collective-permute-done | bytes 442400 | tf_op jit(solution)/shard_map/ppermute | solution.py:236
  53.1 2.0 %collective-permute-start.13 = (bf16[576,384]{1,0:T(8,128)(2,1)S(1)}, bf16[576,384]{1,0:T(8,128)(2,1)S(1)}, u32[]{:S(2)}, u32[]{:S(2)}) collective-permute-start(bf16[576,384]{1,0:T(8,128)(2,1)S(1)} %fusion.1), channel_id=1, source_target_pairs={{0,16},{8,24},{16,0},{24,8},{1,17},{9,25},{17,1},{25,9},{2,18},{10... | collective-permute-start | bytes 1327112 | tf_op jit(solution)/shard_map/ppermute | solution.py:209
  55.1 2.2 %cross.9 = (f32[576,384]{1,0:T(8,128)S(1)}, bf16[576,384]{1,0:T(8,128)(2,1)S(1)}) custom-call(s32[5]{0:T(128)S(1)} %pad_add_fusion.flags, bf16[2,768,768]{2,1,0:T(8,128)(2,1)S(1)} %bitcast.7, bf16[2,144,768]{2,1,0:T(8,128)(2,1)S(1)} %collective-permute-done.16.refs_0_.refs_1_, bf16[2,144,768]{2,1,0:T(8,128)(2,1)S(1)} %collective-permute-done.18.refs_1_.refs_2_, ...), custom_call_target="tpu_custom_call" | custom-call | flops 1358955 | bytes 5899 | tf_op jit(solution)/shard_map/cross/pallas_call | solution.py:59
  58.1 3.6 %collective-permute-done.17.refs_0_ = bf16[2,144,768]{2,1,0:T(8,128)(2,1)S(1)} collective-permute-done((bf16[2,144,768]{2,1,0:T(8,128)(2,1)S(1)}, bf16[2,144,768]{2,1,0:T(8,128)(2,1)S(1)}, u32[]{:S(2)}, u32[]{:S(2)}) %collective-permute-start.17) | collective-permute-done | bytes 442400 | tf_op jit(solution)/shard_map/ppermute | solution.py:236
  61.8 1.8 %collective-permute-start.8 = (bf16[2,144,768]{2,1,0:T(8,128)(2,1)S(1)}, bf16[2,144,768]{2,1,0:T(8,128)(2,1)S(1)}, u32[]{:S(2)}, u32[]{:S(2)}) collective-permute-start(bf16[2,144,768]{2,1,0:T(8,128)(2,1)S(1)} %collective-permute-done.5.refs_2_.refs_3_), channel_id=1, source_target_pairs={{0,2},{2,4},{4,6},{6,7},{7,5},{5,3},{3,1},{1,0},{8,10},{10,12},{12... | collective-permute-start | bytes 1327112 | tf_op jit(solution)/shard_map/ppermute | solution.py:236
  66.9 1.7 %collective-permute-start.24 = (bf16[576,384]{1,0:T(8,128)(2,1)S(1)}, bf16[576,384]{1,0:T(8,128)(2,1)S(1)}, u32[]{:S(2)}, u32[]{:S(2)}) collective-permute-start(bf16[576,384]{1,0:T(8,128)(2,1)S(1)} %fusion.2), channel_id=1, source_target_pairs={{0,16},{8,24},{16,0},{24,8},{1,17},{9,25},{17,1},{25,9},{2,18},{10... | collective-permute-start | bytes 1327112 | tf_op jit(solution)/shard_map/ppermute | solution.py:209
  69.0 5.8 %numer.2.refs_0_ = f32[2,768,768]{2,1,0:T(8,128)S(1)} custom-call(s32[5]{0:T(128)S(1)} %pad_add_fusion.flags, bf16[2,768,768]{2,1,0:T(8,128)(2,1)S(1)} %bitcast.9, bf16[768,768]{1,0:T(8,128)(2,1)S(1)} %copy-done.2, bf16[2,144,768]{2,1,0:T(8,128)(2,1)S(1)} %get-tuple-element.56.refs_0_.refs_2_, bf16[2,144,768]{2,1,0:T(8,128)(2,1)S(1)} %get-tuple-element.55.refs_1_.refs_3_, ...), custom_call_target="tpu_custom_call" | custom-call | flops 4529849 | bytes 12387 | tf_op jit(solution)/shard_map/numer/pallas_call | solution.py:121
  76.4 3.5 %collective-permute-done.24 = bf16[576,384]{1,0:T(8,128)(2,1)S(1)} collective-permute-done((bf16[576,384]{1,0:T(8,128)(2,1)S(1)}, bf16[576,384]{1,0:T(8,128)(2,1)S(1)}, u32[]{:S(2)}, u32[]{:S(2)}) %collective-permute-start.24) | collective-permute-done | bytes 442400 | tf_op jit(solution)/shard_map/ppermute | solution.py:209
  80.2 1.8 %collective-permute-start.22 = (bf16[288,384]{1,0:T(8,128)(2,1)S(1)}, bf16[288,384]{1,0:T(8,128)(2,1)S(1)}, u32[]{:S(2)}, u32[]{:S(2)}) collective-permute-start(bf16[288,384]{1,0:T(8,128)(2,1)S(1)} %fusion.4), channel_id=1, source_target_pairs={{0,16},{8,24},{16,0},{24,8},{1,17},{9,25},{17,1},{25,9},{2,18},{10... | collective-permute-start | bytes 663560 | tf_op jit(solution)/shard_map/ppermute | solution.py:209
  82.0 2.2 %collective-permute-done.26 = bf16[288,384]{1,0:T(8,128)(2,1)S(1)} collective-permute-done((bf16[288,384]{1,0:T(8,128)(2,1)S(1)}, bf16[288,384]{1,0:T(8,128)(2,1)S(1)}, u32[]{:S(2)}, u32[]{:S(2)}) %collective-permute-start.26) | collective-permute-done | bytes 221216 | tf_op jit(solution)/shard_map/ppermute | solution.py:209
  84.4 2.7 %numer.3.acc_ref = f32[2,768,768]{2,1,0:T(8,128)S(1)} custom-call(s32[5]{0:T(128)S(1)} %pad_add_fusion.flags, f32[2,768,768]{2,1,0:T(8,128)S(1)} %numer.2.refs_0_, bf16[2,144,768]{2,1,0:T(8,128)(2,1)S(1)} %collective-permute-done.16.refs_0_.refs_1_, bf16[2,144,768]{2,1,0:T(8,128)(2,1)S(1)} %collective-permute-done.18.refs_1_.refs_2_, ...), custom_call_target="tpu_custom_call", output_to_operand_aliasing={{}: (1, {})} | custom-call | flops 1358955 | bytes 9733 | tf_op jit(solution)/shard_map/numer/pallas_call | solution.py:121
  90.2 3.9 %final.1 = bf16[2,1,768,768]{3,2,1,0:T(8,128)(2,1)} custom-call(s32[5]{0:T(128)S(1)} %pad_add_fusion.flags, f32[8]{0:T(128)S(1)} %copy-done.3, f32[2,768,768]{2,1,0:T(8,128)S(1)} %numer.3.acc_ref, bf16[2,768,768]{2,1,0:T(8,128)(2,1)S(1)} %bitcast.11, f32[1,768]{1,0:T(1,128)S(1)} %broadcast_in_dim.6.eps_row, f32[768,1]{1,0:T(8,128)S(1)} %broadcast_in_dim.8.eps_col, ...), custom_call_target="tpu_custom_call" | custom-call | flops 1358955 | bytes 9438 | tf_op jit(solution)/shard_map/final/pallas_call | solution.py:171
  (68 shorter events, 18.9 us)
Async XLA Ops:
  1.2 14.0 %collective-permute-start = (bf16[2,144,768]{2,1,0:T(8,128)(2,1)S(1)}, bf16[2,144,768]{2,1,0:T(8,128)(2,1)S(1)}, u32[]{:S(2)}, u32[]{:S(2)}) collective-permute-start(bf16[2,144,768]{2,1,0:T(8,128)(2,1)S(1)} %get-tuple-element.56.refs_0_.refs_2_), channel_id=1, source_target_pairs={{0,2},{2,4},{4,6},{6,7},{7,5},{5,3},{3,1},{1,0},{8,10},{10,12},{12... | collective-permute-start | bytes 1327112 | tf_op jit(solution)/shard_map/ppermute | solution.py:236
  4.3 13.1 %collective-permute-start.2 = (bf16[2,144,768]{2,1,0:T(8,128)(2,1)S(1)}, bf16[2,144,768]{2,1,0:T(8,128)(2,1)S(1)}, u32[]{:S(2)}, u32[]{:S(2)}) collective-permute-start(bf16[2,144,768]{2,1,0:T(8,128)(2,1)S(1)} %get-tuple-element.55.refs_1_.refs_3_), channel_id=1, source_target_pairs={{2,0},{4,2},{6,4},{7,6},{5,7},{3,5},{1,3},{0,1},{10,8},{12,10},{14... | collective-permute-start | bytes 1327112 | tf_op jit(solution)/shard_map/ppermute | solution.py:237
  4.3 20.4 %collective-permute-start.10 = (bf16[2,144,768]{2,1,0:T(8,128)(2,1)S(1)}, bf16[2,144,768]{2,1,0:T(8,128)(2,1)S(1)}, u32[]{:S(2)}, u32[]{:S(2)}) collective-permute-start(bf16[2,144,768]{2,1,0:T(8,128)(2,1)S(1)} %get-tuple-element.55.refs_1_.refs_3_), channel_id=1, source_target_pairs={{0,2},{2,4},{4,6},{6,7},{7,5},{5,3},{3,1},{1,0},{8,10},{10,12},{12... | collective-permute-start | bytes 1327112 | tf_op jit(solution)/shard_map/ppermute | solution.py:236
  6.3 20.5 %collective-permute-start.11 = (bf16[2,144,768]{2,1,0:T(8,128)(2,1)S(1)}, bf16[2,144,768]{2,1,0:T(8,128)(2,1)S(1)}, u32[]{:S(2)}, u32[]{:S(2)}) collective-permute-start(bf16[2,144,768]{2,1,0:T(8,128)(2,1)S(1)} %get-tuple-element.56.refs_0_.refs_2_), channel_id=1, source_target_pairs={{2,0},{4,2},{6,4},{7,6},{5,7},{3,5},{1,3},{0,1},{10,8},{12,10},{14... | collective-permute-start | bytes 1327112 | tf_op jit(solution)/shard_map/ppermute | solution.py:237
  15.2 19.0 %collective-permute-start.1 = (bf16[2,144,768]{2,1,0:T(8,128)(2,1)S(1)}, bf16[2,144,768]{2,1,0:T(8,128)(2,1)S(1)}, u32[]{:S(2)}, u32[]{:S(2)}) collective-permute-start(bf16[2,144,768]{2,1,0:T(8,128)(2,1)S(1)} %collective-permute-done.refs_2_.refs_4_), channel_id=1, source_target_pairs={{0,2},{2,4},{4,6},{6,7},{7,5},{5,3},{3,1},{1,0},{8,10},{10,12},{12... | collective-permute-start | bytes 1327112 | tf_op jit(solution)/shard_map/ppermute | solution.py:236
  17.4 19.0 %collective-permute-start.3 = (bf16[2,144,768]{2,1,0:T(8,128)(2,1)S(1)}, bf16[2,144,768]{2,1,0:T(8,128)(2,1)S(1)}, u32[]{:S(2)}, u32[]{:S(2)}) collective-permute-start(bf16[2,144,768]{2,1,0:T(8,128)(2,1)S(1)} %collective-permute-done.2.refs_3_.refs_5_), channel_id=1, source_target_pairs={{2,0},{4,2},{6,4},{7,6},{5,7},{3,5},{1,3},{0,1},{10,8},{12,10},{14... | collective-permute-start | bytes 1327112 | tf_op jit(solution)/shard_map/ppermute | solution.py:237
  21.3 17.4 %collective-permute-start.4 = (bf16[576,384]{1,0:T(8,128)(2,1)S(1)}, bf16[576,384]{1,0:T(8,128)(2,1)S(1)}, u32[]{:S(2)}, u32[]{:S(2)}) collective-permute-start(bf16[576,384]{1,0:T(8,128)(2,1)S(1)} %get-tuple-element.31), channel_id=1, source_target_pairs={{0,8},{8,0},{16,24},{24,16},{1,9},{9,1},{17,25},{25,17},{2,10},{10... | collective-permute-start | bytes 1327112 | tf_op jit(solution)/shard_map/ppermute | solution.py:209
  26.9 16.8 %collective-permute-start.16 = (bf16[2,144,768]{2,1,0:T(8,128)(2,1)S(1)}, bf16[2,144,768]{2,1,0:T(8,128)(2,1)S(1)}, u32[]{:S(2)}, u32[]{:S(2)}) collective-permute-start(bf16[2,144,768]{2,1,0:T(8,128)(2,1)S(1)} %collective-permute-done.10.refs_0_.refs_6_), channel_id=1, source_target_pairs={{0,2},{2,4},{4,6},{6,7},{7,5},{5,3},{3,1},{1,0},{8,10},{10,12},{12... | collective-permute-start | bytes 1327112 | tf_op jit(solution)/shard_map/ppermute | solution.py:236
  28.4 17.2 %collective-permute-start.18 = (bf16[2,144,768]{2,1,0:T(8,128)(2,1)S(1)}, bf16[2,144,768]{2,1,0:T(8,128)(2,1)S(1)}, u32[]{:S(2)}, u32[]{:S(2)}) collective-permute-start(bf16[2,144,768]{2,1,0:T(8,128)(2,1)S(1)} %collective-permute-done.11.refs_1_.refs_7_), channel_id=1, source_target_pairs={{2,0},{4,2},{6,4},{7,6},{5,7},{3,5},{1,3},{0,1},{10,8},{12,10},{14... | collective-permute-start | bytes 1327112 | tf_op jit(solution)/shard_map/ppermute | solution.py:237
  38.6 8.6 %collective-permute-start.12 = (bf16[576,384]{1,0:T(8,128)(2,1)S(1)}, bf16[576,384]{1,0:T(8,128)(2,1)S(1)}, u32[]{:S(2)}, u32[]{:S(2)}) collective-permute-start(bf16[576,384]{1,0:T(8,128)(2,1)S(1)} %get-tuple-element.37), channel_id=1, source_target_pairs={{0,8},{8,0},{16,24},{24,16},{1,9},{9,1},{17,25},{25,17},{2,10},{10... | collective-permute-start | bytes 1327112 | tf_op jit(solution)/shard_map/ppermute | solution.py:209
  38.8 14.4 %collective-permute-start.5 = (bf16[2,144,768]{2,1,0:T(8,128)(2,1)S(1)}, bf16[2,144,768]{2,1,0:T(8,128)(2,1)S(1)}, u32[]{:S(2)}, u32[]{:S(2)}) collective-permute-start(bf16[2,144,768]{2,1,0:T(8,128)(2,1)S(1)} %collective-permute-done.1.refs_2_.refs_8_), channel_id=1, source_target_pairs={{0,2},{2,4},{4,6},{6,7},{7,5},{5,3},{3,1},{1,0},{8,10},{10,12},{12... | collective-permute-start | bytes 1327112 | tf_op jit(solution)/shard_map/ppermute | solution.py:236
  40.4 14.7 %collective-permute-start.6 = (bf16[2,144,768]{2,1,0:T(8,128)(2,1)S(1)}, bf16[2,144,768]{2,1,0:T(8,128)(2,1)S(1)}, u32[]{:S(2)}, u32[]{:S(2)}) collective-permute-start(bf16[2,144,768]{2,1,0:T(8,128)(2,1)S(1)} %collective-permute-done.3.refs_3_.refs_9_), channel_id=1, source_target_pairs={{2,0},{4,2},{6,4},{7,6},{5,7},{3,5},{1,3},{0,1},{10,8},{12,10},{14... | collective-permute-start | bytes 1327112 | tf_op jit(solution)/shard_map/ppermute | solution.py:237
  43.7 13.8 %collective-permute-start.7 = (bf16[576,384]{1,0:T(8,128)(2,1)S(1)}, bf16[576,384]{1,0:T(8,128)(2,1)S(1)}, u32[]{:S(2)}, u32[]{:S(2)}) collective-permute-start(bf16[576,384]{1,0:T(8,128)(2,1)S(1)} %fusion), channel_id=1, source_target_pairs={{0,16},{8,24},{16,0},{24,8},{1,17},{9,25},{17,1},{25,9},{2,18},{10... | collective-permute-start | bytes 1327112 | tf_op jit(solution)/shard_map/ppermute | solution.py:209
  45.6 16.2 %collective-permute-start.17 = (bf16[2,144,768]{2,1,0:T(8,128)(2,1)S(1)}, bf16[2,144,768]{2,1,0:T(8,128)(2,1)S(1)}, u32[]{:S(2)}, u32[]{:S(2)}) collective-permute-start(bf16[2,144,768]{2,1,0:T(8,128)(2,1)S(1)} %collective-permute-done.16.refs_0_.refs_1_), channel_id=1, source_target_pairs={{0,2},{2,4},{4,6},{6,7},{7,5},{5,3},{3,1},{1,0},{8,10},{10,12},{12... | collective-permute-start | bytes 1327112 | tf_op jit(solution)/shard_map/ppermute | solution.py:236
  47.2 16.4 %collective-permute-start.19 = (bf16[2,144,768]{2,1,0:T(8,128)(2,1)S(1)}, bf16[2,144,768]{2,1,0:T(8,128)(2,1)S(1)}, u32[]{:S(2)}, u32[]{:S(2)}) collective-permute-start(bf16[2,144,768]{2,1,0:T(8,128)(2,1)S(1)} %collective-permute-done.18.refs_1_.refs_2_), channel_id=1, source_target_pairs={{2,0},{4,2},{6,4},{7,6},{5,7},{3,5},{1,3},{0,1},{10,8},{12,10},{14... | collective-permute-start | bytes 1327112 | tf_op jit(solution)/shard_map/ppermute | solution.py:237
  53.1 12.1 %collective-permute-start.13 = (bf16[576,384]{1,0:T(8,128)(2,1)S(1)}, bf16[576,384]{1,0:T(8,128)(2,1)S(1)}, u32[]{:S(2)}, u32[]{:S(2)}) collective-permute-start(bf16[576,384]{1,0:T(8,128)(2,1)S(1)} %fusion.1), channel_id=1, source_target_pairs={{0,16},{8,24},{16,0},{24,8},{1,17},{9,25},{17,1},{25,9},{2,18},{10... | collective-permute-start | bytes 1327112 | tf_op jit(solution)/shard_map/ppermute | solution.py:209
  57.3 8.2 %collective-permute-start.23 = (bf16[576,384]{1,0:T(8,128)(2,1)S(1)}, bf16[576,384]{1,0:T(8,128)(2,1)S(1)}, u32[]{:S(2)}, u32[]{:S(2)}) collective-permute-start(bf16[576,384]{1,0:T(8,128)(2,1)S(1)} %get-tuple-element.52), channel_id=1, source_target_pairs={{0,8},{8,0},{16,24},{24,16},{1,9},{9,1},{17,25},{25,17},{2,10},{10... | collective-permute-start | bytes 1327112 | tf_op jit(solution)/shard_map/ppermute | solution.py:209
  57.6 11.0 %collective-permute-start.14 = (bf16[576,384]{1,0:T(8,128)(2,1)S(1)}, bf16[576,384]{1,0:T(8,128)(2,1)S(1)}, u32[]{:S(2)}, u32[]{:S(2)}) collective-permute-start(bf16[576,384]{1,0:T(8,128)(2,1)S(1)} %add_convert_fusion.2.refs_10_), channel_id=1, source_target_pairs={{0,8},{8,0},{16,24},{24,16},{1,9},{9,1},{17,25},{25,17},{2,10},{10... | collective-permute-start | bytes 1327112 | tf_op jit(solution)/shard_map/ppermute | solution.py:209
  61.8 13.0 %collective-permute-start.8 = (bf16[2,144,768]{2,1,0:T(8,128)(2,1)S(1)}, bf16[2,144,768]{2,1,0:T(8,128)(2,1)S(1)}, u32[]{:S(2)}, u32[]{:S(2)}) collective-permute-start(bf16[2,144,768]{2,1,0:T(8,128)(2,1)S(1)} %collective-permute-done.5.refs_2_.refs_3_), channel_id=1, source_target_pairs={{0,2},{2,4},{4,6},{6,7},{7,5},{5,3},{3,1},{1,0},{8,10},{10,12},{12... | collective-permute-start | bytes 1327112 | tf_op jit(solution)/shard_map/ppermute | solution.py:236
  63.6 11.2 %collective-permute-start.9 = (bf16[2,144,768]{2,1,0:T(8,128)(2,1)S(1)}, bf16[2,144,768]{2,1,0:T(8,128)(2,1)S(1)}, u32[]{:S(2)}, u32[]{:S(2)}) collective-permute-start(bf16[2,144,768]{2,1,0:T(8,128)(2,1)S(1)} %collective-permute-done.6.refs_3_.refs_4_), channel_id=1, source_target_pairs={{2,0},{4,2},{6,4},{7,6},{5,7},{3,5},{1,3},{0,1},{10,8},{12,10},{14... | collective-permute-start | bytes 1327112 | tf_op jit(solution)/shard_map/ppermute | solution.py:237
  66.9 13.0 %collective-permute-start.24 = (bf16[576,384]{1,0:T(8,128)(2,1)S(1)}, bf16[576,384]{1,0:T(8,128)(2,1)S(1)}, u32[]{:S(2)}, u32[]{:S(2)}) collective-permute-start(bf16[576,384]{1,0:T(8,128)(2,1)S(1)} %fusion.2), channel_id=1, source_target_pairs={{0,16},{8,24},{16,0},{24,8},{1,17},{9,25},{17,1},{25,9},{2,18},{10... | collective-permute-start | bytes 1327112 | tf_op jit(solution)/shard_map/ppermute | solution.py:209
  68.6 15.6 %collective-permute-start.26 = (bf16[288,384]{1,0:T(8,128)(2,1)S(1)}, bf16[288,384]{1,0:T(8,128)(2,1)S(1)}, u32[]{:S(2)}, u32[]{:S(2)}) collective-permute-start(bf16[288,384]{1,0:T(8,128)(2,1)S(1)} %fusion.3), channel_id=1, source_target_pairs={{0,16},{8,24},{16,0},{24,8},{1,17},{9,25},{17,1},{25,9},{2,18},{10... | collective-permute-start | bytes 663560 | tf_op jit(solution)/shard_map/ppermute | solution.py:209
  80.2 8.4 %collective-permute-start.22 = (bf16[288,384]{1,0:T(8,128)(2,1)S(1)}, bf16[288,384]{1,0:T(8,128)(2,1)S(1)}, u32[]{:S(2)}, u32[]{:S(2)}) collective-permute-start(bf16[288,384]{1,0:T(8,128)(2,1)S(1)} %fusion.4), channel_id=1, source_target_pairs={{0,16},{8,24},{16,0},{24,8},{1,17},{9,25},{17,1},{25,9},{2,18},{10... | collective-permute-start | bytes 663560 | tf_op jit(solution)/shard_map/ppermute | solution.py:209
  84.3 4.6 %collective-permute-start.27 = (bf16[288,384]{1,0:T(8,128)(2,1)S(1)}, bf16[288,384]{1,0:T(8,128)(2,1)S(1)}, u32[]{:S(2)}, u32[]{:S(2)}) collective-permute-start(bf16[288,384]{1,0:T(8,128)(2,1)S(1)} %add_convert_fusion.4.refs_4_), channel_id=1, source_target_pairs={{0,8},{8,0},{16,24},{24,16},{1,9},{9,1},{17,25},{25,17},{2,10},{10... | collective-permute-start | bytes 663560 | tf_op jit(solution)/shard_map/ppermute | solution.py:209
  (10 other events, 34.2 us)

commit v6 on v4

--- a/solution.py
+++ b/solution.py
@@ -209,7 +209,7 @@
         return lax.ppermute(x, "row", [(r, r ^ bit) for r in range(n_row)])
 
     last = n_col - 1
-    own = [shard[:, :cut], shard[:, cut:]]
+    own = [shard[:, :cut], lax.optimization_barrier(shard)[:, cut:]]
     ups, downs = list(own), list(own)
     vals = {}
     pairs = last - 3

time: 94.4 us -> 95.1 us (level)
    ppermute x7, waiting for transfers between devices: 2.24 us -> 9.97 us  [ring_step(): downs[down_h] = lax.ppermute(downs[down_h], 'col', down)]
    ppermute x7, waiting for transfers between devices: 31.3 us -> 24.1 us  [ring_step(): ups[up_h] = lax.ppermute(ups[up_h], 'col', up)]
    slice x1 -> x2, local copies, waits for them, and re-layouts: 1.2 us -> 2.08 us  [local(): own = [shard[:, :cut], lax.optimization_barrier(shard)[:, cut:]]]
  transfers between devices with their start and end apart: 29 -> 29, of which waited for: 12 -> 17; matrix products, arithmetic and copies ran while one was open for 1% -> 2% of each run, Pallas kernels for 19% -> 19%
where the time goes in v6:
time: 95.1 us; the launch traced here: 94.9 us
  waiting for transfers between devices  43.2 us (45%)
  starting transfers between devices  24.2 us (25%)
  Pallas kernels  21.9 us (23%)
  local copies, waits for them, and re-layouts  3.93 us (4%)
  other arithmetic  1.14 us (1%)
    ppermute x7, waiting for transfers between devices, ring_step(): ups[up_h] = lax.ppermute(ups[up_h], 'col', up)  24.1 us
    ppermute x7, starting transfers between devices, ring_step(): ups[up_h] = lax.ppermute(ups[up_h], 'col', up)  14.2 us
    ppermute x7, waiting for transfers between devices, ring_step(): downs[down_h] = lax.ppermute(downs[down_h], 'col', down)  9.97 us
    pallas_call x5, Pallas kernels, cross(): pl.pallas_call(cross_kernel, out_shape=(jax.ShapeDtypeStruct((rows, vir /...  9.62 us
    ppermute x15, waiting for transfers between devices, swap(): return lax.ppermute(x, 'row', [(r, r ^ bit) for r in range(n_row)])  9.13 us
    ppermute x15, starting transfers between devices, swap(): return lax.ppermute(x, 'row', [(r, r ^ bit) for r in range(n_row)])  8.73 us
    pallas_call x2, Pallas kernels, numer(): pl.pallas_call(functools.partial(numer_kernel, len(chunks), len(mine), fr...  8.47 us
    pallas_call x1, Pallas kernels, final(): pl.pallas_call(functools.partial(final_kernel, len(chunks), len(mine)), o...  3.85 us
  transfers between devices with their start and end apart: 29, of which 17 were waited for; matrix products, arithmetic and copies ran while one was open for 2% of the time, Pallas kernels for 19%

profile of v6, /device:TPU:0, one launch (start us, length us, event | category | flops | bytes accessed | tf_op | source)
XLA Modules:
  0.0 94.9 jit_solution(4170182125322279722)
XLA Ops:
  1.0 3.1 %collective-permute-start = (bf16[2,144,768]{2,1,0:T(8,128)(2,1)S(1)}, bf16[2,144,768]{2,1,0:T(8,128)(2,1)S(1)}, u32[]{:S(2)}, u32[]{:S(2)}) collective-permute-start(bf16[2,144,768]{2,1,0:T(8,128)(2,1)S(1)} %slice.12.refs_0_.refs_2_), channel_id=1, source_target_pairs={{0,2},{2,4},{4,6},{6,7},{7,5},{5,3},{3,1},{1,0},{8,10},{10,12},{12... | collective-permute-start | bytes 1327112 | tf_op jit(solution)/shard_map/ppermute | solution.py:236
  5.2 2.0 %collective-permute-start.8 = (bf16[2,144,768]{2,1,0:T(8,128)(2,1)S(1)}, bf16[2,144,768]{2,1,0:T(8,128)(2,1)S(1)}, u32[]{:S(2)}, u32[]{:S(2)}) collective-permute-start(bf16[2,144,768]{2,1,0:T(8,128)(2,1)S(1)} %slice.13.refs_1_.refs_3_), channel_id=1, source_target_pairs={{0,2},{2,4},{4,6},{6,7},{7,5},{5,3},{3,1},{1,0},{8,10},{10,12},{12... | collective-permute-start | bytes 1327112 | tf_op jit(solution)/shard_map/ppermute | solution.py:236
  7.4 7.6 %collective-permute-done.refs_2_.refs_4_ = bf16[2,144,768]{2,1,0:T(8,128)(2,1)S(1)} collective-permute-done((bf16[2,144,768]{2,1,0:T(8,128)(2,1)S(1)}, bf16[2,144,768]{2,1,0:T(8,128)(2,1)S(1)}, u32[]{:S(2)}, u32[]{:S(2)}) %collective-permute-start) | collective-permute-done | bytes 442400 | tf_op jit(solution)/shard_map/ppermute | solution.py:236
  15.1 2.1 %collective-permute-start.1 = (bf16[2,144,768]{2,1,0:T(8,128)(2,1)S(1)}, bf16[2,144,768]{2,1,0:T(8,128)(2,1)S(1)}, u32[]{:S(2)}, u32[]{:S(2)}) collective-permute-start(bf16[2,144,768]{2,1,0:T(8,128)(2,1)S(1)} %collective-permute-done.refs_2_.refs_4_), channel_id=1, source_target_pairs={{0,2},{2,4},{4,6},{6,7},{7,5},{5,3},{3,1},{1,0},{8,10},{10,12},{12... | collective-permute-start | bytes 1327112 | tf_op jit(solution)/shard_map/ppermute | solution.py:236
  18.3 1.7 %copy-done = bf16[2,1,768,768]{3,2,1,0:T(8,128)(2,1)S(1)} copy-done((bf16[2,1,768,768]{3,2,1,0:T(8,128)(2,1)S(1)}, bf16[2,1,768,768]{3,2,1,0:T(8,128)(2,1)}, u32[]{:S(2)}) %copy-start) | copy-done | bytes 2359320
  20.0 2.3 %cross.5 = (f32[576,384]{1,0:T(8,128)S(1)}, bf16[576,384]{1,0:T(8,128)(2,1)S(1)}) custom-call(s32[5]{0:T(128)S(1)} %pad_add_fusion.flags, bf16[2,768,768]{2,1,0:T(8,128)(2,1)S(1)} %bitcast.5, bf16[2,144,768]{2,1,0:T(8,128)(2,1)S(1)} %slice.12.refs_0_.refs_2_, bf16[2,144,768]{2,1,0:T(8,128)(2,1)S(1)} %slice.13.refs_1_.refs_3_, ...), custom_call_target="tpu_custom_call" | custom-call | flops 1358955 | bytes 5899 | tf_op jit(solution)/shard_map/cross/pallas_call | solution.py:59
  22.3 2.2 %collective-permute-done.8.refs_0_.refs_6_ = bf16[2,144,768]{2,1,0:T(8,128)(2,1)S(1)} collective-permute-done((bf16[2,144,768]{2,1,0:T(8,128)(2,1)S(1)}, bf16[2,144,768]{2,1,0:T(8,128)(2,1)S(1)}, u32[]{:S(2)}, u32[]{:S(2)}) %collective-permute-start.8) | collective-permute-done | bytes 442400 | tf_op jit(solution)/shard_map/ppermute | solution.py:236
  24.5 2.1 %collective-permute-start.16 = (bf16[2,144,768]{2,1,0:T(8,128)(2,1)S(1)}, bf16[2,144,768]{2,1,0:T(8,128)(2,1)S(1)}, u32[]{:S(2)}, u32[]{:S(2)}) collective-permute-start(bf16[2,144,768]{2,1,0:T(8,128)(2,1)S(1)} %collective-permute-done.8.refs_0_.refs_6_), channel_id=1, source_target_pairs={{0,2},{2,4},{4,6},{6,7},{7,5},{5,3},{3,1},{1,0},{8,10},{10,12},{12... | collective-permute-start | bytes 1327112 | tf_op jit(solution)/shard_map/ppermute | solution.py:236
  27.8 6.2 %collective-permute-done.1.refs_2_.refs_8_ = bf16[2,144,768]{2,1,0:T(8,128)(2,1)S(1)} collective-permute-done((bf16[2,144,768]{2,1,0:T(8,128)(2,1)S(1)}, bf16[2,144,768]{2,1,0:T(8,128)(2,1)S(1)}, u32[]{:S(2)}, u32[]{:S(2)}) %collective-permute-start.1) | collective-permute-done | bytes 442400 | tf_op jit(solution)/shard_map/ppermute | solution.py:236
  34.0 3.3 %collective-permute-done.3.refs_3_.refs_9_ = bf16[2,144,768]{2,1,0:T(8,128)(2,1)S(1)} collective-permute-done((bf16[2,144,768]{2,1,0:T(8,128)(2,1)S(1)}, bf16[2,144,768]{2,1,0:T(8,128)(2,1)S(1)}, u32[]{:S(2)}, u32[]{:S(2)}) %collective-permute-start.3) | collective-permute-done | bytes 442400 | tf_op jit(solution)/shard_map/ppermute | solution.py:237
  37.3 2.2 %cross.6 = (f32[576,384]{1,0:T(8,128)S(1)}, bf16[576,384]{1,0:T(8,128)(2,1)S(1)}) custom-call(s32[5]{0:T(128)S(1)} %pad_add_fusion.flags, bf16[2,768,768]{2,1,0:T(8,128)(2,1)S(1)} %bitcast.6, bf16[2,144,768]{2,1,0:T(8,128)(2,1)S(1)} %collective-permute-done.8.refs_0_.refs_6_, bf16[2,144,768]{2,1,0:T(8,128)(2,1)S(1)} %collective-permute-done.9.refs_1_.refs_7_, ...), custom_call_target="tpu_custom_call" | custom-call | flops 1358955 | bytes 5899 | tf_op jit(solution)/shard_map/cross/pallas_call | solution.py:59
  42.7 1.7 %collective-permute-start.7 = (bf16[576,384]{1,0:T(8,128)(2,1)S(1)}, bf16[576,384]{1,0:T(8,128)(2,1)S(1)}, u32[]{:S(2)}, u32[]{:S(2)}) collective-permute-start(bf16[576,384]{1,0:T(8,128)(2,1)S(1)} %fusion), channel_id=1, source_target_pairs={{0,16},{8,24},{16,0},{24,8},{1,17},{9,25},{17,1},{25,9},{2,18},{10... | collective-permute-start | bytes 1327112 | tf_op jit(solution)/shard_map/ppermute | solution.py:209
  44.4 2.0 %collective-permute-done.18.refs_1_.refs_2_ = bf16[2,144,768]{2,1,0:T(8,128)(2,1)S(1)} collective-permute-done((bf16[2,144,768]{2,1,0:T(8,128)(2,1)S(1)}, bf16[2,144,768]{2,1,0:T(8,128)(2,1)S(1)}, u32[]{:S(2)}, u32[]{:S(2)}) %collective-permute-start.18) | collective-permute-done | bytes 442400 | tf_op jit(solution)/shard_map/ppermute | solution.py:237
  48.5 4.2 %collective-permute-done.5.refs_2_.refs_3_ = bf16[2,144,768]{2,1,0:T(8,128)(2,1)S(1)} collective-permute-done((bf16[2,144,768]{2,1,0:T(8,128)(2,1)S(1)}, bf16[2,144,768]{2,1,0:T(8,128)(2,1)S(1)}, u32[]{:S(2)}, u32[]{:S(2)}) %collective-permute-start.5) | collective-permute-done | bytes 442400 | tf_op jit(solution)/shard_map/ppermute | solution.py:236
  54.2 1.6 %collective-permute-done.6.refs_3_.refs_4_ = bf16[2,144,768]{2,1,0:T(8,128)(2,1)S(1)} collective-permute-done((bf16[2,144,768]{2,1,0:T(8,128)(2,1)S(1)}, bf16[2,144,768]{2,1,0:T(8,128)(2,1)S(1)}, u32[]{:S(2)}, u32[]{:S(2)}) %collective-permute-start.6) | collective-permute-done | bytes 442400 | tf_op jit(solution)/shard_map/ppermute | solution.py:237
  55.9 2.2 %cross.9 = (f32[576,384]{1,0:T(8,128)S(1)}, bf16[576,384]{1,0:T(8,128)(2,1)S(1)}) custom-call(s32[5]{0:T(128)S(1)} %pad_add_fusion.flags, bf16[2,768,768]{2,1,0:T(8,128)(2,1)S(1)} %bitcast.7, bf16[2,144,768]{2,1,0:T(8,128)(2,1)S(1)} %collective-permute-done.16.refs_0_.refs_1_, bf16[2,144,768]{2,1,0:T(8,128)(2,1)S(1)} %collective-permute-done.18.refs_1_.refs_2_, ...), custom_call_target="tpu_custom_call" | custom-call | flops 1358955 | bytes 5899 | tf_op jit(solution)/shard_map/cross/pallas_call | solution.py:59
  58.9 2.9 %collective-permute-done.17.refs_0_ = bf16[2,144,768]{2,1,0:T(8,128)(2,1)S(1)} collective-permute-done((bf16[2,144,768]{2,1,0:T(8,128)(2,1)S(1)}, bf16[2,144,768]{2,1,0:T(8,128)(2,1)S(1)}, u32[]{:S(2)}, u32[]{:S(2)}) %collective-permute-start.17) | collective-permute-done | bytes 442400 | tf_op jit(solution)/shard_map/ppermute | solution.py:236
  67.6 1.7 %collective-permute-start.24 = (bf16[576,384]{1,0:T(8,128)(2,1)S(1)}, bf16[576,384]{1,0:T(8,128)(2,1)S(1)}, u32[]{:S(2)}, u32[]{:S(2)}) collective-permute-start(bf16[576,384]{1,0:T(8,128)(2,1)S(1)} %fusion.2), channel_id=1, source_target_pairs={{0,16},{8,24},{16,0},{24,8},{1,17},{9,25},{17,1},{25,9},{2,18},{10... | collective-permute-start | bytes 1327112 | tf_op jit(solution)/shard_map/ppermute | solution.py:209
  69.7 5.7 %numer.2.refs_0_ = f32[2,768,768]{2,1,0:T(8,128)S(1)} custom-call(s32[5]{0:T(128)S(1)} %pad_add_fusion.flags, bf16[2,768,768]{2,1,0:T(8,128)(2,1)S(1)} %bitcast.9, bf16[768,768]{1,0:T(8,128)(2,1)S(1)} %copy-done.2, bf16[2,144,768]{2,1,0:T(8,128)(2,1)S(1)} %slice.12.refs_0_.refs_2_, bf16[2,144,768]{2,1,0:T(8,128)(2,1)S(1)} %slice.13.refs_1_.refs_3_, ...), custom_call_target="tpu_custom_call" | custom-call | flops 4529849 | bytes 12387 | tf_op jit(solution)/shard_map/numer/pallas_call | solution.py:121
  77.1 3.5 %collective-permute-done.24 = bf16[576,384]{1,0:T(8,128)(2,1)S(1)} collective-permute-done((bf16[576,384]{1,0:T(8,128)(2,1)S(1)}, bf16[576,384]{1,0:T(8,128)(2,1)S(1)}, u32[]{:S(2)}, u32[]{:S(2)}) %collective-permute-start.24) | collective-permute-done | bytes 442400 | tf_op jit(solution)/shard_map/ppermute | solution.py:209
  80.9 1.7 %collective-permute-start.22 = (bf16[288,384]{1,0:T(8,128)(2,1)S(1)}, bf16[288,384]{1,0:T(8,128)(2,1)S(1)}, u32[]{:S(2)}, u32[]{:S(2)}) collective-permute-start(bf16[288,384]{1,0:T(8,128)(2,1)S(1)} %fusion.4), channel_id=1, source_target_pairs={{0,16},{8,24},{16,0},{24,8},{1,17},{9,25},{17,1},{25,9},{2,18},{10... | collective-permute-start | bytes 663560 | tf_op jit(solution)/shard_map/ppermute | solution.py:209
  82.6 2.3 %collective-permute-done.26 = bf16[288,384]{1,0:T(8,128)(2,1)S(1)} collective-permute-done((bf16[288,384]{1,0:T(8,128)(2,1)S(1)}, bf16[288,384]{1,0:T(8,128)(2,1)S(1)}, u32[]{:S(2)}, u32[]{:S(2)}) %collective-permute-start.26) | collective-permute-done | bytes 221216 | tf_op jit(solution)/shard_map/ppermute | solution.py:209
  85.1 2.7 %numer.3.acc_ref = f32[2,768,768]{2,1,0:T(8,128)S(1)} custom-call(s32[5]{0:T(128)S(1)} %pad_add_fusion.flags, f32[2,768,768]{2,1,0:T(8,128)S(1)} %numer.2.refs_0_, bf16[2,144,768]{2,1,0:T(8,128)(2,1)S(1)} %collective-permute-done.16.refs_0_.refs_1_, bf16[2,144,768]{2,1,0:T(8,128)(2,1)S(1)} %collective-permute-done.18.refs_1_.refs_2_, ...), custom_call_target="tpu_custom_call", output_to_operand_aliasing={{}: (1, {})} | custom-call | flops 1358955 | bytes 9733 | tf_op jit(solution)/shard_map/numer/pallas_call | solution.py:121
  90.9 3.9 %final.1 = bf16[2,1,768,768]{3,2,1,0:T(8,128)(2,1)} custom-call(s32[5]{0:T(128)S(1)} %pad_add_fusion.flags, f32[8]{0:T(128)S(1)} %copy-done.3, f32[2,768,768]{2,1,0:T(8,128)S(1)} %numer.3.acc_ref, bf16[2,768,768]{2,1,0:T(8,128)(2,1)S(1)} %bitcast.11, f32[1,768]{1,0:T(1,128)S(1)} %broadcast_in_dim.6.eps_row, f32[768,1]{1,0:T(8,128)S(1)} %broadcast_in_dim.8.eps_col, ...), custom_call_target="tpu_custom_call" | custom-call | flops 1358955 | bytes 9438 | tf_op jit(solution)/shard_map/final/pallas_call | solution.py:171
  (69 shorter events, 23.4 us)
Async XLA Ops:
  1.0 14.0 %collective-permute-start = (bf16[2,144,768]{2,1,0:T(8,128)(2,1)S(1)}, bf16[2,144,768]{2,1,0:T(8,128)(2,1)S(1)}, u32[]{:S(2)}, u32[]{:S(2)}) collective-permute-start(bf16[2,144,768]{2,1,0:T(8,128)(2,1)S(1)} %slice.12.refs_0_.refs_2_), channel_id=1, source_target_pairs={{0,2},{2,4},{4,6},{6,7},{7,5},{5,3},{3,1},{1,0},{8,10},{10,12},{12... | collective-permute-start | bytes 1327112 | tf_op jit(solution)/shard_map/ppermute | solution.py:236
  5.2 13.1 %collective-permute-start.2 = (bf16[2,144,768]{2,1,0:T(8,128)(2,1)S(1)}, bf16[2,144,768]{2,1,0:T(8,128)(2,1)S(1)}, u32[]{:S(2)}, u32[]{:S(2)}) collective-permute-start(bf16[2,144,768]{2,1,0:T(8,128)(2,1)S(1)} %slice.13.refs_1_.refs_3_), channel_id=1, source_target_pairs={{2,0},{4,2},{6,4},{7,6},{5,7},{3,5},{1,3},{0,1},{10,8},{12,10},{14... | collective-permute-start | bytes 1327112 | tf_op jit(solution)/shard_map/ppermute | solution.py:237
  5.2 19.3 %collective-permute-start.8 = (bf16[2,144,768]{2,1,0:T(8,128)(2,1)S(1)}, bf16[2,144,768]{2,1,0:T(8,128)(2,1)S(1)}, u32[]{:S(2)}, u32[]{:S(2)}) collective-permute-start(bf16[2,144,768]{2,1,0:T(8,128)(2,1)S(1)} %slice.13.refs_1_.refs_3_), channel_id=1, source_target_pairs={{0,2},{2,4},{4,6},{6,7},{7,5},{5,3},{3,1},{1,0},{8,10},{10,12},{12... | collective-permute-start | bytes 1327112 | tf_op jit(solution)/shard_map/ppermute | solution.py:236
  7.2 20.5 %collective-permute-start.9 = (bf16[2,144,768]{2,1,0:T(8,128)(2,1)S(1)}, bf16[2,144,768]{2,1,0:T(8,128)(2,1)S(1)}, u32[]{:S(2)}, u32[]{:S(2)}) collective-permute-start(bf16[2,144,768]{2,1,0:T(8,128)(2,1)S(1)} %slice.12.refs_0_.refs_2_), channel_id=1, source_target_pairs={{2,0},{4,2},{6,4},{7,6},{5,7},{3,5},{1,3},{0,1},{10,8},{12,10},{14... | collective-permute-start | bytes 1327112 | tf_op jit(solution)/shard_map/ppermute | solution.py:237
  15.1 19.0 %collective-permute-start.1 = (bf16[2,144,768]{2,1,0:T(8,128)(2,1)S(1)}, bf16[2,144,768]{2,1,0:T(8,128)(2,1)S(1)}, u32[]{:S(2)}, u32[]{:S(2)}) collective-permute-start(bf16[2,144,768]{2,1,0:T(8,128)(2,1)S(1)} %collective-permute-done.refs_2_.refs_4_), channel_id=1, source_target_pairs={{0,2},{2,4},{4,6},{6,7},{7,5},{5,3},{3,1},{1,0},{8,10},{10,12},{12... | collective-permute-start | bytes 1327112 | tf_op jit(solution)/shard_map/ppermute | solution.py:236
  18.3 19.0 %collective-permute-start.3 = (bf16[2,144,768]{2,1,0:T(8,128)(2,1)S(1)}, bf16[2,144,768]{2,1,0:T(8,128)(2,1)S(1)}, u32[]{:S(2)}, u32[]{:S(2)}) collective-permute-start(bf16[2,144,768]{2,1,0:T(8,128)(2,1)S(1)} %collective-permute-done.2.refs_3_.refs_5_), channel_id=1, source_target_pairs={{2,0},{4,2},{6,4},{7,6},{5,7},{3,5},{1,3},{0,1},{10,8},{12,10},{14... | collective-permute-start | bytes 1327112 | tf_op jit(solution)/shard_map/ppermute | solution.py:237
  22.2 17.4 %collective-permute-start.4 = (bf16[576,384]{1,0:T(8,128)(2,1)S(1)}, bf16[576,384]{1,0:T(8,128)(2,1)S(1)}, u32[]{:S(2)}, u32[]{:S(2)}) collective-permute-start(bf16[576,384]{1,0:T(8,128)(2,1)S(1)} %get-tuple-element.27), channel_id=1, source_target_pairs={{0,8},{8,0},{16,24},{24,16},{1,9},{9,1},{17,25},{25,17},{2,10},{10... | collective-permute-start | bytes 1327112 | tf_op jit(solution)/shard_map/ppermute | solution.py:209
  24.5 18.1 %collective-permute-start.16 = (bf16[2,144,768]{2,1,0:T(8,128)(2,1)S(1)}, bf16[2,144,768]{2,1,0:T(8,128)(2,1)S(1)}, u32[]{:S(2)}, u32[]{:S(2)}) collective-permute-start(bf16[2,144,768]{2,1,0:T(8,128)(2,1)S(1)} %collective-permute-done.8.refs_0_.refs_6_), channel_id=1, source_target_pairs={{0,2},{2,4},{4,6},{6,7},{7,5},{5,3},{3,1},{1,0},{8,10},{10,12},{12... | collective-permute-start | bytes 1327112 | tf_op jit(solution)/shard_map/ppermute | solution.py:236
  27.8 18.6 %collective-permute-start.18 = (bf16[2,144,768]{2,1,0:T(8,128)(2,1)S(1)}, bf16[2,144,768]{2,1,0:T(8,128)(2,1)S(1)}, u32[]{:S(2)}, u32[]{:S(2)}) collective-permute-start(bf16[2,144,768]{2,1,0:T(8,128)(2,1)S(1)} %collective-permute-done.9.refs_1_.refs_7_), channel_id=1, source_target_pairs={{2,0},{4,2},{6,4},{7,6},{5,7},{3,5},{1,3},{0,1},{10,8},{12,10},{14... | collective-permute-start | bytes 1327112 | tf_op jit(solution)/shard_map/ppermute | solution.py:237
  39.5 8.4 %collective-permute-start.10 = (bf16[576,384]{1,0:T(8,128)(2,1)S(1)}, bf16[576,384]{1,0:T(8,128)(2,1)S(1)}, u32[]{:S(2)}, u32[]{:S(2)}) collective-permute-start(bf16[576,384]{1,0:T(8,128)(2,1)S(1)} %get-tuple-element.31), channel_id=1, source_target_pairs={{0,8},{8,0},{16,24},{24,16},{1,9},{9,1},{17,25},{25,17},{2,10},{10... | collective-permute-start | bytes 1327112 | tf_op jit(solution)/shard_map/ppermute | solution.py:209
  39.7 13.0 %collective-permute-start.5 = (bf16[2,144,768]{2,1,0:T(8,128)(2,1)S(1)}, bf16[2,144,768]{2,1,0:T(8,128)(2,1)S(1)}, u32[]{:S(2)}, u32[]{:S(2)}) collective-permute-start(bf16[2,144,768]{2,1,0:T(8,128)(2,1)S(1)} %collective-permute-done.1.refs_2_.refs_8_), channel_id=1, source_target_pairs={{0,2},{2,4},{4,6},{6,7},{7,5},{5,3},{3,1},{1,0},{8,10},{10,12},{12... | collective-permute-start | bytes 1327112 | tf_op jit(solution)/shard_map/ppermute | solution.py:236
  41.3 14.5 %collective-permute-start.6 = (bf16[2,144,768]{2,1,0:T(8,128)(2,1)S(1)}, bf16[2,144,768]{2,1,0:T(8,128)(2,1)S(1)}, u32[]{:S(2)}, u32[]{:S(2)}) collective-permute-start(bf16[2,144,768]{2,1,0:T(8,128)(2,1)S(1)} %collective-permute-done.3.refs_3_.refs_9_), channel_id=1, source_target_pairs={{2,0},{4,2},{6,4},{7,6},{5,7},{3,5},{1,3},{0,1},{10,8},{12,10},{14... | collective-permute-start | bytes 1327112 | tf_op jit(solution)/shard_map/ppermute | solution.py:237
  42.7 15.5 %collective-permute-start.7 = (bf16[576,384]{1,0:T(8,128)(2,1)S(1)}, bf16[576,384]{1,0:T(8,128)(2,1)S(1)}, u32[]{:S(2)}, u32[]{:S(2)}) collective-permute-start(bf16[576,384]{1,0:T(8,128)(2,1)S(1)} %fusion), channel_id=1, source_target_pairs={{0,16},{8,24},{16,0},{24,8},{1,17},{9,25},{17,1},{25,9},{2,18},{10... | collective-permute-start | bytes 1327112 | tf_op jit(solution)/shard_map/ppermute | solution.py:209
  46.4 15.4 %collective-permute-start.17 = (bf16[2,144,768]{2,1,0:T(8,128)(2,1)S(1)}, bf16[2,144,768]{2,1,0:T(8,128)(2,1)S(1)}, u32[]{:S(2)}, u32[]{:S(2)}) collective-permute-start(bf16[2,144,768]{2,1,0:T(8,128)(2,1)S(1)} %collective-permute-done.16.refs_0_.refs_1_), channel_id=1, source_target_pairs={{0,2},{2,4},{4,6},{6,7},{7,5},{5,3},{3,1},{1,0},{8,10},{10,12},{12... | collective-permute-start | bytes 1327112 | tf_op jit(solution)/shard_map/ppermute | solution.py:236
  47.9 16.3 %collective-permute-start.19 = (bf16[2,144,768]{2,1,0:T(8,128)(2,1)S(1)}, bf16[2,144,768]{2,1,0:T(8,128)(2,1)S(1)}, u32[]{:S(2)}, u32[]{:S(2)}) collective-permute-start(bf16[2,144,768]{2,1,0:T(8,128)(2,1)S(1)} %collective-permute-done.18.refs_1_.refs_2_), channel_id=1, source_target_pairs={{2,0},{4,2},{6,4},{7,6},{5,7},{3,5},{1,3},{0,1},{10,8},{12,10},{14... | collective-permute-start | bytes 1327112 | tf_op jit(solution)/shard_map/ppermute | solution.py:237
  52.7 13.3 %collective-permute-start.13 = (bf16[576,384]{1,0:T(8,128)(2,1)S(1)}, bf16[576,384]{1,0:T(8,128)(2,1)S(1)}, u32[]{:S(2)}, u32[]{:S(2)}) collective-permute-start(bf16[576,384]{1,0:T(8,128)(2,1)S(1)} %fusion.1), channel_id=1, source_target_pairs={{0,16},{8,24},{16,0},{24,8},{1,17},{9,25},{17,1},{25,9},{2,18},{10... | collective-permute-start | bytes 1327112 | tf_op jit(solution)/shard_map/ppermute | solution.py:209
  58.1 8.2 %collective-permute-start.23 = (bf16[576,384]{1,0:T(8,128)(2,1)S(1)}, bf16[576,384]{1,0:T(8,128)(2,1)S(1)}, u32[]{:S(2)}, u32[]{:S(2)}) collective-permute-start(bf16[576,384]{1,0:T(8,128)(2,1)S(1)} %get-tuple-element.44), channel_id=1, source_target_pairs={{0,8},{8,0},{16,24},{24,16},{1,9},{9,1},{17,25},{25,17},{2,10},{10... | collective-permute-start | bytes 1327112 | tf_op jit(solution)/shard_map/ppermute | solution.py:209
  58.3 11.0 %collective-permute-start.14 = (bf16[576,384]{1,0:T(8,128)(2,1)S(1)}, bf16[576,384]{1,0:T(8,128)(2,1)S(1)}, u32[]{:S(2)}, u32[]{:S(2)}) collective-permute-start(bf16[576,384]{1,0:T(8,128)(2,1)S(1)} %add_convert_fusion.2.refs_10_), channel_id=1, source_target_pairs={{0,8},{8,0},{16,24},{24,16},{1,9},{9,1},{17,25},{25,17},{2,10},{10... | collective-permute-start | bytes 1327112 | tf_op jit(solution)/shard_map/ppermute | solution.py:209
  61.8 13.7 %collective-permute-start.11 = (bf16[2,144,768]{2,1,0:T(8,128)(2,1)S(1)}, bf16[2,144,768]{2,1,0:T(8,128)(2,1)S(1)}, u32[]{:S(2)}, u32[]{:S(2)}) collective-permute-start(bf16[2,144,768]{2,1,0:T(8,128)(2,1)S(1)} %collective-permute-done.5.refs_2_.refs_3_), channel_id=1, source_target_pairs={{0,2},{2,4},{4,6},{6,7},{7,5},{5,3},{3,1},{1,0},{8,10},{10,12},{12... | collective-permute-start | bytes 1327112 | tf_op jit(solution)/shard_map/ppermute | solution.py:236
  64.2 11.3 %collective-permute-start.12 = (bf16[2,144,768]{2,1,0:T(8,128)(2,1)S(1)}, bf16[2,144,768]{2,1,0:T(8,128)(2,1)S(1)}, u32[]{:S(2)}, u32[]{:S(2)}) collective-permute-start(bf16[2,144,768]{2,1,0:T(8,128)(2,1)S(1)} %collective-permute-done.6.refs_3_.refs_4_), channel_id=1, source_target_pairs={{2,0},{4,2},{6,4},{7,6},{5,7},{3,5},{1,3},{0,1},{10,8},{12,10},{14... | collective-permute-start | bytes 1327112 | tf_op jit(solution)/shard_map/ppermute | solution.py:237
  67.6 13.0 %collective-permute-start.24 = (bf16[576,384]{1,0:T(8,128)(2,1)S(1)}, bf16[576,384]{1,0:T(8,128)(2,1)S(1)}, u32[]{:S(2)}, u32[]{:S(2)}) collective-permute-start(bf16[576,384]{1,0:T(8,128)(2,1)S(1)} %fusion.2), channel_id=1, source_target_pairs={{0,16},{8,24},{16,0},{24,8},{1,17},{9,25},{17,1},{25,9},{2,18},{10... | collective-permute-start | bytes 1327112 | tf_op jit(solution)/shard_map/ppermute | solution.py:209
  69.3 15.6 %collective-permute-start.26 = (bf16[288,384]{1,0:T(8,128)(2,1)S(1)}, bf16[288,384]{1,0:T(8,128)(2,1)S(1)}, u32[]{:S(2)}, u32[]{:S(2)}) collective-permute-start(bf16[288,384]{1,0:T(8,128)(2,1)S(1)} %fusion.3), channel_id=1, source_target_pairs={{0,16},{8,24},{16,0},{24,8},{1,17},{9,25},{17,1},{25,9},{2,18},{10... | collective-permute-start | bytes 663560 | tf_op jit(solution)/shard_map/ppermute | solution.py:209
  80.9 8.4 %collective-permute-start.22 = (bf16[288,384]{1,0:T(8,128)(2,1)S(1)}, bf16[288,384]{1,0:T(8,128)(2,1)S(1)}, u32[]{:S(2)}, u32[]{:S(2)}) collective-permute-start(bf16[288,384]{1,0:T(8,128)(2,1)S(1)} %fusion.4), channel_id=1, source_target_pairs={{0,16},{8,24},{16,0},{24,8},{1,17},{9,25},{17,1},{25,9},{2,18},{10... | collective-permute-start | bytes 663560 | tf_op jit(solution)/shard_map/ppermute | solution.py:209
  85.0 4.6 %collective-permute-start.27 = (bf16[288,384]{1,0:T(8,128)(2,1)S(1)}, bf16[288,384]{1,0:T(8,128)(2,1)S(1)}, u32[]{:S(2)}, u32[]{:S(2)}) collective-permute-start(bf16[288,384]{1,0:T(8,128)(2,1)S(1)} %add_convert_fusion.4.refs_4_), channel_id=1, source_target_pairs={{0,8},{8,0},{16,24},{24,16},{1,9},{9,1},{17,25},{25,17},{2,10},{10... | collective-permute-start | bytes 663560 | tf_op jit(solution)/shard_map/ppermute | solution.py:209
  (10 other events, 34.2 us)
